TPU v7x, 512 devices: a whole 4x8x8 slice. The times are simulated.
512 devices in a mesh: section: 16 (over y, core), dp: 32 (over z, x).
Axes of the slice: x: 4, y: 8, z: 8, core: 2. Of those that a mesh axis runs over, the one named last changes fastest.
Arguments:
- first_activations: bfloat16 [4096, 4096], P('dp', 'section')
- loss_sensitivity: bfloat16 [4096, 4096], P('dp', 'section'), may hold values from -0.25 to 0.25
- computing_worker: int32 [32, 8], replicated, may hold values from 0 to 31, as said below
- scaling_factor: float32 [16, 4096], P('section'), may hold values from 0.1 to 1.9
- narrowing_weights: bfloat16 [16, 64, 4096], P('section', None, 'dp'), may hold values from -0.09375 to 0.09375
- widening_weights: bfloat16 [16, 64, 4096], P('section', None, 'dp'), may hold values from -0.75 to 0.75
Outputs:
- saved_rstd: float32 [16, 32, 160], P('section', 'dp')
- saved_inputs: bfloat16 [16, 32, 160, 4096], P('section', 'dp')
- grad_down: float32 [16, 64, 4096], P('section', None, 'dp')
- grad_up: float32 [16, 64, 4096], P('section', None, 'dp')
Inputs may be any that keep to these rules, and one draw needn't show every extreme that they name: `computing_worker`: A replica either computes all its 8 micro-batches itself, or is one of 4 failed replicas whose micro-batches all go elsewhere: its micro-batches 2j and 2j + 1 go together to one replica that is not failed, and no replica takes more than one such pair. A failed replica computes none, so each replica computes 0, 8 or 10 micro-batches, and 10 occurs in every draw.
All inputs are finite; a program needn't handle non-finite values.
Results may differ from a plain program's by a relative error of at most 0.035.
Values may be sent and summed in bfloat16 or wider, within the bound.
No kernel may reach another device: no remote copies, remote signals or barrier semaphores. Data moves between devices by JAX's collectives and lax.ppermute only.
A program may use at most 64 MiB of HBM per device.

v0:
```python
import jax
import jax.numpy as jnp
from jax import lax
from jax.sharding import PartitionSpec as P

MB = 8
EXTRA = 2
TOK = 16
MICROBATCH_ROOM = 10


EPS = 1e-05


def shifted(value, axis, steps):
    count = lax.axis_size(axis)
    initial, last = (max(0, -steps), min(count, count - steps))
    return lax.ppermute(value, axis, [(source, source + steps) for source in range(initial, last)])


def forward_section(inputs, gain_row, down_weight, up_weight):
    value_rows = inputs.astype(jnp.float32)
    inverse_norm = lax.rsqrt(jnp.mean(value_rows * value_rows, axis=-1, keepdims=True) + EPS)
    normalized_input = (value_rows * inverse_norm * gain_row).astype(jnp.bfloat16)
    preact = lax.dot_general(
        normalized_input, down_weight, (((1,), (1,)), ((), ())), preferred_element_type=jnp.float32
    )
    hidden_state = jax.nn.silu(preact).astype(jnp.bfloat16)
    output = (
        value_rows + jnp.dot(hidden_state, up_weight, preferred_element_type=jnp.float32)
    ).astype(jnp.bfloat16)
    return (output, inverse_norm, normalized_input, preact, hidden_state)


def backward_section(inputs, gain_row, down_weight, up_weight, upstream_gradient):
    output, inverse_norm, normalized_input, preact, hidden_state = forward_section(
        inputs, gain_row, down_weight, up_weight
    )
    dhidden = lax.dot_general(
        upstream_gradient, up_weight, (((1,), (1,)), ((), ())), preferred_element_type=jnp.float32
    )
    sigmoid = jax.nn.sigmoid(preact)
    preactivation_gradient = (dhidden * sigmoid * (1.0 + preact * (1.0 - sigmoid))).astype(
        jnp.bfloat16
    )
    dnormed = jnp.dot(preactivation_gradient, down_weight, preferred_element_type=jnp.float32)
    scaled = dnormed * gain_row
    unit_rows = inputs.astype(jnp.float32) * inverse_norm
    dinputs = (
        upstream_gradient.astype(jnp.float32)
        + inverse_norm * (scaled - unit_rows * jnp.mean(scaled * unit_rows, axis=-1, keepdims=True))
    ).astype(jnp.bfloat16)
    return (dinputs, normalized_input, hidden_state, preactivation_gradient)


def body(
    first_activations,
    loss_sensitivity,
    computing_worker,
    scaling_factor,
    narrowing_weights,
    widening_weights,
):
    sections = lax.axis_size("section")
    worker_sequence = lax.axis_size("dp")
    section_pos = lax.axis_index("section")
    worker_number = lax.axis_index("dp")
    micro_count = MB
    extra_slots = EXTRA
    place_tally = MICROBATCH_ROOM
    tokens = TOK
    local_width = first_activations.shape[1]
    owners = jnp.arange(worker_sequence, dtype=jnp.int32)
    own_line = lax.dynamic_index_in_dim(computing_worker, worker_number, 0, keepdims=False)
    member = (own_line[:, None] == owners[None, :]).astype(jnp.int32)
    pair_rank = jnp.sum((jnp.cumsum(member, axis=0) - 1) * member, axis=1)
    rerouted = own_line != worker_number
    selection = (
        (own_line[None, None, :] == owners[:, None, None])
        & (pair_rank[None, None, :] == jnp.arange(extra_slots, dtype=jnp.int32)[None, :, None])
        & rerouted[None, None, :]
    )
    picked = jnp.any(selection, axis=2)
    chosen = jnp.sum(
        selection.astype(jnp.int32) * jnp.arange(micro_count, dtype=jnp.int32)[None, None, :],
        axis=2,
    ) + micro_count * (1 - picked.astype(jnp.int32))
    zero_block = jnp.zeros((1, tokens, local_width), jnp.bfloat16)
    entry_blocks = first_activations.reshape(micro_count, tokens, local_width)
    cot_blocks = loss_sensitivity.reshape(micro_count, tokens, local_width)

    def outgoing(blocks):
        padded = jnp.concatenate([blocks, zero_block], axis=0)
        return jnp.take(padded, chosen.reshape(-1), axis=0).reshape(
            worker_sequence, extra_slots, tokens, local_width
        )

    arrived_entry, arrived_cot = (
        lax.all_to_all(outgoing(entry_blocks), "dp", split_axis=0, concat_axis=0, tiled=True),
        lax.all_to_all(outgoing(cot_blocks), "dp", split_axis=0, concat_axis=0, tiled=True),
    )
    merged_lines = computing_worker.reshape(-1)
    entries = merged_lines.shape[0]
    assigned = (merged_lines == worker_number).astype(jnp.int32)
    places = jnp.cumsum(assigned) - 1
    holder_worker = (
        jnp.cumsum((computing_worker == worker_number).astype(jnp.int32), axis=1) - 1
    ).reshape(-1)
    micro_ids = jnp.arange(entries, dtype=jnp.int32)
    home_ids = micro_ids // micro_count
    pool_index = jnp.where(
        home_ids == worker_number,
        micro_ids % micro_count,
        micro_count + home_ids * extra_slots + holder_worker,
    )
    matches = (assigned[:, None] == 1) & (
        places[:, None] == jnp.arange(place_tally, dtype=jnp.int32)[None, :]
    )
    filled = jnp.any(matches, axis=0)
    sender_workers = jnp.sum(matches.astype(jnp.int32) * pool_index[:, None], axis=0) + (
        micro_count + worker_sequence * extra_slots
    ) * (1 - filled.astype(jnp.int32))

    def arrange_slots(blocks, arrived):
        pool = jnp.concatenate(
            [
                blocks,
                arrived.reshape(worker_sequence * extra_slots, tokens, local_width),
                zero_block,
            ],
            axis=0,
        )
        return jnp.take(pool, sender_workers, axis=0)

    full_entry, full_cot = (
        lax.all_gather(arrange_slots(entry_blocks, arrived_entry), "section", axis=2, tiled=True),
        lax.all_gather(arrange_slots(cot_blocks, arrived_cot), "section", axis=2, tiled=True),
    )
    down_weight, up_weight = (
        lax.all_gather(narrowing_weights[0], "dp", axis=1, tiled=True),
        lax.all_gather(widening_weights[0], "dp", axis=1, tiled=True),
    )
    gain_row = scaling_factor[0]
    lanes = 1

    def send_forward(value_rows):
        return shifted(value_rows, "section", 1)

    def send_backward(value_rows):
        return shifted(value_rows, "section", -1)

    groups = place_tally // lanes
    group_rows = lanes * tokens
    width = full_entry.shape[2]
    rank_width = down_weight.shape[0]
    steps = sections + groups - 1
    last_section = sections - 1

    def forward_step(step_index, carry):
        inbox, inputs_kept, inverse_kept = carry
        group_index = step_index - section_pos
        active = (group_index >= 0) & (group_index < groups)
        position = jnp.clip(group_index, 0, groups - 1)
        fresh_rows = lax.dynamic_index_in_dim(full_entry, position, 0, keepdims=False)
        current = jnp.where(section_pos == 0, fresh_rows, inbox)
        output, inverse_norm, normalized_input, preact, hidden_state = forward_section(
            current, gain_row, down_weight, up_weight
        )
        earlier = lax.dynamic_index_in_dim(inputs_kept, position, 0, keepdims=False)
        inputs_kept = lax.dynamic_update_index_in_dim(
            inputs_kept, jnp.where(active, current, earlier), position, 0
        )
        earlier_inverse = lax.dynamic_index_in_dim(inverse_kept, position, 0, keepdims=False)
        inverse_kept = lax.dynamic_update_index_in_dim(
            inverse_kept, jnp.where(active, inverse_norm[:, 0], earlier_inverse), position, 0
        )
        return (send_forward(output), inputs_kept, inverse_kept)

    forward_start = (
        jnp.zeros((group_rows, width), jnp.bfloat16),
        jnp.zeros((groups, group_rows, width), jnp.bfloat16),
        jnp.zeros((groups, group_rows), jnp.float32),
    )
    unused_inbox, inputs_kept, inverse_kept = lax.fori_loop(0, steps, forward_step, forward_start)

    def backward_core(step_index, inbox):
        group_index = step_index - (last_section - section_pos)
        active = (group_index >= 0) & (group_index < groups)
        position = jnp.clip(group_index, 0, groups - 1)
        fresh_rows = lax.dynamic_index_in_dim(full_cot, position, 0, keepdims=False)
        upstream_gradient = jnp.where(section_pos == last_section, fresh_rows, inbox)
        current = lax.dynamic_index_in_dim(inputs_kept, position, 0, keepdims=False)
        dinputs, normalized_input, hidden_state, preactivation_gradient = backward_section(
            current, gain_row, down_weight, up_weight, upstream_gradient
        )
        return (
            active,
            position,
            upstream_gradient,
            dinputs,
            normalized_input,
            hidden_state,
            preactivation_gradient,
        )

    contract_rows = (((0,), (0,)), ((), ()))

    def backward_step(step_index, carry):
        inbox, grad_down, grad_up = carry
        (
            active,
            position,
            upstream_gradient,
            dinputs,
            normalized_input,
            hidden_state,
            preactivation_gradient,
        ) = backward_core(step_index, inbox)
        grad_up = grad_up + jnp.where(
            active,
            lax.dot_general(
                hidden_state, upstream_gradient, contract_rows, preferred_element_type=jnp.float32
            ),
            0.0,
        )
        grad_down = grad_down + jnp.where(
            active,
            lax.dot_general(
                preactivation_gradient,
                normalized_input,
                contract_rows,
                preferred_element_type=jnp.float32,
            ),
            0.0,
        )
        return (send_backward(dinputs), grad_down, grad_up)

    backward_start = (
        jnp.zeros((group_rows, width), jnp.bfloat16),
        jnp.zeros((rank_width, width), jnp.float32),
        jnp.zeros((rank_width, width), jnp.float32),
    )
    unused_inbox, grad_down, grad_up = lax.fori_loop(0, steps, backward_step, backward_start)
    grad_down, grad_up = (
        lax.psum_scatter(
            grad_down.astype(jnp.bfloat16), "dp", scatter_dimension=1, tiled=True
        ).astype(jnp.float32),
        lax.psum_scatter(
            grad_up.astype(jnp.bfloat16), "dp", scatter_dimension=1, tiled=True
        ).astype(jnp.float32),
    )
    saved_state = (inverse_kept * filled.astype(jnp.float32)[:, None]).reshape(
        1, 1, place_tally * tokens
    )
    saved_inputs = inputs_kept.reshape(1, 1, place_tally * tokens, width)
    return (saved_state, saved_inputs, grad_down[None], grad_up[None])


def solution(mesh):
    in_specs = (
        P("dp", "section"),
        P("dp", "section"),
        P(),
        P("section", None),
        P("section", None, "dp"),
        P("section", None, "dp"),
    )
    out_specs = (
        P("section", "dp", None),
        P("section", "dp", None, None),
        P("section", None, "dp"),
        P("section", None, "dp"),
    )
    return jax.shard_map(body, mesh=mesh, in_specs=in_specs, out_specs=out_specs, check_vma=False)
```

profile of v0, /device:TPU:1, one launch (start us, length us, event | category | flops | bytes accessed | tf_op | source)
XLA Modules:
  0.0 1226.9 jit_solution(9888545197219009049)
XLA Ops:
  12.1 13.8 %all-to-all-start.1 = ((bf16[32,2,16,256]{3,2,1,0:T(8,128)(2,1)}), bf16[32,2,16,256]{3,2,1,0:T(8,128)(2,1)S(1)}, u32[]{:S(2)}, u32[]{:S(2)}) async-start(bf16[32,2,16,256]{3,2,1,0:T(8,128)(2,1)} %bitcast.13), calls=%async_computation.1 | async-start | bytes 1048576 | tf_op jit(solution)/shard_map/all_to_all | solution.py:100
  26.6 15.6 %all-to-all-done.1 = bf16[32,2,16,256]{3,2,1,0:T(8,128)(2,1)S(1)} async-done(((bf16[32,2,16,256]{3,2,1,0:T(8,128)(2,1)}), bf16[32,2,16,256]{3,2,1,0:T(8,128)(2,1)S(1)}, u32[]{:S(2)}, u32[]{:S(2)}) %all-to-all-start.1) | async-done | bytes 524320 | tf_op jit(solution)/shard_map/all_to_all | solution.py:100
  42.2 5.2 all-to-all-start
  49.0 13.5 %all-to-all-done = bf16[32,2,16,256]{3,2,1,0:T(8,128)(2,1)S(1)} async-done(((bf16[32,2,16,256]{3,2,1,0:T(8,128)(2,1)}), bf16[32,2,16,256]{3,2,1,0:T(8,128)(2,1)S(1)}, u32[]{:S(2)}, u32[]{:S(2)}) %all-to-all-start) | async-done | bytes 524320 | tf_op jit(solution)/shard_map/all_to_all | solution.py:99
  64.7 37.9 %all-gather = bf16[1,64,4096]{2,1,0:T(8,128)(2,1)S(1)} all-gather(bf16[1,64,128]{2,1,0:T(8,128)(2,1)S(1)} %copy-done.10), channel_id=2, replica_groups=mesh['section'=16,'dp'=32] {'dp'}, dimensions={2}, use_global_device_ids=true | all-gather | bytes 540672 | tf_op jit(solution)/shard_map/all_gather | solution.py:140
  102.5 36.4 %all-gather.1 = bf16[1,64,4096]{2,1,0:T(8,128)(2,1)S(1)} all-gather(bf16[1,64,128]{2,1,0:T(8,128)(2,1)S(1)} %copy-done.11), channel_id=3, replica_groups=mesh['section'=16,'dp'=32] {'dp'}, dimensions={2}, use_global_device_ids=true | all-gather | bytes 540672 | tf_op jit(solution)/shard_map/all_gather | solution.py:141
  140.9 295.5 %while.38 = (s32[]{:T(128)}, bf16[16,4096]{1,0:T(8,128)(2,1)S(1)}, bf16[10,16,4096]{2,1,0:T(8,128)(2,1)}, f32[10,16]{1,0:T(8,128)}, pred[]{:T(512)}, /*index=5*/...) while((s32[]{:T(128)}, bf16[16,4096]{1,0:T(8,128)(2,1)S(1)}, ...), condition=%wide.region_11.14_spmd, body=%wide.region_9.13_spmd.sunk | while | flops 17568840 | bytes 2901588 | solution.py:184
  144.8 30.0 %collective-permute-start = (bf16[16,4096]{1,0:T(8,128)(2,1)S(1)}, bf16[16,4096]{1,0:T(8,128)(2,1)S(1)}, u32[]{:S(2)}, u32[]{:S(2)}) collective-permute-start(bf16[16,4096]{1,0:T(8,128)(2,1)S(1)} %fusion.75), channel_id=1, source_target_pairs={{0,32},{32,64},{64,96},{96,128},{128,160},{160,192},{192,224},{224... | collective-permute-start | bytes 393224 | tf_op jit(solution)/shard_map/while/body/eval_jaxpr/ppermute | solution.py:18
  180.8 4.4 collective-permute-start
  191.7 4.4 collective-permute-start
  202.3 4.4 collective-permute-start
  212.7 4.3 collective-permute-start
  222.9 4.3 collective-permute-start
  233.1 4.3 collective-permute-start
  243.3 4.3 collective-permute-start
  253.5 4.3 collective-permute-start
  263.7 4.3 collective-permute-start
  273.9 4.3 collective-permute-start
  284.1 4.3 collective-permute-start
  294.3 4.3 collective-permute-start
  304.5 4.3 collective-permute-start
  314.7 5.5 collective-permute-start
  326.1 5.5 collective-permute-start
  337.6 5.5 collective-permute-start
  349.0 5.5 collective-permute-start
  360.4 5.5 collective-permute-start
  371.8 5.5 collective-permute-start
  383.2 5.5 collective-permute-start
  394.6 5.5 collective-permute-start
  406.0 5.5 collective-permute-start
  417.4 5.5 collective-permute-start
  428.9 5.5 collective-permute-start
  436.4 331.0 %while.39 = (s32[]{:T(128)}, bf16[16,4096]{1,0:T(8,128)(2,1)S(1)}, f32[64,4096]{1,0:T(8,128)S(1)}, f32[64,4096]{1,0:T(8,128)S(1)}, pred[]{:T(512)}, /*index=5*/s...) while((s32[]{:T(128)}, bf16[16,4096]{1,0:T(8,128)(2,1)S(1)}, ...), condition=%wide.region_15.18_spmd.clone, body=%wide.region_12.17_spmd.clone.sunk | while | flops 45168660 | bytes 8490592 | solution.py:243
  446.6 3.7 collective-permute-done.1
  472.6 3.7 collective-permute-done.1
  498.6 3.7 collective-permute-done.1
  520.2 1.9 collective-permute-start.1
  524.6 3.7 collective-permute-done.1
  534.1 1.9 collective-permute-start.1
  538.5 3.1 collective-permute-done.1
  551.8 3.1 collective-permute-done.1
  565.1 3.1 collective-permute-done.1
  573.9 1.9 collective-permute-start.1
  578.3 3.1 collective-permute-done.1
  587.2 1.9 collective-permute-start.1
  591.6 3.1 collective-permute-done.1
  600.5 1.9 collective-permute-start.1
  604.9 3.1 collective-permute-done.1
  618.2 3.1 collective-permute-done.1
  631.5 3.1 collective-permute-done.1
  640.4 1.9 collective-permute-start.1
  644.8 3.1 collective-permute-done.1
  653.6 1.9 collective-permute-start.1
  658.0 3.1 collective-permute-done.1
  671.3 3.1 collective-permute-done.1
  684.6 3.1 collective-permute-done.1
  697.9 3.1 collective-permute-done.1
  711.2 3.1 collective-permute-done.1
  724.4 3.1 collective-permute-done.1
  737.7 3.1 collective-permute-done.1
  751.0 3.1 collective-permute-done.1
  764.3 3.1 collective-permute-done.1
  771.1 225.2 %reduce-scatter.7.cloned.1.call-done = bf16[128,64]{1,0:T(8,128)(2,1)} async-done(((bf16[4096,64]{1,0:T(8,128)(2,1)}), bf16[128,64]{1,0:T(8,128)(2,1)}) %reduce-scatter.7.cloned.1.call-update) | async-done | bytes 16400
  997.7 221.1 %reduce-scatter.9.cloned.1.call-done = bf16[128,64]{1,0:T(8,128)(2,1)} async-done(((bf16[4096,64]{1,0:T(8,128)(2,1)}), bf16[128,64]{1,0:T(8,128)(2,1)}) %reduce-scatter.9.cloned.1.call-update) | async-done | bytes 16400
  (857 shorter events, 410.4 us)
Async XLA Ops:
  11.0 15.0 %copy-start.12 = (s32[32,8]{0,1:T(8,128)S(1)}, s32[32,8]{0,1:T(8,128)}, u32[]{:S(2)}) copy-start(s32[32,8]{0,1:T(8,128)} %param.16) | copy-start | bytes 3076
  12.1 50.4 %copy-start.4 = (bf16[128,256]{1,0:T(8,128)(2,1)S(1)}, bf16[128,256]{1,0:T(8,128)(2,1)}, u32[]{:S(2)}) copy-start(bf16[128,256]{1,0:T(8,128)(2,1)} %param.15) | copy-start | bytes 196612
  12.1 30.1 %all-to-all-start.1 = ((bf16[32,2,16,256]{3,2,1,0:T(8,128)(2,1)}), bf16[32,2,16,256]{3,2,1,0:T(8,128)(2,1)S(1)}, u32[]{:S(2)}, u32[]{:S(2)}) async-start(bf16[32,2,16,256]{3,2,1,0:T(8,128)(2,1)} %bitcast.13), calls=%async_computation.1 | async-start | bytes 1048576 | tf_op jit(solution)/shard_map/all_to_all | solution.py:100
  42.2 20.3 %all-to-all-start = ((bf16[32,2,16,256]{3,2,1,0:T(8,128)(2,1)}), bf16[32,2,16,256]{3,2,1,0:T(8,128)(2,1)S(1)}, u32[]{:S(2)}, u32[]{:S(2)}) async-start(bf16[32,2,16,256]{3,2,1,0:T(8,128)(2,1)} %bitcast.7), calls=%async_computation | async-start | bytes 1048576 | tf_op jit(solution)/shard_map/all_to_all | solution.py:99
  47.5 91.6 %all-gather.5.cloned.1.call-start = ((), (), s32[]{:S(2)}) async-start(), calls=%async_computation.4 | async-start | bytes 1392640 | tf_op jit(solution)/shard_map/all_gather | solution.py:136
  62.5 40.0 %copy-start.11 = (bf16[1,64,128]{2,1,0:T(8,128)(2,1)S(1)}, bf16[1,64,128]{2,1,0:T(8,128)(2,1)}, u32[]{:S(2)}) copy-start(bf16[1,64,128]{2,1,0:T(8,128)(2,1)} %param.19) | copy-start | bytes 49156
  64.6 371.8 %all-gather.7.cloned.1.call-start = ((), (), s32[]{:S(2)}) async-start(), calls=%async_computation.5 | async-start | bytes 1392640 | tf_op jit(solution)/shard_map/all_gather | solution.py:137
  64.7 76.2 %copy-start = (f32[1,4096]{1,0:T(1,128)S(1)}, f32[1,4096]{1,0:T(1,128)}, u32[]{:S(2)}) copy-start(f32[1,4096]{1,0:T(1,128)} %param.17) | copy-start | bytes 49156
  139.0 857.3 %reduce-scatter.7.cloned.1.call-start = ((), (), s32[]{:S(2)}) async-start(), calls=%async_computation.6 | async-start | bytes 1081344
  144.8 32.1 %collective-permute-start = (bf16[16,4096]{1,0:T(8,128)(2,1)S(1)}, bf16[16,4096]{1,0:T(8,128)(2,1)S(1)}, u32[]{:S(2)}, u32[]{:S(2)}) collective-permute-start(bf16[16,4096]{1,0:T(8,128)(2,1)S(1)} %fusion.75), channel_id=1, source_target_pairs={{0,32},{32,64},{64,96},{96,128},{128,160},{160,192},{192,224},{224... | collective-permute-start | bytes 393224 | tf_op jit(solution)/shard_map/while/body/eval_jaxpr/ppermute | solution.py:18
  180.8 7.0 collective-permute-start
  191.7 6.7 collective-permute-start
  202.3 6.4 collective-permute-start
  212.7 6.3 collective-permute-start
  222.9 6.3 collective-permute-start
  233.1 6.3 collective-permute-start
  243.3 6.3 collective-permute-start
  253.5 6.3 collective-permute-start
  263.7 6.3 collective-permute-start
  273.9 6.3 collective-permute-start
  284.1 6.3 collective-permute-start
  294.3 6.3 collective-permute-start
  304.5 6.3 collective-permute-start
  314.7 7.5 collective-permute-start
  326.1 7.5 collective-permute-start
  337.6 7.5 collective-permute-start
  349.0 7.5 collective-permute-start
  360.4 7.5 collective-permute-start
  371.8 7.5 collective-permute-start
  383.2 7.5 collective-permute-start
  394.6 7.5 collective-permute-start
  406.0 7.5 collective-permute-start
  417.4 7.5 collective-permute-start
  428.9 7.5 collective-permute-start
  442.2 8.1 collective-permute-start.1
  456.1 6.3 collective-permute-start.1
  468.2 8.1 collective-permute-start.1
  482.1 6.3 collective-permute-start.1
  494.2 8.1 collective-permute-start.1
  503.4 3.6 copy-start.6
  508.1 6.3 collective-permute-start.1
  520.2 8.1 collective-permute-start.1
  529.4 3.6 copy-start.6
  534.1 7.5 collective-permute-start.1
  547.4 7.5 collective-permute-start.1
  560.7 7.5 collective-permute-start.1
  573.9 7.5 collective-permute-start.1
  587.2 7.5 collective-permute-start.1
  595.8 3.6 copy-start.6
  600.5 7.5 collective-permute-start.1
  613.8 7.5 collective-permute-start.1
  627.1 7.5 collective-permute-start.1
  640.4 7.5 collective-permute-start.1
  653.6 7.5 collective-permute-start.1
  662.2 3.6 copy-start.6
  666.9 7.5 collective-permute-start.1
  680.2 7.5 collective-permute-start.1
  693.5 7.5 collective-permute-start.1
  706.8 7.5 collective-permute-start.1
  720.0 7.5 collective-permute-start.1
  733.3 7.5 collective-permute-start.1
  746.6 7.5 collective-permute-start.1
  759.9 7.5 collective-permute-start.1
  768.8 450.0 %reduce-scatter.9.cloned.1.call-start = ((), (), s32[]{:S(2)}) async-start(), calls=%async_computation.7 | async-start | bytes 1081344
  (150 other events, 225.1 us)
Sparse Core Ops, SparseCore 0:
  64.7 40.4 all-gather.4
  139.1 65.1 all-gather.6
  768.9 227.2 reduce-scatter.6
  1000.5 218.2 reduce-scatter.8
where the time goes:
time: 1240 us; the launch traced here: 1230 us
  waiting for transfers between devices  553 us (45%)
  starting transfers between devices  213 us (17%)
  other arithmetic  143 us (12%)
  matrix products  143 us (12%)
  local copies, waits for them, and re-layouts  82.2 us (7%)
  blocking collectives  74.2 us (6%)
  between operations  14 us (1%)
    unnamed x6, waiting for transfers between devices  446 us
    ppermute x50, starting transfers between devices, shifted(): lax.ppermute(value, axis, [(source, source + steps) for source in range(i...  194 us
    ppermute x50, waiting for transfers between devices, shifted(): lax.ppermute(value, axis, [(source, source + steps) for source in range(i...  77.4 us
    dynamic_update_slice x25, other arithmetic, forward_step(): lax.dynamic_update_index_in_dim(inputs_kept, jnp.where(active, current, e...  40.5 us
    all_gather x1, blocking collectives, body(): lax.all_gather(narrowing_weights[0], 'dp', axis=1, tiled=True)  37.9 us
    all_gather x1, blocking collectives, body(): lax.all_gather(widening_weights[0], 'dp', axis=1, tiled=True)  36.4 us
    dot_general x25, matrix products, backward_step(): lax.dot_general(preactivation_gradient, normalized_input, contract_rows,...  32.7 us
    dynamic_update_slice x25, local copies, waits for them, and re-layouts, forward_step(): lax.dynamic_update_index_in_dim(inverse_kept, jnp.where(active, inverse_n...  32.4 us
  transfers between devices with their start and end apart: 56, of which 32 were waited for; matrix products, arithmetic and copies ran while one was open for 16% of the time, Pallas kernels for 0%

commit v1 on v0

v1 whole, which is shorter than its diff:
```python
import jax
import jax.numpy as jnp
from jax import lax
from jax.experimental import pallas as pl
from jax.experimental.pallas import tpu as pltpu
from jax.sharding import PartitionSpec as P


EPS = 1e-05
SECT = 16
DP = 32
RANK = 64
D = 4096
F = 256
ROWS = 128
PAIR = 32
PIECE = 4224
BACK = 2432
GW = 1152
F32 = jnp.float32
BF = jnp.bfloat16
NT = (((1,), (1,)), ((), ()))
NN = (((1,), (0,)), ((), ()))
Y_GROUPS = [[2 * y + c for y in range(8)] for c in range(2)]
VMEM_LIMIT = 48 * 1024 * 1024


def dot(a, b, dims):
    return lax.dot_general(a, b, dims, preferred_element_type=F32)


def hi_lo(v):
    hi = v.astype(BF).astype(F32)
    return hi, v - hi


def vmem(n):
    return [pl.BlockSpec(memory_space=pltpu.VMEM)] * n


SMEM = pl.BlockSpec(memory_space=pltpu.SMEM)


def project_kernel(ints, x_ref, pair_ref, g_ref, w_ref, out_ref, wc_ref, uc_ref, ex_ref, gr_ref, mi_ref):
    for s in range(SECT):
        for h in range(2):
            block = w_ref[2 * s + h]
            lanes = slice(128 * h, 128 * h + 128)
            wc_ref[128 * s : 128 * s + 128, lanes] = block
            uc_ref[64 * s : 64 * s + 64, lanes] = block[64:128]
    x = x_ref[...]
    pair = pair_ref[...]
    out_ref[:, 0:2048] = dot(x, wc_ref[...], NT).astype(BF)
    out_ref[:, 2048:3072] = dot(g_ref[...], uc_ref[...], NT).astype(BF)
    extra = dot(pair, wc_ref[...], NT)
    for i in range(2):
        for k in range(4):
            for b in range(4):
                at = 512 * k + 128 * b
                ex_ref[pl.ds(128 * b + 4 * i + k, 16, stride=8), :] = extra[16 * i : 16 * i + 16, at : at + 128]
    for b in range(4):
        out_ref[:, 3072 + 128 * b : 3200 + 128 * b] = ex_ref[128 * b : 128 * b + 128, :].astype(BF)

    p = ints[0]
    quarter = ints[1]
    m = p // 2 + 1
    small_rows = wc_ref[pl.ds(pl.multiple_of(128 * p + 32 * quarter, 32), 32), :]
    big_rows = wc_ref[pl.ds(pl.multiple_of(128 * (15 - p) + 32 * quarter, 32), 32), :]
    small = dot(small_rows, uc_ref[0:512, :], NT)
    big = dot(big_rows, uc_ref[...], NT)
    st = [small[:, 128 * t : 128 * t + 128] for t in range(4)]
    tiles = [big[:, 128 * t : 128 * t + 128] for t in range(8)]
    tiles.append(st[3])
    for t in range(5, 9):
        for mm in range(1, 5):
            j = t - (9 - mm)
            if 0 <= j < 4:
                tiles[t] = jnp.where(m == mm, st[j], tiles[t])
    gr_ref[...] = jnp.zeros_like(gr_ref)
    for c in range(2):
        for y in range(8):
            rows = slice(8 * (2 * y + c), 8 * (2 * y + c) + 8)
            for b in range(2 if y == 7 else 1):
                tile = tiles[y + b]
                gr_ref[rows, 128 * b : 128 * b + 128] = tile[16 * c : 16 * c + 8]
                gr_ref[rows, 256 + 128 * b : 384 + 128 * b] = tile[16 * c + 8 : 16 * c + 16]
    out_ref[:, 3584:4096] = gr_ref[...].astype(BF)

    xf = x.astype(F32)
    pf = pair.astype(F32)
    own_hi, own_lo = hi_lo(jnp.sum(xf * xf, axis=1, keepdims=True))
    pair_hi, pair_lo = hi_lo(jnp.sum(pf * pf, axis=1, keepdims=True))
    mi_ref[...] = jnp.zeros_like(mi_ref)
    lane = lax.broadcasted_iota(jnp.int32, (PAIR, 128), 1)
    pair_part = jnp.where(lane == 2, pair_hi, 0.0) + jnp.where(lane == 3, pair_lo, 0.0)
    for i in range(2):
        mi_ref[pl.ds(i, 16, stride=8), :] = pair_part[16 * i : 16 * i + 16]
    lane = lax.broadcasted_iota(jnp.int32, (ROWS, 128), 1)
    own_part = jnp.where(lane == 0, own_hi, 0.0) + jnp.where(lane == 1, own_lo, 0.0)
    out_ref[:, 4096:4224] = (mi_ref[...] + own_part).astype(BF)


def slab_place(s):
    if s >= 8:
        return 15 - s, 0
    return s, 128 * (9 - (s // 2 + 1))


def recur_kernel(ints, sum_ref, mine_ref, other_ref, out_ref, slab_ref, pq_ref, h_ref, acc_ref, t_ref, pre_ref, ds_ref, ho_ref):
    core = ints[0]
    mine_row = pl.multiple_of(16 * core, 16)
    other_row = pl.multiple_of(16 * (1 - core), 16)
    for q in range(DP):
        base = 128 * (q // 4) + 32 * (q % 4)
        slab_ref[pl.ds(base + mine_row, 16), :] = mine_ref[q]
        slab_ref[pl.ds(base + other_row, 16), :] = other_ref[q]
    pq_ref[...] = jnp.zeros_like(pq_ref)
    pq_ref[0:8, :] = sum_ref[:, 0:3072]
    for i in range(2):
        for k in range(4):
            pq_ref[8 + i : 9 + i, 512 * k : 512 * k + 512] = sum_ref[4 * i + k : 4 * i + k + 1, 3072:3584]
    h_ref[...] = jnp.zeros_like(h_ref)
    acc_ref[...] = jnp.zeros_like(acc_ref)
    misc = sum_ref[:, 4096:4224]
    n = jnp.concatenate([misc[:, 0:1] + misc[:, 1:2], misc[:, 2:3] + misc[:, 3:4]], axis=0)
    row = lax.broadcasted_iota(jnp.int32, (16, 1), 0)
    n = jnp.where(row < 10, n, 0.0)

    inverse = []
    zeros = jnp.zeros((16, RANK), BF)
    for s in range(SECT):
        place, off = slab_place(s)
        r0 = 128 * place
        depth = 128 * ((s + 1) // 2)
        tp = pq_ref[:, 128 * s : 128 * s + 64]
        tq = pq_ref[:, 128 * s + 64 : 128 * s + 128]
        if s:
            before = h_ref[:, 0:depth]
            tp = tp + dot(before, slab_ref[r0 : r0 + 64, off : off + depth], NT)
            tq = tq + dot(before, slab_ref[r0 + 64 : r0 + 128, off : off + depth], NT)
        inv = lax.rsqrt(jnp.maximum(n, 0.0) * (1.0 / D) + EPS)
        inverse.append(inv)
        pre = inv * tp
        sig = 1.0 / (1.0 + jnp.exp(-pre))
        hf = pre * sig
        h = hf.astype(BF)
        pre_ref[:, 64 * s : 64 * s + 64] = pre
        ds_ref[:, 64 * s : 64 * s + 64] = sig * (1.0 + pre * (1.0 - sig))
        tile = slice(128 * (s // 2), 128 * (s // 2) + 128)
        own = jnp.concatenate([zeros, h] if s % 2 else [h, zeros], axis=1)
        h_ref[:, tile] = h_ref[:, tile] + own if s % 2 else own
        hd = dot(own, slab_ref[r0 + 64 : r0 + 128, off + tile.start : off + tile.stop], NT)
        n = n + jnp.sum(h.astype(F32) * (2.0 * tq + hd), axis=1, keepdims=True)
        t_ref[:, 64 * s : 64 * s + 64] = tq + hd

    lane16 = lax.broadcasted_iota(jnp.int32, (16, 128), 1)
    beta_sum = jnp.zeros((16, 1), F32)
    misc_out = jnp.zeros((16, 128), F32)
    for s in range(SECT - 1, -1, -1):
        place, off = slab_place(s)
        r0 = 128 * place
        cols = slice(64 * s, 64 * s + 64)
        inv = inverse[s]
        hf = h_ref[:, cols].astype(F32)
        dh = pq_ref[:, 2048 + 64 * s : 2048 + 64 * s + 64] + acc_ref[:, cols] - beta_sum * t_ref[:, cols]
        dp = (dh * ds_ref[:, cols]).astype(BF).astype(F32)
        beta = inv * inv * (jnp.sum(dp * pre_ref[:, cols], axis=1, keepdims=True) * (1.0 / D))
        z = (inv * dp).astype(BF)
        hb = (beta_sum * hf).astype(BF)
        depth = 128 * ((s + 1) // 2)
        for start in range(depth - 128, -1, -128):
            part = slice(start, start + 128)
            acc_ref[:, part] = (
                acc_ref[:, part]
                + dot(z, slab_ref[r0 : r0 + 64, off + start : off + start + 128], NN)
                - dot(hb, slab_ref[r0 + 64 : r0 + 128, off + start : off + start + 128], NN)
            )
        beta_sum = beta_sum + beta
        ho_ref[0:8, 1024 + 64 * s : 1024 + 64 * s + 64] = z[0:8].astype(F32)
        inv_hi, inv_lo = hi_lo(inv)
        misc_out = jnp.where(lane16 == s, beta, misc_out)
        misc_out = jnp.where(lane16 == 16 + s, inv_hi, misc_out)
        misc_out = jnp.where(lane16 == 32 + s, inv_lo, misc_out)
    h_all = h_ref[...].astype(F32)
    ho_ref[0:8, 0:1024] = h_all[0:8]
    for i in range(2):
        for k in range(4):
            ho_ref[4 * i + k : 4 * i + k + 1, 2048:2304] = h_all[8 + i : 9 + i, 256 * k : 256 * k + 256]
    extra_misc = pltpu.roll(misc_out[8:16], 32, 1)
    lane8 = lax.broadcasted_iota(jnp.int32, (8, 128), 1)
    row8 = lax.broadcasted_iota(jnp.int32, (8, 128), 0)
    keep = (lane8 >= 48) & (lane8 < 80) & (row8 < 2)
    ho_ref[0:8, 2304:2432] = jnp.where(keep, extra_misc, jnp.where(lane8 < 48, misc_out[0:8], 0.0))
    out_ref[...] = ho_ref[...].astype(BF)


def rebuild_kernel(ints, x_ref, pair_ref, back_ref, eh_ref, wc_ref, out_ref):
    own_at = pl.multiple_of(ints[0], 32)
    pair_at = pl.multiple_of(ints[1], 32)
    alive = ints[2] > 0
    x = x_ref[...].astype(F32)
    e = pair_ref[...].astype(F32)
    for s in range(SECT):
        out_ref[s, pl.ds(own_at, ROWS), :] = jnp.where(alive, x, 0.0).astype(BF)
        out_ref[s, pl.ds(pair_at, PAIR), :] = e.astype(BF)
        if s < SECT - 1:
            up = wc_ref[128 * s + 64 : 128 * s + 128, :]
            x = x + dot(back_ref[:, 64 * s : 64 * s + 64], up, NN)
            e = e + dot(eh_ref[:, 64 * s : 64 * s + 64], up, NN)


def grads_kernel(x_ref, g_ref, back_ref, wc_ref, out_ref, xs_ref, ht_ref, zt_ref):
    ht_ref[...] = back_ref[:, 0:1024].T
    zt_ref[...] = back_ref[:, 1024:2048].T
    x = x_ref[...].astype(F32)
    for s in range(SECT):
        xs_ref[s] = x.astype(BF)
        if s < SECT - 1:
            x = x + dot(back_ref[:, 64 * s : 64 * s + 64], wc_ref[128 * s + 64 : 128 * s + 128, :], NN)
    g = g_ref[...].astype(F32)
    betas = back_ref[:, 2304:2432].astype(F32)
    for s in range(SECT - 1, -1, -1):
        xs = xs_ref[s]
        up = dot(ht_ref[64 * s : 64 * s + 64, :], g.astype(BF), NN).astype(BF)
        down = dot(zt_ref[64 * s : 64 * s + 64, :], xs, NN).astype(BF)
        for h in range(2):
            lanes = slice(128 * h, 128 * h + 128)
            out_ref[2 * s + h, 0:64, :] = up[:, lanes]
            out_ref[2 * s + h, 64:128, :] = down[:, lanes]
        if s:
            z = back_ref[:, 1024 + 64 * s : 1024 + 64 * s + 64]
            g = g + dot(z, wc_ref[128 * s : 128 * s + 64, :], NN) - betas[:, s : s + 1] * xs.astype(F32)


def call(kernel, n_in, outs, scratch, flops, nbytes, with_ints=True):
    return pl.pallas_call(
        kernel,
        out_shape=outs,
        in_specs=([SMEM] if with_ints else []) + vmem(n_in),
        out_specs=jax.tree.map(lambda _: pl.BlockSpec(memory_space=pltpu.VMEM), outs),
        scratch_shapes=scratch,
        compiler_params=pltpu.CompilerParams(vmem_limit_bytes=VMEM_LIMIT),
        cost_estimate=pl.CostEstimate(flops=flops, bytes_accessed=nbytes, transcendentals=0),
    )


def shape(*dims, kind=BF):
    return jax.ShapeDtypeStruct(dims, kind)


def exchange(value, axis, groups=None):
    return lax.all_to_all(value, axis, 0, 0, tiled=True, axis_index_groups=groups)


def body(x, g, worker, gain, narrow, widen):
    sec = lax.axis_index("section")
    me = lax.axis_index("dp")

    gain_here = lax.dynamic_slice(gain, (0, 128 * me), (1, 128))
    block = jnp.concatenate([(narrow[0].astype(F32) * gain_here).astype(BF), widen[0]], axis=0)
    there = [(s * DP + d, (d // 2) * DP + 2 * s + d % 2) for s in range(SECT) for d in range(DP)]
    back_again = [(b, a) for a, b in there]
    block = lax.ppermute(block, ("section", "dp"), there)

    owners = jnp.arange(DP, dtype=jnp.int32)
    takers = worker[:, ::2]
    mine = lax.dynamic_index_in_dim(takers, me, 0, keepdims=False)
    alive = mine[0] == me
    goes = (mine[None, :] == owners[:, None]) & jnp.logical_not(alive)
    quads = x.reshape(4, PAIR, F)
    outgoing = jnp.zeros((DP, PAIR, F), BF)
    for j in range(4):
        outgoing = jnp.where(goes[:, j][:, None, None], quads[j][None], outgoing)
    arrived = exchange(outgoing, "dp")
    comes = jnp.any((takers == me) & (owners != me)[:, None], axis=1)
    source = jnp.sum(jnp.where(comes, owners, 0))
    taking = jnp.any(comes)
    pair = lax.dynamic_index_in_dim(arrived, source, 0, keepdims=False)
    pair = jnp.where(taking, pair, jnp.zeros_like(pair))
    pair_first = taking & (source < me)

    weights = exchange(jnp.broadcast_to(block[None], (DP, 128, 128)), "dp")
    pieces, wc = call(
        project_kernel,
        4,
        (shape(ROWS, PIECE), shape(2048, F)),
        [
            pltpu.VMEM((1024, F), BF),
            pltpu.VMEM((4 * ROWS, 128), F32),
            pltpu.VMEM((ROWS, 512), F32),
            pltpu.VMEM((ROWS, 128), F32),
        ],
        3 * 10**8,
        3 * 10**6,
    )(jnp.stack([me // 4, me % 4]).astype(jnp.int32), x, pair, g, weights)
    pieces = exchange(pieces.reshape(SECT, 8, PIECE), "section")
    total = jnp.sum(pieces.astype(F32), axis=0)

    share = jnp.concatenate([total[:, 3584:3840], total[:, 3840:4096]], axis=0).astype(BF)
    share = exchange(jnp.broadcast_to(share[None], (8, 16, 256)), "section", Y_GROUPS)
    share = jnp.concatenate([share[y, :, 0:128] for y in range(8)] + [share[7, :, 128:256]], axis=1)
    half = exchange(jnp.broadcast_to(share[None], (DP, 16, GW)), "dp")
    other = lax.ppermute(half, "section", [(i, i ^ 1) for i in range(SECT)])

    back = call(
        recur_kernel,
        3,
        shape(8, BACK),
        [
            pltpu.VMEM((1024, GW), BF),
            pltpu.VMEM((16, 3072), F32),
            pltpu.VMEM((16, 1024), BF),
            pltpu.VMEM((16, 1024), F32),
            pltpu.VMEM((16, 1024), F32),
            pltpu.VMEM((16, 1024), F32),
            pltpu.VMEM((16, 1024), F32),
            pltpu.VMEM((8, BACK), F32),
        ],
        2 * 10**8,
        3 * 10**6,
    )((sec % 2).reshape(1).astype(jnp.int32), total, half, other)
    back = exchange(jnp.broadcast_to(back[None], (SECT, 8, BACK)), "section")

    grads = call(
        grads_kernel,
        4,
        shape(DP, 128, 128),
        [pltpu.VMEM((SECT, ROWS, F), BF), pltpu.VMEM((1024, ROWS), BF), pltpu.VMEM((1024, ROWS), BF)],
        3 * 10**8,
        3 * 10**6,
        False,
    )(x, g, back.reshape(ROWS, BACK), wc)
    grads = exchange(grads, "dp")
    grads = jnp.sum(grads.astype(F32), axis=0)
    grads = lax.ppermute(grads, ("section", "dp"), back_again)

    extra_h = back[:, :, 2048:2304].reshape(SECT, 2, 4, 256).transpose(1, 0, 2, 3).reshape(PAIR, 1024)
    own_at = jnp.where(pair_first, PAIR, 0)
    pair_at = jnp.where(pair_first, 0, ROWS)
    rows_out = call(
        rebuild_kernel,
        5,
        shape(SECT, ROWS + PAIR, F),
        [],
        2 * 10**8,
        3 * 10**6,
    )(jnp.stack([own_at, pair_at, alive.astype(jnp.int32)]).astype(jnp.int32), x, pair, back.reshape(ROWS, BACK), extra_h, wc)
    saved = exchange(rows_out, "section")
    saved = saved.transpose(1, 0, 2).reshape(1, 1, ROWS + PAIR, D)

    misc = back[:, :, 2304:2432].astype(F32)
    own_inv = misc[:, :, 16:32] + misc[:, :, 32:48]
    pair_inv = misc[:, 0:2, 48:64] + misc[:, 0:2, 64:80]
    own_inv = lax.dynamic_index_in_dim(own_inv, sec, 2, keepdims=False).reshape(ROWS)
    pair_inv = lax.dynamic_index_in_dim(pair_inv, sec, 2, keepdims=False).T.reshape(PAIR)
    own_inv = jnp.where(alive, own_inv, 0.0)
    pair_inv = jnp.where(taking, pair_inv, 0.0)
    rstd = jnp.where(
        pair_first, jnp.concatenate([pair_inv, own_inv]), jnp.concatenate([own_inv, pair_inv])
    ).reshape(1, 1, ROWS + PAIR)
    return rstd, saved, (grads[64:128] * gain_here)[None], grads[0:64][None]


def solution(mesh):
    in_specs = (
        P("dp", "section"),
        P("dp", "section"),
        P(),
        P("section", None),
        P("section", None, "dp"),
        P("section", None, "dp"),
    )
    out_specs = (
        P("section", "dp", None),
        P("section", "dp", None, None),
        P("section", None, "dp"),
        P("section", None, "dp"),
    )
    return jax.shard_map(body, mesh=mesh, in_specs=in_specs, out_specs=out_specs, check_vma=False)
```

time: 1240 us -> 279 us (0.23)
  waiting for transfers between devices: 553 us -> 82.9 us
  starting transfers between devices: 213 us -> 47 us
  matrix products: 143 us -> 0 us
  other arithmetic: 143 us -> 6.92 us
  local copies, waits for them, and re-layouts: 82.2 us -> 6.36 us
  blocking collectives: 74.2 us -> 108 us
  Pallas kernels: 0 us -> 17.9 us
    unnamed x6 -> x0, waiting for transfers between devices: 446 us -> none
    ppermute x50 -> x3, starting transfers between devices: 194 us -> 15.8 us  [the longest x1 5.76 us: body(): block = lax.ppermute(block, ('section', 'dp'), there)]
    dot_general x150 -> x0, matrix products: 143 us -> none  [the longest x25 32.7 us: backward_step(): lax.dot_general(preactivation_gradient, normalized_input, contract_rows,...]
    all_to_all x0 -> x4, blocking collectives: none -> 108 us  [exchange(): lax.all_to_all(value, axis, 0, 0, tiled=True, axis_index_groups=groups)]
    all_gather x2 -> x0, blocking collectives: 74.2 us -> none  [the longest x1 37.9 us: body(): lax.all_gather(narrowing_weights[0], 'dp', axis=1, tiled=True)]
    ppermute x50 -> x3, waiting for transfers between devices: 77.4 us -> 6.86 us  [the longest x1 2.57 us: body(): other = lax.ppermute(half, 'section', [(i, i ^ 1) for i in range(SECT)])]
    all_to_all x2 -> x4, waiting for transfers between devices: 29.2 us -> 76 us  [exchange(): lax.all_to_all(value, axis, 0, 0, tiled=True, axis_index_groups=groups)]
    dynamic_update_slice x25 -> x0, other arithmetic: 40.5 us -> none  [forward_step(): lax.dynamic_update_index_in_dim(inputs_kept, jnp.where(active, current, e...]
  transfers between devices with their start and end apart: 56 -> 7, of which waited for: 32 -> 7; matrix products, arithmetic and copies ran while one was open for 16% -> 2% of each run, Pallas kernels for 0% -> 1%
where the time goes in v1:
time: 279 us; the launch traced here: 274 us
  blocking collectives  108 us (39%)
  waiting for transfers between devices  82.9 us (30%)
  starting transfers between devices  47 us (17%)
  Pallas kernels  17.9 us (6%)
  other arithmetic  6.92 us (2%)
  local copies, waits for them, and re-layouts  6.36 us (2%)
  between operations  4.86 us (2%)
    all_to_all x4, blocking collectives, exchange(): lax.all_to_all(value, axis, 0, 0, tiled=True, axis_index_groups=groups)  108 us
    all_to_all x4, waiting for transfers between devices, exchange(): lax.all_to_all(value, axis, 0, 0, tiled=True, axis_index_groups=groups)  76 us
    all_to_all x4, starting transfers between devices, exchange(): lax.all_to_all(value, axis, 0, 0, tiled=True, axis_index_groups=groups)  31.1 us
    pallas_call x1, Pallas kernels, body(): call(recur_kernel, 3, shape(8, BACK), [pltpu.VMEM((1024, GW), BF), pltpu....  11.8 us
    ppermute x1, starting transfers between devices, body(): block = lax.ppermute(block, ('section', 'dp'), there)  5.76 us
  transfers between devices with their start and end apart: 7, of which 7 were waited for; matrix products, arithmetic and copies ran while one was open for 2% of the time, Pallas kernels for 1%

profile of v1, /device:TPU:1, one launch (start us, length us, event | category | flops | bytes accessed | tf_op | source)
XLA Modules:
  0.0 274.3 jit_solution(9701566930410608566)
XLA Ops:
  0.6 0.0 copy-start
  0.6 0.0 copy-start.3
  0.7 0.0 copy-start.4
  0.7 0.7 slice.94
  1.4 0.2 fusion.8
  1.6 0.5 slice.95
  2.7 0.1 fusion.5
  2.8 0.8 fusion.12
  3.6 1.0 select_select_fusion
  4.6 13.7 %all-to-all-start = ((bf16[32,32,256]{2,1,0:T(8,128)(2,1)}), bf16[32,32,256]{2,1,0:T(8,128)(2,1)S(1)}, u32[]{:S(2)}, u32[]{:S(2)}) async-start(bf16[32,32,256]{2,1,0:T(8,128)(2,1)} %select_select_fusion), calls=%async_computation | async-start | bytes 1048576 | tf_op jit(solution)/shard_map/all_to_all | solution.py:252
  18.3 0.0 copy-done
  18.4 0.0 copy-done.3
  18.4 0.0 copy-done.4
  18.4 5.8 %collective-permute-start = (bf16[128,128]{1,0:T(8,128)(2,1)S(1)}, bf16[128,128]{1,0:T(8,128)(2,1)S(1)}, u32[]{:S(2)}, u32[]{:S(2)}) collective-permute-start(bf16[128,128]{1,0:T(8,128)(2,1)S(1)} %pad_maximum_fusion), channel_id=1, source_target_pairs={{0,0},{1,1},{2,32},{3,33},{4,64},{5,65},{6,96},{7,97},{8,128},{9,1... | collective-permute-start | bytes 98312 | tf_op jit(solution)/shard_map/ppermute | solution.py:263
  24.2 2.3 collective-permute-done
  26.5 8.4 %all-to-all-done = bf16[32,32,256]{2,1,0:T(8,128)(2,1)S(1)} async-done(((bf16[32,32,256]{2,1,0:T(8,128)(2,1)}), bf16[32,32,256]{2,1,0:T(8,128)(2,1)S(1)}, u32[]{:S(2)}, u32[]{:S(2)}) %all-to-all-start) | async-done | bytes 524320 | tf_op jit(solution)/shard_map/all_to_all | solution.py:252
  34.9 1.2 broadcast_in_dim.120
  36.1 0.0 copy-start.1
  36.1 0.0 copy-start.2
  36.1 7.9 %all-to-all-start.1 = ((bf16[32,128,128]{2,1,0:T(8,128)(2,1)}), bf16[32,128,128]{2,1,0:T(8,128)(2,1)S(1)}, u32[]{:S(2)}, u32[]{:S(2)}) async-start(bf16[32,128,128]{2,1,0:T(8,128)(2,1)} %broadcast_in_dim.120), calls=%async_computation.1 | async-start | bytes 2097152 | tf_op jit(solution)/shard_map/all_to_all | solution.py:252
  44.0 0.6 fusion.7
  44.7 0.6 select_reduce_fusion
  47.2 0.1 pad_add_fusion.ints
  47.3 0.7 select_bitcast_fusion.pair_ref
  48.0 20.8 %all-to-all-done.1.w_ref = bf16[32,128,128]{2,1,0:T(8,128)(2,1)S(1)} async-done(((bf16[32,128,128]{2,1,0:T(8,128)(2,1)}), bf16[32,128,128]{2,1,0:T(8,128)(2,1)S(1)}, u32[]{:S(2)}, u32[]{:S(2)}) %all-to-all-start.1) | async-done | bytes 1048608 | tf_op jit(solution)/shard_map/all_to_all | solution.py:252
  68.8 0.0 copy-done.1
  68.8 0.0 copy-done.2
  68.8 1.8 shard_map.93
  70.6 41.2 %all_to_all.40 = bf16[16,8,4224]{2,1,0:T(8,128)(2,1)S(1)} all-to-all(bf16[16,8,4224]{2,1,0:T(8,128)(2,1)S(1)} %bitcast.77), channel_id=1, replica_groups=mesh['section'=16,'dp'=32] {'section'}, dimensions={0} | all-to-all | bytes 2162688 | tf_op jit(solution)/shard_map/all_to_all | solution.py:252
  111.8 0.1 convert_reduce_fusion.sum_ref
  112.0 9.5 %all_to_all.41 = bf16[8,16,256]{2,1,0:T(8,128)(2,1)S(1)} all-to-all(bf16[8,16,256]{2,1,0:T(8,128)(2,1)S(1)} %broadcast_in_dim.121), channel_id=1, replica_groups={{0,64,128,192,256,320,384,448},{32,96,160,224,288,352,416,480},{1,65,12..., dimensions={0} | all-to-all | bytes 131072 | tf_op jit(solution)/shard_map/all_to_all | solution.py:252
  121.6 0.1 broadcast_in_dim.122
  121.7 35.3 %all_to_all.42.mine_ref = bf16[32,16,1152]{2,1,0:T(8,128)(2,1)S(1)} all-to-all(bf16[32,16,1152]{2,1,0:T(8,128)(2,1)S(1)} %broadcast_in_dim.122), channel_id=1, replica_groups=mesh['section'=16,'dp'=32] {'dp'}, dimensions={0} | all-to-all | bytes 2359296 | tf_op jit(solution)/shard_map/all_to_all | solution.py:252
  156.9 5.3 %collective-permute-start.1 = (bf16[32,16,1152]{2,1,0:T(8,128)(2,1)S(1)}, bf16[32,16,1152]{2,1,0:T(8,128)(2,1)}, u32[]{:S(2)}, u32[]{:S(2)}) collective-permute-start(bf16[32,16,1152]{2,1,0:T(8,128)(2,1)S(1)} %all_to_all.42.mine_ref), channel_id=1, source_target_pairs={{0,32},{32,0},{64,96},{96,64},{128,160},{160,128},{192,224},{224,1... | collective-permute-start | bytes 3538952 | tf_op jit(solution)/shard_map/ppermute | solution.py:303
  162.3 2.6 collective-permute-done.1.other_ref
  164.8 11.8 %shard_map.94 = bf16[8,2432]{1,0:T(8,128)(2,1)S(1)} custom-call(s32[1]{0:T(128)} %bitcast.ints, f32[8,4224]{1,0:T(8,128)S(1)} %convert_reduce_fusion.sum_ref, bf16[32,16,1152]{2,1,0:T(8,128)(2,1)S(1)} %all_to_all.42.mine_ref, bf16[32,16,1152]{2,1,0:T(8,128)(2,1)} %collective-permute-done.1.other_ref), custom_call_target="tpu_custom_call" | custom-call | flops 200000000 | bytes 3000000 | tf_op jit(solution)/shard_map/pallas_call | solution.py:305
  176.7 22.5 %all_to_all.43 = bf16[16,8,2432]{2,1,0:T(8,128)(2,1)S(1)} all-to-all(bf16[16,8,2432]{2,1,0:T(8,128)(2,1)S(1)} %broadcast_in_dim.123), channel_id=1, replica_groups=mesh['section'=16,'dp'=32] {'section'}, dimensions={0} | all-to-all | bytes 1245184 | tf_op jit(solution)/shard_map/all_to_all | solution.py:252
  199.2 2.2 shard_map.96
  201.4 4.7 %all-to-all-start.7 = ((bf16[32,128,128]{2,1,0:T(8,128)(2,1)}), bf16[32,128,128]{2,1,0:T(8,128)(2,1)}, u32[]{:S(2)}, u32[]{:S(2)}) async-start(bf16[32,128,128]{2,1,0:T(8,128)(2,1)} %shard_map.96), calls=%async_computation.7 | async-start | bytes 2097152 | tf_op jit(solution)/shard_map/all_to_all | solution.py:252
  207.4 0.1 pad_add_fusion.1.ints
  207.6 2.1 shard_map.95
  209.7 24.3 %all-to-all-done.7 = bf16[32,128,128]{2,1,0:T(8,128)(2,1)} async-done(((bf16[32,128,128]{2,1,0:T(8,128)(2,1)}), bf16[32,128,128]{2,1,0:T(8,128)(2,1)}, u32[]{:S(2)}, u32[]{:S(2)}) %all-to-all-start.7) | async-done | bytes 1048608 | tf_op jit(solution)/shard_map/all_to_all | solution.py:252
  234.0 4.9 %all-to-all-start.6 = ((bf16[16,160,256]{2,1,0:T(8,128)(2,1)}), bf16[16,160,256]{2,1,0:T(8,128)(2,1)S(1)}, u32[]{:S(2)}, u32[]{:S(2)}) async-start(bf16[16,160,256]{2,1,0:T(8,128)(2,1)} %shard_map.95), calls=%async_computation.6 | async-start | bytes 2621440 | tf_op jit(solution)/shard_map/all_to_all | solution.py:252
  238.9 0.1 fusion.10
  239.0 0.7 fusion.4
  239.7 0.1 copy.22
  239.8 0.1 concatenate.41
  239.9 0.1 fusion.11
  240.0 0.2 fusion.1
  240.2 0.1 concatenate.42
  240.3 1.4 convert_reduce_fusion.1
  241.7 4.7 %collective-permute-start.2 = (f32[128,128]{1,0:T(8,128)S(1)}, f32[128,128]{1,0:T(8,128)S(1)}, u32[]{:S(2)}, u32[]{:S(2)}) collective-permute-start(f32[128,128]{1,0:T(8,128)S(1)} %convert_reduce_fusion.1), channel_id=1, source_target_pairs={{0,0},{1,1},{32,2},{33,3},{64,4},{65,5},{96,6},{97,7},{128,8},{129... | collective-permute-start | bytes 196616 | tf_op jit(solution)/shard_map/ppermute | solution.py:335
  246.4 0.6 broadcast_select_fusion
  247.1 2.0 collective-permute-done.2
  249.1 0.6 slice_bitcast_fusion
  249.7 22.4 %all-to-all-done.6 = bf16[16,160,256]{2,1,0:T(8,128)(2,1)S(1)} async-done(((bf16[16,160,256]{2,1,0:T(8,128)(2,1)}), bf16[16,160,256]{2,1,0:T(8,128)(2,1)S(1)}, u32[]{:S(2)}, u32[]{:S(2)}) %all-to-all-start.6) | async-done | bytes 1310752 | tf_op jit(solution)/shard_map/all_to_all | solution.py:252
  272.1 0.7 copy.25
  272.9 1.5 reshape.138
  (24 shorter events, 0.2 us)
Async XLA Ops:
  0.6 17.7 %copy-start = (f32[1,4096]{1,0:T(1,128)S(1)}, f32[1,4096]{1,0:T(1,128)}, u32[]{:S(2)}) copy-start(f32[1,4096]{1,0:T(1,128)} %param.9) | copy-start | bytes 49156
  0.6 17.7 %copy-start.3 = (bf16[1,64,128]{2,1,0:T(8,128)(2,1)S(1)}, bf16[1,64,128]{2,1,0:T(8,128)(2,1)}, u32[]{:S(2)}) copy-start(bf16[1,64,128]{2,1,0:T(8,128)(2,1)} %param.10) | copy-start | bytes 49156
  0.7 17.7 %copy-start.4 = (bf16[1,64,128]{2,1,0:T(8,128)(2,1)S(1)}, bf16[1,64,128]{2,1,0:T(8,128)(2,1)}, u32[]{:S(2)}) copy-start(bf16[1,64,128]{2,1,0:T(8,128)(2,1)} %param.11) | copy-start | bytes 49156
  4.6 30.3 %all-to-all-start = ((bf16[32,32,256]{2,1,0:T(8,128)(2,1)}), bf16[32,32,256]{2,1,0:T(8,128)(2,1)S(1)}, u32[]{:S(2)}, u32[]{:S(2)}) async-start(bf16[32,32,256]{2,1,0:T(8,128)(2,1)} %select_select_fusion), calls=%async_computation | async-start | bytes 1048576 | tf_op jit(solution)/shard_map/all_to_all | solution.py:252
  18.4 8.1 %collective-permute-start = (bf16[128,128]{1,0:T(8,128)(2,1)S(1)}, bf16[128,128]{1,0:T(8,128)(2,1)S(1)}, u32[]{:S(2)}, u32[]{:S(2)}) collective-permute-start(bf16[128,128]{1,0:T(8,128)(2,1)S(1)} %pad_maximum_fusion), channel_id=1, source_target_pairs={{0,0},{1,1},{2,32},{3,33},{4,64},{5,65},{6,96},{7,97},{8,128},{9,1... | collective-permute-start | bytes 98312 | tf_op jit(solution)/shard_map/ppermute | solution.py:263
  36.1 32.7 %copy-start.1 = (bf16[128,256]{1,0:T(8,128)(2,1)S(1)}, bf16[128,256]{1,0:T(8,128)(2,1)}, u32[]{:S(2)}) copy-start(bf16[128,256]{1,0:T(8,128)(2,1)} %x_ref.5) | copy-start | bytes 196612
  36.1 32.7 %copy-start.2 = (bf16[128,256]{1,0:T(8,128)(2,1)S(1)}, bf16[128,256]{1,0:T(8,128)(2,1)}, u32[]{:S(2)}) copy-start(bf16[128,256]{1,0:T(8,128)(2,1)} %g_ref.3) | copy-start | bytes 196612
  36.1 32.7 %all-to-all-start.1 = ((bf16[32,128,128]{2,1,0:T(8,128)(2,1)}), bf16[32,128,128]{2,1,0:T(8,128)(2,1)S(1)}, u32[]{:S(2)}, u32[]{:S(2)}) async-start(bf16[32,128,128]{2,1,0:T(8,128)(2,1)} %broadcast_in_dim.120), calls=%async_computation.1 | async-start | bytes 2097152 | tf_op jit(solution)/shard_map/all_to_all | solution.py:252
  156.9 7.9 %collective-permute-start.1 = (bf16[32,16,1152]{2,1,0:T(8,128)(2,1)S(1)}, bf16[32,16,1152]{2,1,0:T(8,128)(2,1)}, u32[]{:S(2)}, u32[]{:S(2)}) collective-permute-start(bf16[32,16,1152]{2,1,0:T(8,128)(2,1)S(1)} %all_to_all.42.mine_ref), channel_id=1, source_target_pairs={{0,32},{32,0},{64,96},{96,64},{128,160},{160,128},{192,224},{224,1... | collective-permute-start | bytes 3538952 | tf_op jit(solution)/shard_map/ppermute | solution.py:303
  201.4 32.6 %all-to-all-start.7 = ((bf16[32,128,128]{2,1,0:T(8,128)(2,1)}), bf16[32,128,128]{2,1,0:T(8,128)(2,1)}, u32[]{:S(2)}, u32[]{:S(2)}) async-start(bf16[32,128,128]{2,1,0:T(8,128)(2,1)} %shard_map.96), calls=%async_computation.7 | async-start | bytes 2097152 | tf_op jit(solution)/shard_map/all_to_all | solution.py:252
  234.0 38.1 %all-to-all-start.6 = ((bf16[16,160,256]{2,1,0:T(8,128)(2,1)}), bf16[16,160,256]{2,1,0:T(8,128)(2,1)S(1)}, u32[]{:S(2)}, u32[]{:S(2)}) async-start(bf16[16,160,256]{2,1,0:T(8,128)(2,1)} %shard_map.95), calls=%async_computation.6 | async-start | bytes 2621440 | tf_op jit(solution)/shard_map/all_to_all | solution.py:252
  241.7 7.4 %collective-permute-start.2 = (f32[128,128]{1,0:T(8,128)S(1)}, f32[128,128]{1,0:T(8,128)S(1)}, u32[]{:S(2)}, u32[]{:S(2)}) collective-permute-start(f32[128,128]{1,0:T(8,128)S(1)} %convert_reduce_fusion.1), channel_id=1, source_target_pairs={{0,0},{1,1},{32,2},{33,3},{64,4},{65,5},{96,6},{97,7},{128,8},{129... | collective-permute-start | bytes 196616 | tf_op jit(solution)/shard_map/ppermute | solution.py:335

commit v2 on v1

--- a/solution.py
+++ b/solution.py
@@ -14,7 +14,7 @@
 F = 256
 ROWS = 128
 PAIR = 32
-PIECE = 4224
+PIECE = 3712
 BACK = 2432
 GW = 1152
 F32 = jnp.float32
@@ -41,17 +41,23 @@
 SMEM = pl.BlockSpec(memory_space=pltpu.SMEM)
 
 
-def project_kernel(ints, x_ref, pair_ref, g_ref, w_ref, out_ref, wc_ref, uc_ref, ex_ref, gr_ref, mi_ref):
+def project_kernel(ints, x_ref, g_ref, w_ref, keep_ref, send_ref, wc_ref, pair_ref, uc_ref, res_ref, gr_ref, ex_ref):
+    p, quarter, core, source = ints[0], ints[1], ints[2], ints[3]
+    taking = ints[4] > 0
     for s in range(SECT):
         for h in range(2):
-            block = w_ref[2 * s + h]
+            block = w_ref[2 * s + h, 0:128, :]
             lanes = slice(128 * h, 128 * h + 128)
             wc_ref[128 * s : 128 * s + 128, lanes] = block
             uc_ref[64 * s : 64 * s + 64, lanes] = block[64:128]
+    for h in range(2):
+        part = w_ref[source, 128 + 32 * h : 160 + 32 * h, :]
+        pair_ref[:, 128 * h : 128 * h + 128] = jnp.where(taking, part, jnp.zeros_like(part))
+
     x = x_ref[...]
     pair = pair_ref[...]
-    out_ref[:, 0:2048] = dot(x, wc_ref[...], NT).astype(BF)
-    out_ref[:, 2048:3072] = dot(g_ref[...], uc_ref[...], NT).astype(BF)
+    res_ref[:, 0:2048] = dot(x, wc_ref[...], NT)
+    res_ref[:, 2048:3072] = dot(g_ref[...], uc_ref[...], NT)
     extra = dot(pair, wc_ref[...], NT)
     for i in range(2):
         for k in range(4):
@@ -59,10 +65,21 @@
                 at = 512 * k + 128 * b
                 ex_ref[pl.ds(128 * b + 4 * i + k, 16, stride=8), :] = extra[16 * i : 16 * i + 16, at : at + 128]
     for b in range(4):
-        out_ref[:, 3072 + 128 * b : 3200 + 128 * b] = ex_ref[128 * b : 128 * b + 128, :].astype(BF)
-
-    p = ints[0]
-    quarter = ints[1]
+        res_ref[:, 3072 + 128 * b : 3200 + 128 * b] = ex_ref[128 * b : 128 * b + 128, :]
+
+    xf = x.astype(F32)
+    pf = pair.astype(F32)
+    own_hi, own_lo = hi_lo(jnp.sum(xf * xf, axis=1, keepdims=True))
+    pair_hi, pair_lo = hi_lo(jnp.sum(pf * pf, axis=1, keepdims=True))
+    ex_ref[0:ROWS, :] = jnp.zeros((ROWS, 128), F32)
+    lane = lax.broadcasted_iota(jnp.int32, (PAIR, 128), 1) - 4 * core
+    pair_part = jnp.where(lane == 2, pair_hi, 0.0) + jnp.where(lane == 3, pair_lo, 0.0)
+    for i in range(2):
+        ex_ref[pl.ds(i, 16, stride=8), :] = pair_part[16 * i : 16 * i + 16]
+    lane = lax.broadcasted_iota(jnp.int32, (ROWS, 128), 1) - 4 * core
+    own_part = jnp.where(lane == 0, own_hi, 0.0) + jnp.where(lane == 1, own_lo, 0.0)
+    res_ref[:, 3584:3712] = ex_ref[0:ROWS, :] + own_part
+
     m = p // 2 + 1
     small_rows = wc_ref[pl.ds(pl.multiple_of(128 * p + 32 * quarter, 32), 32), :]
     big_rows = wc_ref[pl.ds(pl.multiple_of(128 * (15 - p) + 32 * quarter, 32), 32), :]
@@ -76,28 +93,16 @@
             j = t - (9 - mm)
             if 0 <= j < 4:
                 tiles[t] = jnp.where(m == mm, st[j], tiles[t])
-    gr_ref[...] = jnp.zeros_like(gr_ref)
-    for c in range(2):
-        for y in range(8):
-            rows = slice(8 * (2 * y + c), 8 * (2 * y + c) + 8)
-            for b in range(2 if y == 7 else 1):
-                tile = tiles[y + b]
-                gr_ref[rows, 128 * b : 128 * b + 128] = tile[16 * c : 16 * c + 8]
-                gr_ref[rows, 256 + 128 * b : 384 + 128 * b] = tile[16 * c + 8 : 16 * c + 16]
-    out_ref[:, 3584:4096] = gr_ref[...].astype(BF)
-
-    xf = x.astype(F32)
-    pf = pair.astype(F32)
-    own_hi, own_lo = hi_lo(jnp.sum(xf * xf, axis=1, keepdims=True))
-    pair_hi, pair_lo = hi_lo(jnp.sum(pf * pf, axis=1, keepdims=True))
-    mi_ref[...] = jnp.zeros_like(mi_ref)
-    lane = lax.broadcasted_iota(jnp.int32, (PAIR, 128), 1)
-    pair_part = jnp.where(lane == 2, pair_hi, 0.0) + jnp.where(lane == 3, pair_lo, 0.0)
-    for i in range(2):
-        mi_ref[pl.ds(i, 16, stride=8), :] = pair_part[16 * i : 16 * i + 16]
-    lane = lax.broadcasted_iota(jnp.int32, (ROWS, 128), 1)
-    own_part = jnp.where(lane == 0, own_hi, 0.0) + jnp.where(lane == 1, own_lo, 0.0)
-    out_ref[:, 4096:4224] = (mi_ref[...] + own_part).astype(BF)
+    for t in range(9):
+        gr_ref[:, 128 * t : 128 * t + 128] = tiles[t]
+
+    for ref, parity in ((keep_ref, core), (send_ref, 1 - core)):
+        for y in range(0, 8, 2):
+            first = res_ref[pl.ds(pl.multiple_of(16 * y + 8 * parity, 8), 8), :]
+            second = res_ref[pl.ds(pl.multiple_of(16 * y + 16 + 8 * parity, 8), 8), :]
+            ref[8 * y : 8 * y + 16, :] = jnp.concatenate([first, second], axis=0).astype(BF)
+        ref[64:80, 0:GW] = gr_ref[pl.ds(pl.multiple_of(16 * parity, 16), 16), :].astype(BF)
+        ref[64:80, GW:PIECE] = jnp.zeros((16, PIECE - GW), BF)
 
 
 def slab_place(s):
@@ -116,12 +121,14 @@
         slab_ref[pl.ds(base + other_row, 16), :] = other_ref[q]
     pq_ref[...] = jnp.zeros_like(pq_ref)
     pq_ref[0:8, :] = sum_ref[:, 0:3072]
+    more = sum_ref[:, 3072:3584]
     for i in range(2):
         for k in range(4):
-            pq_ref[8 + i : 9 + i, 512 * k : 512 * k + 512] = sum_ref[4 * i + k : 4 * i + k + 1, 3072:3584]
+            pq_ref[8 + i : 9 + i, 512 * k : 512 * k + 512] = more[4 * i + k : 4 * i + k + 1]
     h_ref[...] = jnp.zeros_like(h_ref)
     acc_ref[...] = jnp.zeros_like(acc_ref)
-    misc = sum_ref[:, 4096:4224]
+    misc = sum_ref[:, 3584:3712]
+    misc = misc + pltpu.roll(misc, 124, 1)
     n = jnp.concatenate([misc[:, 0:1] + misc[:, 1:2], misc[:, 2:3] + misc[:, 3:4]], axis=0)
     row = lax.broadcasted_iota(jnp.int32, (16, 1), 0)
     n = jnp.where(row < 10, n, 0.0)
@@ -209,7 +216,8 @@
             e = e + dot(eh_ref[:, 64 * s : 64 * s + 64], up, NN)
 
 
-def grads_kernel(x_ref, g_ref, back_ref, wc_ref, out_ref, xs_ref, ht_ref, zt_ref):
+def grads_kernel(ints, x_ref, g_ref, back_ref, wc_ref, keep_ref, send_ref, xs_ref, ht_ref, zt_ref):
+    upper = ints[0] > 0
     ht_ref[...] = back_ref[:, 0:1024].T
     zt_ref[...] = back_ref[:, 1024:2048].T
     x = x_ref[...].astype(F32)
@@ -223,13 +231,17 @@
         xs = xs_ref[s]
         up = dot(ht_ref[64 * s : 64 * s + 64, :], g.astype(BF), NN).astype(BF)
         down = dot(zt_ref[64 * s : 64 * s + 64, :], xs, NN).astype(BF)
-        for h in range(2):
-            lanes = slice(128 * h, 128 * h + 128)
-            out_ref[2 * s + h, 0:64, :] = up[:, lanes]
-            out_ref[2 * s + h, 64:128, :] = down[:, lanes]
+        for rows, value in ((slice(0, 64), up), (slice(64, 128), down)):
+            keep_ref[s, rows, :] = jnp.where(upper, value[:, 128:256], value[:, 0:128])
+            send_ref[s, rows, :] = jnp.where(upper, value[:, 0:128], value[:, 128:256])
         if s:
             z = back_ref[:, 1024 + 64 * s : 1024 + 64 * s + 64]
             g = g + dot(z, wc_ref[128 * s : 128 * s + 64, :], NN) - betas[:, s : s + 1] * xs.astype(F32)
+
+
+def join_kernel(in_ref, out_ref):
+    for k in range(SECT):
+        out_ref[0, 0, :, F * k : F * k + F] = in_ref[k]
 
 
 def call(kernel, n_in, outs, scratch, flops, nbytes, with_ints=True):
@@ -252,55 +264,71 @@
     return lax.all_to_all(value, axis, 0, 0, tiled=True, axis_index_groups=groups)
 
 
+def scatter_sum(keep, send, me):
+    for b in range(4):
+        value = keep.astype(F32) + lax.ppermute(send, "dp", [(i, i ^ (1 << b)) for i in range(DP)]).astype(F32)
+        value = value.astype(BF).reshape((value.shape[0] // 2, 2) + value.shape[1:])
+        bit = (me >> (b + 1)) & 1
+        keep = lax.dynamic_index_in_dim(value, bit, 1, keepdims=False)
+        send = lax.dynamic_index_in_dim(value, 1 - bit, 1, keepdims=False)
+    both = ("section", "dp")
+    mine = lax.ppermute(keep[0], both, [(a, owner(a // DP, a % DP)) for a in range(SECT * DP)])
+    theirs = lax.ppermute(send[0], both, [(a, owner(a // DP, a % DP ^ 16)) for a in range(SECT * DP)])
+    return mine.astype(F32) + theirs.astype(F32)
+
+
+def owner(sec, q):
+    return (q // 2) * DP + 2 * sec + q % 2
+
+
 def body(x, g, worker, gain, narrow, widen):
     sec = lax.axis_index("section")
     me = lax.axis_index("dp")
 
     gain_here = lax.dynamic_slice(gain, (0, 128 * me), (1, 128))
     block = jnp.concatenate([(narrow[0].astype(F32) * gain_here).astype(BF), widen[0]], axis=0)
-    there = [(s * DP + d, (d // 2) * DP + 2 * s + d % 2) for s in range(SECT) for d in range(DP)]
-    back_again = [(b, a) for a, b in there]
-    block = lax.ppermute(block, ("section", "dp"), there)
+    block = lax.ppermute(block, ("section", "dp"), [(owner(a // DP, a % DP), a) for a in range(SECT * DP)])
 
     owners = jnp.arange(DP, dtype=jnp.int32)
     takers = worker[:, ::2]
     mine = lax.dynamic_index_in_dim(takers, me, 0, keepdims=False)
     alive = mine[0] == me
-    goes = (mine[None, :] == owners[:, None]) & jnp.logical_not(alive)
-    quads = x.reshape(4, PAIR, F)
-    outgoing = jnp.zeros((DP, PAIR, F), BF)
-    for j in range(4):
-        outgoing = jnp.where(goes[:, j][:, None, None], quads[j][None], outgoing)
-    arrived = exchange(outgoing, "dp")
     comes = jnp.any((takers == me) & (owners != me)[:, None], axis=1)
     source = jnp.sum(jnp.where(comes, owners, 0))
     taking = jnp.any(comes)
-    pair = lax.dynamic_index_in_dim(arrived, source, 0, keepdims=False)
-    pair = jnp.where(taking, pair, jnp.zeros_like(pair))
     pair_first = taking & (source < me)
-
-    weights = exchange(jnp.broadcast_to(block[None], (DP, 128, 128)), "dp")
-    pieces, wc = call(
+    goes = (mine[None, :] == owners[:, None]) & jnp.logical_not(alive)
+    quads = jnp.concatenate([x[:, 0:128].reshape(4, PAIR, 128), x[:, 128:256].reshape(4, PAIR, 128)], axis=1)
+    outgoing = jnp.zeros((DP, 2 * PAIR, 128), BF)
+    for j in range(4):
+        outgoing = jnp.where(goes[:, j][:, None, None], quads[j][None], outgoing)
+    weights = jnp.concatenate([jnp.broadcast_to(block[None], (DP, 128, 128)), outgoing], axis=1)
+    weights = exchange(weights, "dp")
+
+    core = sec % 2
+    keep, send, wc, pair = call(
         project_kernel,
-        4,
-        (shape(ROWS, PIECE), shape(2048, F)),
+        3,
+        (shape(80, PIECE), shape(80, PIECE), shape(2048, F), shape(PAIR, F)),
         [
             pltpu.VMEM((1024, F), BF),
+            pltpu.VMEM((ROWS, PIECE), F32),
+            pltpu.VMEM((32, GW), F32),
             pltpu.VMEM((4 * ROWS, 128), F32),
-            pltpu.VMEM((ROWS, 512), F32),
-            pltpu.VMEM((ROWS, 128), F32),
         ],
-        3 * 10**8,
+        4 * 10**8,
         3 * 10**6,
-    )(jnp.stack([me // 4, me % 4]).astype(jnp.int32), x, pair, g, weights)
-    pieces = exchange(pieces.reshape(SECT, 8, PIECE), "section")
-    total = jnp.sum(pieces.astype(F32), axis=0)
-
-    share = jnp.concatenate([total[:, 3584:3840], total[:, 3840:4096]], axis=0).astype(BF)
-    share = exchange(jnp.broadcast_to(share[None], (8, 16, 256)), "section", Y_GROUPS)
-    share = jnp.concatenate([share[y, :, 0:128] for y in range(8)] + [share[7, :, 128:256]], axis=1)
+    )(jnp.stack([me // 4, me % 4, core, source, taking.astype(jnp.int32)]).astype(jnp.int32), x, g, weights)
+    swap = [(i, i ^ 1) for i in range(SECT)]
+    pieces = (keep.astype(F32) + lax.ppermute(send, "section", swap).astype(F32)).astype(BF)
+    share = jnp.concatenate([pieces[64:72, 0:GW], pieces[72:80, 0:GW]], axis=1)
+    pieces = jnp.concatenate(
+        [pieces[0:64].reshape(8, 8, PIECE), jnp.broadcast_to(share[None], (8, 8, 2 * GW))], axis=2
+    )
+    total = jnp.sum(exchange(pieces, "section", Y_GROUPS).astype(F32), axis=0)
+    share = jnp.concatenate([total[:, PIECE : PIECE + GW], total[:, PIECE + GW :]], axis=0).astype(BF)
     half = exchange(jnp.broadcast_to(share[None], (DP, 16, GW)), "dp")
-    other = lax.ppermute(half, "section", [(i, i ^ 1) for i in range(SECT)])
+    other = lax.ppermute(half, "section", swap)
 
     back = call(
         recur_kernel,
@@ -318,21 +346,18 @@
         ],
         2 * 10**8,
         3 * 10**6,
-    )((sec % 2).reshape(1).astype(jnp.int32), total, half, other)
+    )(core.reshape(1).astype(jnp.int32), total, half, other)
     back = exchange(jnp.broadcast_to(back[None], (SECT, 8, BACK)), "section")
 
-    grads = call(
+    keep, send = call(
         grads_kernel,
         4,
-        shape(DP, 128, 128),
+        (shape(SECT, 128, 128), shape(SECT, 128, 128)),
         [pltpu.VMEM((SECT, ROWS, F), BF), pltpu.VMEM((1024, ROWS), BF), pltpu.VMEM((1024, ROWS), BF)],
         3 * 10**8,
         3 * 10**6,
-        False,
-    )(x, g, back.reshape(ROWS, BACK), wc)
-    grads = exchange(grads, "dp")
-    grads = jnp.sum(grads.astype(F32), axis=0)
-    grads = lax.ppermute(grads, ("section", "dp"), back_again)
+    )((me % 2).reshape(1).astype(jnp.int32), x, g, back.reshape(ROWS, BACK), wc)
+    grads = scatter_sum(keep, send, me)
 
     extra_h = back[:, :, 2048:2304].reshape(SECT, 2, 4, 256).transpose(1, 0, 2, 3).reshape(PAIR, 1024)
     own_at = jnp.where(pair_first, PAIR, 0)
@@ -346,7 +371,7 @@
         3 * 10**6,
     )(jnp.stack([own_at, pair_at, alive.astype(jnp.int32)]).astype(jnp.int32), x, pair, back.reshape(ROWS, BACK), extra_h, wc)
     saved = exchange(rows_out, "section")
-    saved = saved.transpose(1, 0, 2).reshape(1, 1, ROWS + PAIR, D)
+    saved = call(join_kernel, 1, shape(1, 1, ROWS + PAIR, D), [], 0, 3 * 10**6, False)(saved)
 
     misc = back[:, :, 2304:2432].astype(F32)
     own_inv = misc[:, :, 16:32] + misc[:, :, 32:48]

time: 279 us -> 246 us (0.88); the launches traced: 274 us -> 245 us
  blocking collectives: 108 us -> 61.7 us
  starting transfers between devices: 47 us -> 66.6 us
    all_to_all x4 -> x2, blocking collectives: 108 us -> 61.7 us  [exchange(): lax.all_to_all(value, axis, 0, 0, tiled=True, axis_index_groups=groups)]
    ppermute x3 -> x9, starting transfers between devices: 15.8 us -> 39.8 us  [the longest x4 9.71 us: scatter_sum(): lax.ppermute(send, 'dp', [(i, i ^ 1 << b) for i in range(DP)]).astype(F32)]
    all_to_all x4 -> x3, waiting for transfers between devices: 76 us -> 52.3 us  [exchange(): lax.all_to_all(value, axis, 0, 0, tiled=True, axis_index_groups=groups)]
    ppermute x3 -> x9, waiting for transfers between devices: 6.86 us -> 29.3 us  [the longest x4 21.6 us: scatter_sum(): lax.ppermute(send, 'dp', [(i, i ^ 1 << b) for i in range(DP)]).astype(F32)]
    all_to_all x4 -> x3, starting transfers between devices: 31.1 us -> 26.8 us  [exchange(): lax.all_to_all(value, axis, 0, 0, tiled=True, axis_index_groups=groups)]
  transfers between devices with their start and end apart: 7 -> 12, of which waited for: 7 -> 9; matrix products, arithmetic and copies ran while one was open for 2% -> 4% of each run, Pallas kernels for 1% -> 1%
where the time goes in v2:
time: 246 us; the launch traced here: 245 us
  waiting for transfers between devices  81.5 us (33%)
  starting transfers between devices  66.6 us (27%)
  blocking collectives  61.7 us (25%)
  Pallas kernels  17.8 us (7%)
  other arithmetic  8.22 us (3%)
  local copies, waits for them, and re-layouts  5.48 us (2%)
  between operations  3.65 us (1%)
    all_to_all x2, blocking collectives, exchange(): lax.all_to_all(value, axis, 0, 0, tiled=True, axis_index_groups=groups)  61.7 us
    all_to_all x3, waiting for transfers between devices, exchange(): lax.all_to_all(value, axis, 0, 0, tiled=True, axis_index_groups=groups)  52.3 us
    all_to_all x3, starting transfers between devices, exchange(): lax.all_to_all(value, axis, 0, 0, tiled=True, axis_index_groups=groups)  26.8 us
    ppermute x4, waiting for transfers between devices, scatter_sum(): lax.ppermute(send, 'dp', [(i, i ^ 1 << b) for i in range(DP)]).astype(F32)  21.6 us
    pallas_call x1, Pallas kernels, body(): call(recur_kernel, 3, shape(8, BACK), [pltpu.VMEM((1024, GW), BF), pltpu....  10.6 us
    ppermute x4, starting transfers between devices, scatter_sum(): lax.ppermute(send, 'dp', [(i, i ^ 1 << b) for i in range(DP)]).astype(F32)  9.71 us
    ppermute x1, starting transfers between devices, scatter_sum(): lax.ppermute(send[0], both, [(a, owner(a // DP, a % DP ^ 16)) for a in ra...  7.33 us
    ppermute x1, starting transfers between devices, body(): lax.ppermute(send, 'section', swap).astype(F32)  6.32 us
  transfers between devices with their start and end apart: 12, of which 9 were waited for; matrix products, arithmetic and copies ran while one was open for 4% of the time, Pallas kernels for 1%

profile of v2, /device:TPU:1, one launch (start us, length us, event | category | flops | bytes accessed | tf_op | source)
XLA Modules:
  0.0 245.0 jit_solution(6880408967442043539)
XLA Ops:
  0.6 0.0 copy-start
  0.7 0.7 copy-done
  1.4 0.7 fusion.6
  2.1 0.7 pad_maximum_fusion.4
  2.8 6.0 %collective-permute-start = (bf16[128,128]{1,0:T(8,128)(2,1)S(1)}, bf16[128,128]{1,0:T(8,128)(2,1)S(1)}, u32[]{:S(2)}, u32[]{:S(2)}) collective-permute-start(bf16[128,128]{1,0:T(8,128)(2,1)S(1)} %pad_maximum_fusion.4), channel_id=1, source_target_pairs={{0,0},{1,1},{32,2},{33,3},{64,4},{65,5},{96,6},{97,7},{128,8},{129... | collective-permute-start | bytes 98312 | tf_op jit(solution)/shard_map/ppermute | solution.py:290
  8.8 0.7 slice.78
  9.5 0.2 fusion.18
  9.7 0.5 slice.79
  10.9 0.1 fusion.15
  11.0 0.8 fusion.23
  11.8 0.2 select_select_fusion
  12.0 0.0 collective-permute-done
  12.0 0.2 broadcast_in_dim.111
  12.2 1.3 pad_maximum_fusion
  13.5 19.4 %all-to-all-start = ((bf16[32,192,128]{2,1,0:T(8,128)(2,1)}), bf16[32,192,128]{2,1,0:T(8,128)(2,1)S(1)}, u32[]{:S(2)}, u32[]{:S(2)}) async-start(bf16[32,192,128]{2,1,0:T(8,128)(2,1)} %pad_maximum_fusion), calls=%async_computation | async-start | bytes 3145728 | tf_op jit(solution)/shard_map/all_to_all | solution.py:264
  33.0 0.6 fusion.17
  34.3 0.6 select_reduce_fusion
  34.9 0.7 stack.39.ints
  35.7 32.9 %all-to-all-done.w_ref = bf16[32,192,128]{2,1,0:T(8,128)(2,1)S(1)} async-done(((bf16[32,192,128]{2,1,0:T(8,128)(2,1)}), bf16[32,192,128]{2,1,0:T(8,128)(2,1)S(1)}, u32[]{:S(2)}, u32[]{:S(2)}) %all-to-all-start) | async-done | bytes 1572896 | tf_op jit(solution)/shard_map/all_to_all | solution.py:264
  68.6 0.0 copy-done.1
  68.6 1.9 shard_map.93
  70.5 6.3 %collective-permute-start.1 = (bf16[80,3712]{1,0:T(8,128)(2,1)S(1)}, bf16[80,3712]{1,0:T(8,128)(2,1)S(1)}, u32[]{:S(2)}, u32[]{:S(2)}) collective-permute-start(bf16[80,3712]{1,0:T(8,128)(2,1)S(1)} %get-tuple-element.11), channel_id=1, source_target_pairs={{0,32},{32,0},{64,96},{96,64},{128,160},{160,128},{192,224},{224,1... | collective-permute-start | bytes 1781768 | tf_op jit(solution)/shard_map/ppermute | solution.py:323
  76.8 1.6 collective-permute-done.1
  78.4 0.2 add_convert_fusion
  78.7 0.1 pad_maximum_fusion.1
  78.8 26.3 %all_to_all.25 = bf16[8,8,6016]{2,1,0:T(8,128)(2,1)S(1)} all-to-all(bf16[8,8,6016]{2,1,0:T(8,128)(2,1)S(1)} %pad_maximum_fusion.1), channel_id=1, replica_groups={{0,64,128,192,256,320,384,448},{32,96,160,224,288,352,416,480},{1,65,12..., dimensions={0} | all-to-all | bytes 1540096 | tf_op jit(solution)/shard_map/all_to_all | solution.py:264
  105.1 0.1 convert_reduce_fusion.sum_ref
  105.3 0.1 broadcast_in_dim.130
  105.4 35.4 %all_to_all.26.mine_ref = bf16[32,16,1152]{2,1,0:T(8,128)(2,1)S(1)} all-to-all(bf16[32,16,1152]{2,1,0:T(8,128)(2,1)S(1)} %broadcast_in_dim.130), channel_id=1, replica_groups=mesh['section'=16,'dp'=32] {'dp'}, dimensions={0} | all-to-all | bytes 2359296 | tf_op jit(solution)/shard_map/all_to_all | solution.py:264
  140.7 5.7 %collective-permute-start.2 = (bf16[32,16,1152]{2,1,0:T(8,128)(2,1)S(1)}, bf16[32,16,1152]{2,1,0:T(8,128)(2,1)S(1)}, u32[]{:S(2)}, u32[]{:S(2)}) collective-permute-start(bf16[32,16,1152]{2,1,0:T(8,128)(2,1)S(1)} %all_to_all.26.mine_ref), channel_id=1, source_target_pairs={{0,32},{32,0},{64,96},{96,64},{128,160},{160,128},{192,224},{224,1... | collective-permute-start | bytes 3538952 | tf_op jit(solution)/shard_map/ppermute | solution.py:331
  146.5 2.5 %collective-permute-done.2.other_ref = bf16[32,16,1152]{2,1,0:T(8,128)(2,1)S(1)} collective-permute-done((bf16[32,16,1152]{2,1,0:T(8,128)(2,1)S(1)}, bf16[32,16,1152]{2,1,0:T(8,128)(2,1)S(1)}, u32[]{:S(2)}, u32[]{:S(2)}) %collective-permute-start.2) | collective-permute-done | bytes 1179680 | tf_op jit(solution)/shard_map/ppermute | solution.py:331
  148.9 10.6 %shard_map.94 = bf16[8,2432]{1,0:T(8,128)(2,1)S(1)} custom-call(s32[1]{0:T(128)} %bitcast.ints, f32[8,6016]{1,0:T(8,128)S(1)} %convert_reduce_fusion.sum_ref, bf16[32,16,1152]{2,1,0:T(8,128)(2,1)S(1)} %all_to_all.26.mine_ref, bf16[32,16,1152]{2,1,0:T(8,128)(2,1)S(1)} %collective-permute-done.2.other_ref), custom_call_target="tpu_custom_call" | custom-call | flops 200000000 | bytes 3000000 | tf_op jit(solution)/shard_map/pallas_call | solution.py:333
  159.5 0.9 broadcast_in_dim.131
  160.4 3.8 %all-to-all-start.3 = ((bf16[16,8,2432]{2,1,0:T(8,128)(2,1)}), bf16[16,8,2432]{2,1,0:T(8,128)(2,1)S(1)}, u32[]{:S(2)}, u32[]{:S(2)}) async-start(bf16[16,8,2432]{2,1,0:T(8,128)(2,1)} %broadcast_in_dim.131), calls=%async_computation.3 | async-start | bytes 1245184 | tf_op jit(solution)/shard_map/all_to_all | solution.py:264
  164.1 19.3 %all-to-all-done.3 = bf16[16,8,2432]{2,1,0:T(8,128)(2,1)S(1)} async-done(((bf16[16,8,2432]{2,1,0:T(8,128)(2,1)}), bf16[16,8,2432]{2,1,0:T(8,128)(2,1)S(1)}, u32[]{:S(2)}, u32[]{:S(2)}) %all-to-all-start.3) | async-done | bytes 622624 | tf_op jit(solution)/shard_map/all_to_all | solution.py:264
  183.5 2.0 shard_map.97
  185.5 1.9 collective-permute-start.3
  188.7 0.1 pad_add_fusion.ints
  188.9 2.1 shard_map.95
  191.0 3.6 %all-to-all-start.4 = ((bf16[16,160,256]{2,1,0:T(8,128)(2,1)}), bf16[16,160,256]{2,1,0:T(8,128)(2,1)S(1)}, u32[]{:S(2)}, u32[]{:S(2)}) async-start(bf16[16,160,256]{2,1,0:T(8,128)(2,1)} %shard_map.95), calls=%async_computation.4 | async-start | bytes 2621440 | tf_op jit(solution)/shard_map/all_to_all | solution.py:264
  194.6 6.0 %collective-permute-done.3 = bf16[16,128,128]{2,1,0:T(8,128)(2,1)} collective-permute-done((bf16[16,128,128]{2,1,0:T(8,128)(2,1)}, bf16[16,128,128]{2,1,0:T(8,128)(2,1)}, u32[]{:S(2)}, u32[]{:S(2)}) %collective-permute-start.3) | collective-permute-done | bytes 524320 | tf_op jit(solution)/shard_map/ppermute | solution.py:269
  200.5 1.2 add_convert_fusion.1
  201.8 2.7 %collective-permute-start.4 = (bf16[8,128,128]{2,1,0:T(8,128)(2,1)S(1)}, bf16[8,128,128]{2,1,0:T(8,128)(2,1)S(1)}, u32[]{:S(2)}, u32[]{:S(2)}) collective-permute-start(bf16[8,128,128]{2,1,0:T(8,128)(2,1)S(1)} %dynamic-slice_bitcast_fusion), channel_id=1, source_target_pairs={{0,2},{1,3},{2,0},{3,1},{4,6},{5,7},{6,4},{7,5},{8,10},{9,11},{10,... | collective-permute-start | bytes 786440 | tf_op jit(solution)/shard_map/ppermute | solution.py:269
  204.4 0.1 fusion.22
  204.5 8.9 %collective-permute-done.4 = bf16[8,128,128]{2,1,0:T(8,128)(2,1)S(1)} collective-permute-done((bf16[8,128,128]{2,1,0:T(8,128)(2,1)S(1)}, bf16[8,128,128]{2,1,0:T(8,128)(2,1)S(1)}, u32[]{:S(2)}, u32[]{:S(2)}) %collective-permute-start.4) | collective-permute-done | bytes 262176 | tf_op jit(solution)/shard_map/ppermute | solution.py:269
  213.5 0.1 fusion
  213.6 2.4 collective-permute-start.5
  216.0 0.1 fusion.21
  216.1 4.1 %collective-permute-done.5 = bf16[4,128,128]{2,1,0:T(8,128)(2,1)S(1)} collective-permute-done((bf16[4,128,128]{2,1,0:T(8,128)(2,1)S(1)}, bf16[4,128,128]{2,1,0:T(8,128)(2,1)S(1)}, u32[]{:S(2)}, u32[]{:S(2)}) %collective-permute-start.5) | collective-permute-done | bytes 131104 | tf_op jit(solution)/shard_map/ppermute | solution.py:269
  220.2 2.7 %collective-permute-start.6 = (bf16[2,128,128]{2,1,0:T(8,128)(2,1)S(1)}, bf16[2,128,128]{2,1,0:T(8,128)(2,1)S(1)}, u32[]{:S(2)}, u32[]{:S(2)}) collective-permute-start(bf16[2,128,128]{2,1,0:T(8,128)(2,1)S(1)} %dynamic-slice_bitcast_fusion.2), channel_id=1, source_target_pairs={{0,8},{1,9},{2,10},{3,11},{4,12},{5,13},{6,14},{7,15},{8,0},{9,1},... | collective-permute-start | bytes 196616 | tf_op jit(solution)/shard_map/ppermute | solution.py:269
  223.0 0.7 fusion.13
  223.7 0.1 copy.21
  223.8 0.1 concatenate.53
  223.9 0.2 fusion.4
  224.1 0.1 concatenate.54
  224.2 2.7 %collective-permute-done.6 = bf16[2,128,128]{2,1,0:T(8,128)(2,1)S(1)} collective-permute-done((bf16[2,128,128]{2,1,0:T(8,128)(2,1)S(1)}, bf16[2,128,128]{2,1,0:T(8,128)(2,1)S(1)}, u32[]{:S(2)}, u32[]{:S(2)}) %collective-permute-start.6) | collective-permute-done | bytes 65568 | tf_op jit(solution)/shard_map/ppermute | solution.py:269
  226.9 4.7 %collective-permute-start.7 = (bf16[128,128]{1,0:T(8,128)(2,1)S(1)}, bf16[128,128]{1,0:T(8,128)(2,1)S(1)}, u32[]{:S(2)}, u32[]{:S(2)}) collective-permute-start(bf16[128,128]{1,0:T(8,128)(2,1)S(1)} %get-tuple-element.26), channel_id=1, source_target_pairs={{0,0},{1,1},{2,32},{3,33},{4,64},{5,65},{6,96},{7,97},{8,128},{9,1... | collective-permute-start | bytes 98312 | tf_op jit(solution)/shard_map/ppermute | solution.py:275
  231.6 7.3 %collective-permute-start.8 = (bf16[128,128]{1,0:T(8,128)(2,1)S(1)}, bf16[128,128]{1,0:T(8,128)(2,1)S(1)}, u32[]{:S(2)}, u32[]{:S(2)}) collective-permute-start(bf16[128,128]{1,0:T(8,128)(2,1)S(1)} %get-tuple-element.27), channel_id=1, source_target_pairs={{0,256},{1,257},{2,288},{3,289},{4,320},{5,321},{6,352},{7,353},{8... | collective-permute-start | bytes 98312 | tf_op jit(solution)/shard_map/ppermute | solution.py:276
  239.0 0.6 broadcast_select_fusion
  239.6 0.0 collective-permute-done.7
  239.6 3.6 %collective-permute-done.8 = bf16[128,128]{1,0:T(8,128)(2,1)S(1)} collective-permute-done((bf16[128,128]{1,0:T(8,128)(2,1)S(1)}, bf16[128,128]{1,0:T(8,128)(2,1)S(1)}, u32[]{:S(2)}, u32[]{:S(2)}) %collective-permute-start.8) | collective-permute-done | bytes 32800 | tf_op jit(solution)/shard_map/ppermute | solution.py:276
  243.2 0.6 slice_bitcast_fusion.1
  243.8 0.0 all-to-all-done.4.in_ref
  243.8 1.2 shard_map.96
  (26 shorter events, 0.3 us)
Async XLA Ops:
  0.6 0.7 copy-start
  2.8 9.2 %collective-permute-start = (bf16[128,128]{1,0:T(8,128)(2,1)S(1)}, bf16[128,128]{1,0:T(8,128)(2,1)S(1)}, u32[]{:S(2)}, u32[]{:S(2)}) collective-permute-start(bf16[128,128]{1,0:T(8,128)(2,1)S(1)} %pad_maximum_fusion.4), channel_id=1, source_target_pairs={{0,0},{1,1},{32,2},{33,3},{64,4},{65,5},{96,6},{97,7},{128,8},{129... | collective-permute-start | bytes 98312 | tf_op jit(solution)/shard_map/ppermute | solution.py:290
  13.5 55.1 %copy-start.1 = (bf16[128,256]{1,0:T(8,128)(2,1)S(1)}, bf16[128,256]{1,0:T(8,128)(2,1)}, u32[]{:S(2)}) copy-start(bf16[128,256]{1,0:T(8,128)(2,1)} %x_ref.5) | copy-start | bytes 196612
  13.5 55.1 %copy-start.2 = (bf16[128,256]{1,0:T(8,128)(2,1)S(1)}, bf16[128,256]{1,0:T(8,128)(2,1)}, u32[]{:S(2)}) copy-start(bf16[128,256]{1,0:T(8,128)(2,1)} %g_ref.3) | copy-start | bytes 196612
  13.5 55.1 %all-to-all-start = ((bf16[32,192,128]{2,1,0:T(8,128)(2,1)}), bf16[32,192,128]{2,1,0:T(8,128)(2,1)S(1)}, u32[]{:S(2)}, u32[]{:S(2)}) async-start(bf16[32,192,128]{2,1,0:T(8,128)(2,1)} %pad_maximum_fusion), calls=%async_computation | async-start | bytes 3145728 | tf_op jit(solution)/shard_map/all_to_all | solution.py:264
  70.5 7.9 %collective-permute-start.1 = (bf16[80,3712]{1,0:T(8,128)(2,1)S(1)}, bf16[80,3712]{1,0:T(8,128)(2,1)S(1)}, u32[]{:S(2)}, u32[]{:S(2)}) collective-permute-start(bf16[80,3712]{1,0:T(8,128)(2,1)S(1)} %get-tuple-element.11), channel_id=1, source_target_pairs={{0,32},{32,0},{64,96},{96,64},{128,160},{160,128},{192,224},{224,1... | collective-permute-start | bytes 1781768 | tf_op jit(solution)/shard_map/ppermute | solution.py:323
  140.7 8.2 %collective-permute-start.2 = (bf16[32,16,1152]{2,1,0:T(8,128)(2,1)S(1)}, bf16[32,16,1152]{2,1,0:T(8,128)(2,1)S(1)}, u32[]{:S(2)}, u32[]{:S(2)}) collective-permute-start(bf16[32,16,1152]{2,1,0:T(8,128)(2,1)S(1)} %all_to_all.26.mine_ref), channel_id=1, source_target_pairs={{0,32},{32,0},{64,96},{96,64},{128,160},{160,128},{192,224},{224,1... | collective-permute-start | bytes 3538952 | tf_op jit(solution)/shard_map/ppermute | solution.py:331
  160.4 23.1 %all-to-all-start.3 = ((bf16[16,8,2432]{2,1,0:T(8,128)(2,1)}), bf16[16,8,2432]{2,1,0:T(8,128)(2,1)S(1)}, u32[]{:S(2)}, u32[]{:S(2)}) async-start(bf16[16,8,2432]{2,1,0:T(8,128)(2,1)} %broadcast_in_dim.131), calls=%async_computation.3 | async-start | bytes 1245184 | tf_op jit(solution)/shard_map/all_to_all | solution.py:264
  185.5 15.1 %collective-permute-start.3 = (bf16[16,128,128]{2,1,0:T(8,128)(2,1)}, bf16[16,128,128]{2,1,0:T(8,128)(2,1)}, u32[]{:S(2)}, u32[]{:S(2)}) collective-permute-start(bf16[16,128,128]{2,1,0:T(8,128)(2,1)} %get-tuple-element.15), channel_id=1, source_target_pairs={{0,1},{1,0},{2,3},{3,2},{4,5},{5,4},{6,7},{7,6},{8,9},{9,8},{10,11... | collective-permute-start | bytes 1572872 | tf_op jit(solution)/shard_map/ppermute | solution.py:269
  191.0 52.9 %all-to-all-start.4 = ((bf16[16,160,256]{2,1,0:T(8,128)(2,1)}), bf16[16,160,256]{2,1,0:T(8,128)(2,1)S(1)}, u32[]{:S(2)}, u32[]{:S(2)}) async-start(bf16[16,160,256]{2,1,0:T(8,128)(2,1)} %shard_map.95), calls=%async_computation.4 | async-start | bytes 2621440 | tf_op jit(solution)/shard_map/all_to_all | solution.py:264
  201.8 11.7 %collective-permute-start.4 = (bf16[8,128,128]{2,1,0:T(8,128)(2,1)S(1)}, bf16[8,128,128]{2,1,0:T(8,128)(2,1)S(1)}, u32[]{:S(2)}, u32[]{:S(2)}) collective-permute-start(bf16[8,128,128]{2,1,0:T(8,128)(2,1)S(1)} %dynamic-slice_bitcast_fusion), channel_id=1, source_target_pairs={{0,2},{1,3},{2,0},{3,1},{4,6},{5,7},{6,4},{7,5},{8,10},{9,11},{10,... | collective-permute-start | bytes 786440 | tf_op jit(solution)/shard_map/ppermute | solution.py:269
  213.6 6.6 %collective-permute-start.5 = (bf16[4,128,128]{2,1,0:T(8,128)(2,1)S(1)}, bf16[4,128,128]{2,1,0:T(8,128)(2,1)S(1)}, u32[]{:S(2)}, u32[]{:S(2)}) collective-permute-start(bf16[4,128,128]{2,1,0:T(8,128)(2,1)S(1)} %dynamic-slice_bitcast_fusion.1), channel_id=1, source_target_pairs={{0,4},{1,5},{2,6},{3,7},{4,0},{5,1},{6,2},{7,3},{8,12},{9,13},{10,... | collective-permute-start | bytes 393224 | tf_op jit(solution)/shard_map/ppermute | solution.py:269
  220.2 6.6 %collective-permute-start.6 = (bf16[2,128,128]{2,1,0:T(8,128)(2,1)S(1)}, bf16[2,128,128]{2,1,0:T(8,128)(2,1)S(1)}, u32[]{:S(2)}, u32[]{:S(2)}) collective-permute-start(bf16[2,128,128]{2,1,0:T(8,128)(2,1)S(1)} %dynamic-slice_bitcast_fusion.2), channel_id=1, source_target_pairs={{0,8},{1,9},{2,10},{3,11},{4,12},{5,13},{6,14},{7,15},{8,0},{9,1},... | collective-permute-start | bytes 196616 | tf_op jit(solution)/shard_map/ppermute | solution.py:269
  226.9 12.7 %collective-permute-start.7 = (bf16[128,128]{1,0:T(8,128)(2,1)S(1)}, bf16[128,128]{1,0:T(8,128)(2,1)S(1)}, u32[]{:S(2)}, u32[]{:S(2)}) collective-permute-start(bf16[128,128]{1,0:T(8,128)(2,1)S(1)} %get-tuple-element.26), channel_id=1, source_target_pairs={{0,0},{1,1},{2,32},{3,33},{4,64},{5,65},{6,96},{7,97},{8,128},{9,1... | collective-permute-start | bytes 98312 | tf_op jit(solution)/shard_map/ppermute | solution.py:275
  231.6 11.5 %collective-permute-start.8 = (bf16[128,128]{1,0:T(8,128)(2,1)S(1)}, bf16[128,128]{1,0:T(8,128)(2,1)S(1)}, u32[]{:S(2)}, u32[]{:S(2)}) collective-permute-start(bf16[128,128]{1,0:T(8,128)(2,1)S(1)} %get-tuple-element.27), channel_id=1, source_target_pairs={{0,256},{1,257},{2,288},{3,289},{4,320},{5,321},{6,352},{7,353},{8... | collective-permute-start | bytes 98312 | tf_op jit(solution)/shard_map/ppermute | solution.py:276

commit v3 on v2

--- a/solution.py
+++ b/solution.py
@@ -41,44 +41,18 @@
 SMEM = pl.BlockSpec(memory_space=pltpu.SMEM)
 
 
-def project_kernel(ints, x_ref, g_ref, w_ref, keep_ref, send_ref, wc_ref, pair_ref, uc_ref, res_ref, gr_ref, ex_ref):
+def gram_kernel(ints, w_ref, gkeep_ref, gsend_ref, wc_ref, uc_ref, pair_ref, gr_ref):
     p, quarter, core, source = ints[0], ints[1], ints[2], ints[3]
     taking = ints[4] > 0
     for s in range(SECT):
         for h in range(2):
-            block = w_ref[2 * s + h, 0:128, :]
+            block = w_ref[2 * (s ^ 8) + h, 0:128, :]
             lanes = slice(128 * h, 128 * h + 128)
             wc_ref[128 * s : 128 * s + 128, lanes] = block
             uc_ref[64 * s : 64 * s + 64, lanes] = block[64:128]
     for h in range(2):
         part = w_ref[source, 128 + 32 * h : 160 + 32 * h, :]
         pair_ref[:, 128 * h : 128 * h + 128] = jnp.where(taking, part, jnp.zeros_like(part))
-
-    x = x_ref[...]
-    pair = pair_ref[...]
-    res_ref[:, 0:2048] = dot(x, wc_ref[...], NT)
-    res_ref[:, 2048:3072] = dot(g_ref[...], uc_ref[...], NT)
-    extra = dot(pair, wc_ref[...], NT)
-    for i in range(2):
-        for k in range(4):
-            for b in range(4):
-                at = 512 * k + 128 * b
-                ex_ref[pl.ds(128 * b + 4 * i + k, 16, stride=8), :] = extra[16 * i : 16 * i + 16, at : at + 128]
-    for b in range(4):
-        res_ref[:, 3072 + 128 * b : 3200 + 128 * b] = ex_ref[128 * b : 128 * b + 128, :]
-
-    xf = x.astype(F32)
-    pf = pair.astype(F32)
-    own_hi, own_lo = hi_lo(jnp.sum(xf * xf, axis=1, keepdims=True))
-    pair_hi, pair_lo = hi_lo(jnp.sum(pf * pf, axis=1, keepdims=True))
-    ex_ref[0:ROWS, :] = jnp.zeros((ROWS, 128), F32)
-    lane = lax.broadcasted_iota(jnp.int32, (PAIR, 128), 1) - 4 * core
-    pair_part = jnp.where(lane == 2, pair_hi, 0.0) + jnp.where(lane == 3, pair_lo, 0.0)
-    for i in range(2):
-        ex_ref[pl.ds(i, 16, stride=8), :] = pair_part[16 * i : 16 * i + 16]
-    lane = lax.broadcasted_iota(jnp.int32, (ROWS, 128), 1) - 4 * core
-    own_part = jnp.where(lane == 0, own_hi, 0.0) + jnp.where(lane == 1, own_lo, 0.0)
-    res_ref[:, 3584:3712] = ex_ref[0:ROWS, :] + own_part
 
     m = p // 2 + 1
     small_rows = wc_ref[pl.ds(pl.multiple_of(128 * p + 32 * quarter, 32), 32), :]
@@ -95,14 +69,39 @@
                 tiles[t] = jnp.where(m == mm, st[j], tiles[t])
     for t in range(9):
         gr_ref[:, 128 * t : 128 * t + 128] = tiles[t]
-
-    for ref, parity in ((keep_ref, core), (send_ref, 1 - core)):
-        for y in range(0, 8, 2):
-            first = res_ref[pl.ds(pl.multiple_of(16 * y + 8 * parity, 8), 8), :]
-            second = res_ref[pl.ds(pl.multiple_of(16 * y + 16 + 8 * parity, 8), 8), :]
-            ref[8 * y : 8 * y + 16, :] = jnp.concatenate([first, second], axis=0).astype(BF)
-        ref[64:80, 0:GW] = gr_ref[pl.ds(pl.multiple_of(16 * parity, 16), 16), :].astype(BF)
-        ref[64:80, GW:PIECE] = jnp.zeros((16, PIECE - GW), BF)
+    for gref, part in ((gkeep_ref, core), (gsend_ref, 1 - core)):
+        gref[...] = gr_ref[pl.ds(pl.multiple_of(16 * part, 16), 16), :].astype(BF)
+
+
+def project_kernel(ints, x_ref, pair_ref, g_ref, wc_ref, uc_ref, keep_ref, send_ref, res_ref, ex_ref):
+    core, sec = ints[2], ints[5]
+    x = x_ref[...]
+    pair = pair_ref[...]
+    res_ref[:, 0:2048] = dot(x, wc_ref[...], NT)
+    res_ref[:, 2048:3072] = dot(g_ref[...], uc_ref[...], NT)
+    extra = dot(pair, wc_ref[...], NT)
+    for i in range(2):
+        for k in range(4):
+            for b in range(4):
+                at = 512 * k + 128 * b
+                ex_ref[pl.ds(128 * b + 4 * i + k, 16, stride=8), :] = extra[16 * i : 16 * i + 16, at : at + 128]
+    for b in range(4):
+        res_ref[:, 3072 + 128 * b : 3200 + 128 * b] = ex_ref[128 * b : 128 * b + 128, :]
+
+    xf = x.astype(F32)
+    pf = pair.astype(F32)
+    own_hi, own_lo = hi_lo(jnp.sum(xf * xf, axis=1, keepdims=True))
+    pair_hi, pair_lo = hi_lo(jnp.sum(pf * pf, axis=1, keepdims=True))
+    ex_ref[0:ROWS, :] = jnp.zeros((ROWS, 128), F32)
+    lane = lax.broadcasted_iota(jnp.int32, (PAIR, 128), 1) - 4 * sec
+    pair_part = jnp.where(lane == 2, pair_hi, 0.0) + jnp.where(lane == 3, pair_lo, 0.0)
+    for i in range(2):
+        ex_ref[pl.ds(i, 16, stride=8), :] = pair_part[16 * i : 16 * i + 16]
+    lane = lax.broadcasted_iota(jnp.int32, (ROWS, 128), 1) - 4 * sec
+    own_part = jnp.where(lane == 0, own_hi, 0.0) + jnp.where(lane == 1, own_lo, 0.0)
+    res_ref[:, 3584:3712] = ex_ref[0:ROWS, :] + own_part
+    for ref, part in ((keep_ref, core), (send_ref, 1 - core)):
+        ref[...] = res_ref[pl.ds(pl.multiple_of(64 * part, 64), 64), :].astype(BF)
 
 
 def slab_place(s):
@@ -128,8 +127,10 @@
     h_ref[...] = jnp.zeros_like(h_ref)
     acc_ref[...] = jnp.zeros_like(acc_ref)
     misc = sum_ref[:, 3584:3712]
-    misc = misc + pltpu.roll(misc, 124, 1)
-    n = jnp.concatenate([misc[:, 0:1] + misc[:, 1:2], misc[:, 2:3] + misc[:, 3:4]], axis=0)
+    pair_lane = lax.broadcasted_iota(jnp.int32, (8, 128), 1) % 4 >= 2
+    n_own = jnp.sum(jnp.where(pair_lane, 0.0, misc), axis=1, keepdims=True)
+    n_pair = jnp.sum(jnp.where(pair_lane, misc, 0.0), axis=1, keepdims=True)
+    n = jnp.concatenate([n_own, n_pair], axis=0)
     row = lax.broadcasted_iota(jnp.int32, (16, 1), 0)
     n = jnp.where(row < 10, n, 0.0)
 
@@ -148,7 +149,7 @@
         inv = lax.rsqrt(jnp.maximum(n, 0.0) * (1.0 / D) + EPS)
         inverse.append(inv)
         pre = inv * tp
-        sig = 1.0 / (1.0 + jnp.exp(-pre))
+        sig = 0.5 + 0.5 * jnp.tanh(0.5 * pre)
         hf = pre * sig
         h = hf.astype(BF)
         pre_ref[:, 64 * s : 64 * s + 64] = pre
@@ -201,7 +202,8 @@
     out_ref[...] = ho_ref[...].astype(BF)
 
 
-def rebuild_kernel(ints, x_ref, pair_ref, back_ref, eh_ref, wc_ref, out_ref):
+def rebuild_kernel(ints, x_ref, pair_ref, mine_ref, other_ref, eh_ref, wc_ref, out_ref, back_ref):
+    gather_rows(ints[3], mine_ref, other_ref, back_ref)
     own_at = pl.multiple_of(ints[0], 32)
     pair_at = pl.multiple_of(ints[1], 32)
     alive = ints[2] > 0
@@ -216,8 +218,21 @@
             e = e + dot(eh_ref[:, 64 * s : 64 * s + 64], up, NN)
 
 
-def grads_kernel(ints, x_ref, g_ref, back_ref, wc_ref, keep_ref, send_ref, xs_ref, ht_ref, zt_ref):
-    upper = ints[0] > 0
+def gather_rows(core, mine_ref, other_ref, full_ref):
+    full_ref[pl.ds(pl.multiple_of(64 * core, 64), 64), :] = mine_ref[...]
+    full_ref[pl.ds(pl.multiple_of(64 * (1 - core), 64), 64), :] = other_ref[...]
+
+
+def pick(values, index):
+    out = values[0]
+    for k in range(1, len(values)):
+        out = jnp.where(index == k, values[k], out)
+    return out
+
+
+def grads_kernel(ints, x_ref, g_ref, mine_ref, other_ref, wc_ref, o0, o1, o2, o3, back_ref, xs_ref, ht_ref, zt_ref):
+    gather_rows(ints[0], mine_ref, other_ref, back_ref)
+    along = ints[1]
     ht_ref[...] = back_ref[:, 0:1024].T
     zt_ref[...] = back_ref[:, 1024:2048].T
     x = x_ref[...].astype(F32)
@@ -227,13 +242,17 @@
             x = x + dot(back_ref[:, 64 * s : 64 * s + 64], wc_ref[128 * s + 64 : 128 * s + 128, :], NN)
     g = g_ref[...].astype(F32)
     betas = back_ref[:, 2304:2432].astype(F32)
+    blocks = [None] * 4
     for s in range(SECT - 1, -1, -1):
         xs = xs_ref[s]
-        up = dot(ht_ref[64 * s : 64 * s + 64, :], g.astype(BF), NN).astype(BF)
-        down = dot(zt_ref[64 * s : 64 * s + 64, :], xs, NN).astype(BF)
-        for rows, value in ((slice(0, 64), up), (slice(64, 128), down)):
-            keep_ref[s, rows, :] = jnp.where(upper, value[:, 128:256], value[:, 0:128])
-            send_ref[s, rows, :] = jnp.where(upper, value[:, 0:128], value[:, 128:256])
+        up = dot(ht_ref[64 * s : 64 * s + 64, :], g.astype(BF), NN)
+        down = dot(zt_ref[64 * s : 64 * s + 64, :], xs, NN)
+        both = jnp.concatenate([up, down], axis=0).astype(BF)
+        for h in range(2):
+            blocks[2 * (s % 2) + h] = both[:, 128 * h : 128 * h + 128]
+        if s % 2 == 0:
+            for k, ref in enumerate((o0, o1, o2, o3)):
+                ref[s // 2 ^ 4] = pick(blocks, along ^ k)
         if s:
             z = back_ref[:, 1024 + 64 * s : 1024 + 64 * s + 64]
             g = g + dot(z, wc_ref[128 * s : 128 * s + 64, :], NN) - betas[:, s : s + 1] * xs.astype(F32)
@@ -264,21 +283,31 @@
     return lax.all_to_all(value, axis, 0, 0, tiled=True, axis_index_groups=groups)
 
 
-def scatter_sum(keep, send, me):
-    for b in range(4):
-        value = keep.astype(F32) + lax.ppermute(send, "dp", [(i, i ^ (1 << b)) for i in range(DP)]).astype(F32)
-        value = value.astype(BF).reshape((value.shape[0] // 2, 2) + value.shape[1:])
-        bit = (me >> (b + 1)) & 1
-        keep = lax.dynamic_index_in_dim(value, bit, 1, keepdims=False)
-        send = lax.dynamic_index_in_dim(value, 1 - bit, 1, keepdims=False)
+def flip(value, bits):
+    return lax.ppermute(value, "dp", [(i, i ^ bits) for i in range(DP)])
+
+
+def scatter_sum(own, arrived, me):
+    value = own.astype(F32)
+    for part in arrived:
+        value = value + part.astype(F32)
+    for b in (2, 4, 3):
+        blocks = value.astype(BF).reshape((-1, 2, 128, 128))
+        if b == 4:
+            blocks = blocks.reshape(2, 2, 128, 128).swapaxes(0, 1)
+        bit = (me >> b) & 1
+        keep = lax.dynamic_index_in_dim(blocks, bit, 1, keepdims=False)
+        send = lax.dynamic_index_in_dim(blocks, 1 - bit, 1, keepdims=False)
+        if b != 3:
+            value = keep.astype(F32) + flip(send, 1 << b).astype(F32)
     both = ("section", "dp")
     mine = lax.ppermute(keep[0], both, [(a, owner(a // DP, a % DP)) for a in range(SECT * DP)])
-    theirs = lax.ppermute(send[0], both, [(a, owner(a // DP, a % DP ^ 16)) for a in range(SECT * DP)])
+    theirs = lax.ppermute(send[0], both, [(a, owner(a // DP, a % DP ^ 8)) for a in range(SECT * DP)])
     return mine.astype(F32) + theirs.astype(F32)
 
 
 def owner(sec, q):
-    return (q // 2) * DP + 2 * sec + q % 2
+    return (q // 2 ^ 8) * DP + 2 * sec + q % 2
 
 
 def body(x, g, worker, gain, narrow, widen):
@@ -306,28 +335,41 @@
     weights = exchange(weights, "dp")
 
     core = sec % 2
-    keep, send, wc, pair = call(
+    ints = jnp.stack([me // 4, me % 4, core, source, taking.astype(jnp.int32), sec]).astype(jnp.int32)
+    gkeep, gsend, wc, uc, pair = call(
+        gram_kernel,
+        1,
+        (shape(16, GW), shape(16, GW), shape(2048, F), shape(1024, F), shape(PAIR, F)),
+        [pltpu.VMEM((32, GW), F32)],
+        10**8,
+        3 * 10**6,
+    )(ints, weights)
+    swap = [(i, i ^ 1) for i in range(SECT)]
+    share = (gkeep.astype(F32) + lax.ppermute(gsend, "section", swap).astype(F32)).astype(BF)
+    keep, send = call(
         project_kernel,
-        3,
-        (shape(80, PIECE), shape(80, PIECE), shape(2048, F), shape(PAIR, F)),
-        [
-            pltpu.VMEM((1024, F), BF),
-            pltpu.VMEM((ROWS, PIECE), F32),
-            pltpu.VMEM((32, GW), F32),
-            pltpu.VMEM((4 * ROWS, 128), F32),
-        ],
-        4 * 10**8,
+        5,
+        (shape(64, PIECE), shape(64, PIECE)),
+        [pltpu.VMEM((ROWS, PIECE), F32), pltpu.VMEM((4 * ROWS, 128), F32)],
+        3 * 10**8,
         3 * 10**6,
-    )(jnp.stack([me // 4, me % 4, core, source, taking.astype(jnp.int32)]).astype(jnp.int32), x, g, weights)
-    swap = [(i, i ^ 1) for i in range(SECT)]
-    pieces = (keep.astype(F32) + lax.ppermute(send, "section", swap).astype(F32)).astype(BF)
-    share = jnp.concatenate([pieces[64:72, 0:GW], pieces[72:80, 0:GW]], axis=1)
-    pieces = jnp.concatenate(
-        [pieces[0:64].reshape(8, 8, PIECE), jnp.broadcast_to(share[None], (8, 8, 2 * GW))], axis=2
-    )
-    total = jnp.sum(exchange(pieces, "section", Y_GROUPS).astype(F32), axis=0)
-    share = jnp.concatenate([total[:, PIECE : PIECE + GW], total[:, PIECE + GW :]], axis=0).astype(BF)
+    )(ints, x, pair, g, wc, uc)
+    share = exchange(jnp.broadcast_to(share[None], (8, 16, GW)), "section", Y_GROUPS)
+    share = jnp.sum(share.astype(F32), axis=0).astype(BF)
     half = exchange(jnp.broadcast_to(share[None], (DP, 16, GW)), "dp")
+
+    rows = (keep.astype(F32) + lax.ppermute(send, "section", swap).astype(F32)).astype(BF).reshape(8, 8, PIECE)
+    bit = (sec >> 1) & 1
+    both = rows.reshape(4, 2, 8, PIECE)
+    send = lax.dynamic_index_in_dim(both, 1 - bit, 1, keepdims=False)
+    send = lax.ppermute(send, "section", [(i, i ^ 2) for i in range(SECT)])
+    rows = (lax.dynamic_index_in_dim(both, bit, 1, keepdims=False).astype(F32) + send.astype(F32)).astype(BF)
+    here = sec // 4
+    total = lax.dynamic_index_in_dim(rows, here, 0, keepdims=False).astype(F32)
+    for k in range(1, 4):
+        send = lax.dynamic_index_in_dim(rows, here ^ k, 0, keepdims=False)
+        total = total + lax.ppermute(send, "section", [(i, i ^ (4 * k)) for i in range(SECT)]).astype(F32)
+    half, total = lax.optimization_barrier((half, total))
     other = lax.ppermute(half, "section", swap)
 
     back = call(
@@ -347,33 +389,44 @@
         2 * 10**8,
         3 * 10**6,
     )(core.reshape(1).astype(jnp.int32), total, half, other)
-    back = exchange(jnp.broadcast_to(back[None], (SECT, 8, BACK)), "section")
-
-    keep, send = call(
+    back = exchange(jnp.broadcast_to(back[None], (8, 8, BACK)), "section", Y_GROUPS).reshape(64, BACK)
+    back_other = lax.ppermute(back, "section", swap)
+
+    blocks = call(
         grads_kernel,
-        4,
-        (shape(SECT, 128, 128), shape(SECT, 128, 128)),
-        [pltpu.VMEM((SECT, ROWS, F), BF), pltpu.VMEM((1024, ROWS), BF), pltpu.VMEM((1024, ROWS), BF)],
+        5,
+        (shape(8, 128, 128),) * 4,
+        [
+            pltpu.VMEM((ROWS, BACK), BF),
+            pltpu.VMEM((SECT, ROWS, F), BF),
+            pltpu.VMEM((1024, ROWS), BF),
+            pltpu.VMEM((1024, ROWS), BF),
+        ],
         3 * 10**8,
         3 * 10**6,
-    )((me % 2).reshape(1).astype(jnp.int32), x, g, back.reshape(ROWS, BACK), wc)
-    grads = scatter_sum(keep, send, me)
-
-    extra_h = back[:, :, 2048:2304].reshape(SECT, 2, 4, 256).transpose(1, 0, 2, 3).reshape(PAIR, 1024)
+    )(jnp.stack([core, me % 4]).astype(jnp.int32), x, g, back, back_other, wc)
+    arrived = [flip(blocks[k], k) for k in (1, 3, 2)]
+
+    small, small_other = back[:, 2048:2432], back_other[:, 2048:2432]
+    small = jnp.where(
+        core == 0, jnp.concatenate([small, small_other], axis=0), jnp.concatenate([small_other, small], axis=0)
+    ).reshape(SECT, 8, 384)
+    extra_h = small[:, :, 0:256].reshape(SECT, 2, 4, 256).transpose(1, 0, 2, 3).reshape(PAIR, 1024)
     own_at = jnp.where(pair_first, PAIR, 0)
     pair_at = jnp.where(pair_first, 0, ROWS)
     rows_out = call(
         rebuild_kernel,
-        5,
+        6,
         shape(SECT, ROWS + PAIR, F),
-        [],
+        [pltpu.VMEM((ROWS, BACK), BF)],
         2 * 10**8,
         3 * 10**6,
-    )(jnp.stack([own_at, pair_at, alive.astype(jnp.int32)]).astype(jnp.int32), x, pair, back.reshape(ROWS, BACK), extra_h, wc)
+    )(jnp.stack([own_at, pair_at, alive.astype(jnp.int32), core]).astype(jnp.int32), x, pair, back, back_other, extra_h, wc)
     saved = exchange(rows_out, "section")
+    grads = scatter_sum(blocks[0], arrived, me)
     saved = call(join_kernel, 1, shape(1, 1, ROWS + PAIR, D), [], 0, 3 * 10**6, False)(saved)
 
-    misc = back[:, :, 2304:2432].astype(F32)
+    misc = small[:, :, 256:384].astype(F32)
     own_inv = misc[:, :, 16:32] + misc[:, :, 32:48]
     pair_inv = misc[:, 0:2, 48:64] + misc[:, 0:2, 64:80]
     own_inv = lax.dynamic_index_in_dim(own_inv, sec, 2, keepdims=False).reshape(ROWS)

time: 246 us -> 239 us (0.972)
  blocking collectives: 61.7 us -> 15.4 us
  starting transfers between devices: 66.6 us -> 100 us
  waiting for transfers between devices: 81.5 us -> 84 us
    all_to_all x2 -> x1, blocking collectives: 61.7 us -> 15.4 us  [exchange(): lax.all_to_all(value, axis, 0, 0, tiled=True, axis_index_groups=groups)]
    ppermute x5 -> x12, starting transfers between devices: 17 us -> 40.9 us  [the longest x5 15.7 us: flip(): return lax.ppermute(value, 'dp', [(i, i ^ bits) for i in range(DP)])]
    ppermute x1, starting transfers between devices: 4.72 us -> 13.7 us  [scatter_sum(): lax.ppermute(keep[0], both, [(a, owner(a // DP, a % DP)) for a in range(S...]
    ppermute x1, starting transfers between devices: 6.03 us -> 14.5 us  [body(): lax.ppermute(block, ('section', 'dp'), [(owner(a // DP, a % DP), a) for a...]
    ppermute x1, starting transfers between devices: 6.32 us -> 1.92 us  [body(): lax.ppermute(send, 'section', swap).astype(F32)]
    all_to_all x3 -> x4, starting transfers between devices: 26.8 us -> 23.1 us  [exchange(): lax.all_to_all(value, axis, 0, 0, tiled=True, axis_index_groups=groups)]
    all_to_all x3 -> x4, waiting for transfers between devices: 52.3 us -> 54.9 us  [exchange(): lax.all_to_all(value, axis, 0, 0, tiled=True, axis_index_groups=groups)]
    ppermute x5 -> x12, waiting for transfers between devices: 25.2 us -> 26.6 us  [the longest x5 16.9 us: flip(): return lax.ppermute(value, 'dp', [(i, i ^ bits) for i in range(DP)])]
  transfers between devices with their start and end apart: 12 -> 20, of which waited for: 9 -> 10; matrix products, arithmetic and copies ran while one was open for 4% -> 4% of each run, Pallas kernels for 1% -> 2%
where the time goes in v3:
time: 239 us; the launch traced here: 236 us
  starting transfers between devices  100 us (42%)
  waiting for transfers between devices  84 us (35%)
  Pallas kernels  18.1 us (8%)
  blocking collectives  15.4 us (6%)
  local copies, waits for them, and re-layouts  7.69 us (3%)
  other arithmetic  6.92 us (3%)
  between operations  3.83 us (2%)
    all_to_all x4, waiting for transfers between devices, exchange(): lax.all_to_all(value, axis, 0, 0, tiled=True, axis_index_groups=groups)  54.9 us
    all_to_all x4, starting transfers between devices, exchange(): lax.all_to_all(value, axis, 0, 0, tiled=True, axis_index_groups=groups)  23.1 us
    ppermute x5, waiting for transfers between devices, flip(): return lax.ppermute(value, 'dp', [(i, i ^ bits) for i in range(DP)])  16.9 us
    ppermute x5, starting transfers between devices, flip(): return lax.ppermute(value, 'dp', [(i, i ^ bits) for i in range(DP)])  15.7 us
    all_to_all x1, blocking collectives, exchange(): lax.all_to_all(value, axis, 0, 0, tiled=True, axis_index_groups=groups)  15.4 us
    ppermute x1, starting transfers between devices, body(): lax.ppermute(block, ('section', 'dp'), [(owner(a // DP, a % DP), a) for a...  14.5 us
    ppermute x1, starting transfers between devices, scatter_sum(): lax.ppermute(keep[0], both, [(a, owner(a // DP, a % DP)) for a in range(S...  13.7 us
    ppermute x3, starting transfers between devices, body(): lax.ppermute(send, 'section', [(i, i ^ 4 * k) for i in range(SECT)])  11.4 us
  transfers between devices with their start and end apart: 20, of which 10 were waited for; matrix products, arithmetic and copies ran while one was open for 4% of the time, Pallas kernels for 2%

profile of v3, /device:TPU:1, one launch (start us, length us, event | category | flops | bytes accessed | tf_op | source)
XLA Modules:
  0.0 236.3 jit_solution(15123365899790575789)
XLA Ops:
  0.7 0.7 copy-done
  1.4 0.7 fusion.7
  2.1 0.7 pad_maximum_fusion.1
  2.8 14.5 %collective-permute-start = (bf16[128,128]{1,0:T(8,128)(2,1)S(1)}, bf16[128,128]{1,0:T(8,128)(2,1)S(1)}, u32[]{:S(2)}, u32[]{:S(2)}) collective-permute-start(bf16[128,128]{1,0:T(8,128)(2,1)S(1)} %pad_maximum_fusion.1), channel_id=1, source_target_pairs={{256,0},{257,1},{288,2},{289,3},{320,4},{321,5},{352,6},{353,7},{3... | collective-permute-start | bytes 98312 | tf_op jit(solution)/shard_map/ppermute | solution.py:319
  17.3 0.7 slice.67
  18.0 0.2 fusion.20
  18.2 0.5 slice.68
  19.3 0.1 fusion.17
  19.4 0.8 fusion.23
  20.2 0.2 select_select_fusion
  20.4 0.2 broadcast_in_dim.111
  20.7 1.3 pad_maximum_fusion
  22.0 7.2 %all-to-all-start = ((bf16[32,192,128]{2,1,0:T(8,128)(2,1)}), bf16[32,192,128]{2,1,0:T(8,128)(2,1)S(1)}, u32[]{:S(2)}, u32[]{:S(2)}) async-start(bf16[32,192,128]{2,1,0:T(8,128)(2,1)} %pad_maximum_fusion), calls=%async_computation | async-start | bytes 3145728 | tf_op jit(solution)/shard_map/all_to_all | solution.py:283
  29.3 0.6 fusion.19
  30.6 0.6 select_reduce_fusion
  31.2 0.7 stack.49.ints
  32.0 33.5 %all-to-all-done.w_ref = bf16[32,192,128]{2,1,0:T(8,128)(2,1)S(1)} async-done(((bf16[32,192,128]{2,1,0:T(8,128)(2,1)}), bf16[32,192,128]{2,1,0:T(8,128)(2,1)S(1)}, u32[]{:S(2)}, u32[]{:S(2)}) %all-to-all-start) | async-done | bytes 1572896 | tf_op jit(solution)/shard_map/all_to_all | solution.py:283
  65.5 1.1 shard_map.93
  66.5 5.7 %collective-permute-start.1 = (bf16[16,1152]{1,0:T(8,128)(2,1)S(1)}, bf16[16,1152]{1,0:T(8,128)(2,1)S(1)}, u32[]{:S(2)}, u32[]{:S(2)}) collective-permute-start(bf16[16,1152]{1,0:T(8,128)(2,1)S(1)} %get-tuple-element.18), channel_id=1, source_target_pairs={{0,32},{32,0},{64,96},{96,64},{128,160},{160,128},{192,224},{224,1... | collective-permute-start | bytes 110600 | tf_op jit(solution)/shard_map/ppermute | solution.py:348
  72.3 1.6 shard_map.94
  73.9 1.9 collective-permute-start.2
  75.9 0.7 broadcast_in_dim.129
  76.6 6.7 %all-to-all-start.1 = ((bf16[8,16,1152]{2,1,0:T(8,128)(2,1)}), bf16[8,16,1152]{2,1,0:T(8,128)(2,1)S(1)}, u32[]{:S(2)}, u32[]{:S(2)}) async-start(bf16[8,16,1152]{2,1,0:T(8,128)(2,1)} %broadcast_in_dim.129), calls=%async_computation.1 | async-start | bytes 589824 | tf_op jit(solution)/shard_map/all_to_all | solution.py:283
  83.3 0.1 add_convert_fusion
  83.5 3.4 %collective-permute-start.3 = (bf16[4,8,3712]{2,1,0:T(8,128)(2,1)S(1)}, bf16[4,8,3712]{2,1,0:T(8,128)(2,1)S(1)}, u32[]{:S(2)}, u32[]{:S(2)}) collective-permute-start(bf16[4,8,3712]{2,1,0:T(8,128)(2,1)S(1)} %dynamic-slice_bitcast_fusion), channel_id=1, source_target_pairs={{0,64},{32,96},{64,0},{96,32},{128,192},{160,224},{192,128},{224,1... | collective-permute-start | bytes 712712 | tf_op jit(solution)/shard_map/ppermute | solution.py:365
  86.9 8.2 %all-to-all-done.1 = bf16[8,16,1152]{2,1,0:T(8,128)(2,1)S(1)} async-done(((bf16[8,16,1152]{2,1,0:T(8,128)(2,1)}), bf16[8,16,1152]{2,1,0:T(8,128)(2,1)S(1)}, u32[]{:S(2)}, u32[]{:S(2)}) %all-to-all-start.1) | async-done | bytes 294944 | tf_op jit(solution)/shard_map/all_to_all | solution.py:283
  95.1 1.1 broadcast_in_dim.130
  96.2 5.5 %all-to-all-start.2 = ((bf16[32,16,1152]{2,1,0:T(8,128)(2,1)}), bf16[32,16,1152]{2,1,0:T(8,128)(2,1)S(1)}, u32[]{:S(2)}, u32[]{:S(2)}) async-start(bf16[32,16,1152]{2,1,0:T(8,128)(2,1)} %broadcast_in_dim.130), calls=%async_computation.2 | async-start | bytes 2359296 | tf_op jit(solution)/shard_map/all_to_all | solution.py:283
  101.8 1.9 collective-permute-start.4
  103.7 4.6 %collective-permute-start.5 = (bf16[8,3712]{1,0:T(8,128)(2,1)S(1)}, bf16[8,3712]{1,0:T(8,128)(2,1)S(1)}, u32[]{:S(2)}, u32[]{:S(2)}) collective-permute-start(bf16[8,3712]{1,0:T(8,128)(2,1)S(1)} %get-tuple-element.40), channel_id=1, source_target_pairs={{0,256},{32,288},{64,320},{96,352},{128,384},{160,416},{192,448},{... | collective-permute-start | bytes 178184 | tf_op jit(solution)/shard_map/ppermute | solution.py:371
  108.3 4.9 %collective-permute-start.6 = (bf16[8,3712]{1,0:T(8,128)(2,1)S(1)}, bf16[8,3712]{1,0:T(8,128)(2,1)S(1)}, u32[]{:S(2)}, u32[]{:S(2)}) collective-permute-start(bf16[8,3712]{1,0:T(8,128)(2,1)S(1)} %get-tuple-element.39), channel_id=1, source_target_pairs={{0,384},{32,416},{64,448},{96,480},{128,256},{160,288},{192,320},{... | collective-permute-start | bytes 178184 | tf_op jit(solution)/shard_map/ppermute | solution.py:371
  113.3 2.4 %collective-permute-done.6 = bf16[8,3712]{1,0:T(8,128)(2,1)S(1)} collective-permute-done((bf16[8,3712]{1,0:T(8,128)(2,1)S(1)}, bf16[8,3712]{1,0:T(8,128)(2,1)S(1)}, u32[]{:S(2)}, u32[]{:S(2)}) %collective-permute-start.6) | collective-permute-done | bytes 59424 | tf_op jit(solution)/shard_map/ppermute | solution.py:371
  115.7 13.2 %all-to-all-done.2.mine_ref = bf16[32,16,1152]{2,1,0:T(8,128)(2,1)S(1)} async-done(((bf16[32,16,1152]{2,1,0:T(8,128)(2,1)}), bf16[32,16,1152]{2,1,0:T(8,128)(2,1)S(1)}, u32[]{:S(2)}, u32[]{:S(2)}) %all-to-all-start.2) | async-done | bytes 1179680 | tf_op jit(solution)/shard_map/all_to_all | solution.py:283
  129.0 6.4 %collective-permute-start.7 = (bf16[32,16,1152]{2,1,0:T(8,128)(2,1)S(1)}, bf16[32,16,1152]{2,1,0:T(8,128)(2,1)S(1)}, u32[]{:S(2)}, u32[]{:S(2)}) collective-permute-start(bf16[32,16,1152]{2,1,0:T(8,128)(2,1)S(1)} %all-to-all-done.2.mine_ref), channel_id=1, source_target_pairs={{0,32},{32,0},{64,96},{96,64},{128,160},{160,128},{192,224},{224,1... | collective-permute-start | bytes 3538952 | tf_op jit(solution)/shard_map/ppermute | solution.py:373
  135.4 2.5 %collective-permute-done.7.other_ref = bf16[32,16,1152]{2,1,0:T(8,128)(2,1)S(1)} collective-permute-done((bf16[32,16,1152]{2,1,0:T(8,128)(2,1)S(1)}, bf16[32,16,1152]{2,1,0:T(8,128)(2,1)S(1)}, u32[]{:S(2)}, u32[]{:S(2)}) %collective-permute-start.7) | collective-permute-done | bytes 1179680 | tf_op jit(solution)/shard_map/ppermute | solution.py:373
  137.8 10.4 %shard_map.95 = bf16[8,2432]{1,0:T(8,128)(2,1)S(1)} custom-call(s32[1]{0:T(128)} %bitcast.ints, f32[8,3712]{1,0:T(8,128)S(1)} %fusion.4.sum_ref, bf16[32,16,1152]{2,1,0:T(8,128)(2,1)S(1)} %all-to-all-done.2.mine_ref, bf16[32,16,1152]{2,1,0:T(8,128)(2,1)S(1)} %collective-permute-done.7.other_ref), custom_call_target="tpu_custom_call" | custom-call | flops 200000000 | bytes 3000000 | tf_op jit(solution)/shard_map/pallas_call | solution.py:375
  148.2 15.4 %all_to_all.25 = bf16[8,8,2432]{2,1,0:T(8,128)(2,1)S(1)} all-to-all(bf16[8,8,2432]{2,1,0:T(8,128)(2,1)S(1)} %broadcast_in_dim.131), channel_id=1, replica_groups={{0,64,128,192,256,320,384,448},{32,96,160,224,288,352,416,480},{1,65,12..., dimensions={0} | all-to-all | bytes 622592 | tf_op jit(solution)/shard_map/all_to_all | solution.py:283
  163.6 2.8 %collective-permute-start.8 = (bf16[64,2432]{1,0:T(8,128)(2,1)S(1)}, bf16[64,2432]{1,0:T(8,128)(2,1)S(1)}, u32[]{:S(2)}, u32[]{:S(2)}) collective-permute-start(bf16[64,2432]{1,0:T(8,128)(2,1)S(1)} %bitcast.83), channel_id=1, source_target_pairs={{0,32},{32,0},{64,96},{96,64},{128,160},{160,128},{192,224},{224,1... | collective-permute-start | bytes 933896 | tf_op jit(solution)/shard_map/ppermute | solution.py:393
  167.7 0.1 pad_add_fusion.ints
  167.9 1.1 shard_map.96
  169.0 1.0 copy-done.1
  170.1 3.7 %all-to-all-start.4 = ((bf16[16,160,256]{2,1,0:T(8,128)(2,1)}), bf16[16,160,256]{2,1,0:T(8,128)(2,1)S(1)}, u32[]{:S(2)}, u32[]{:S(2)}) async-start(bf16[16,160,256]{2,1,0:T(8,128)(2,1)} %copy-done.1), calls=%async_computation.4 | async-start | bytes 2621440 | tf_op jit(solution)/shard_map/all_to_all | solution.py:283
  173.8 2.8 %shard_map.98 = (bf16[8,128,128]{2,1,0:T(8,128)(2,1)S(1)}, bf16[8,128,128]{2,1,0:T(8,128)(2,1)}, bf16[8,128,128]{2,1,0:T(8,128)(2,1)}, bf16[8,128,128]{2,1,0:T(8,128)(2,1)}) custom-call(s32[2]{0:T(128)S(1)} %pad_add_fusion.1.ints, bf16[128,256]{1,0:T(8,128)(2,1)S(1)} %copy-done.2, bf16[128,256]{1,0:T(8,128)(2,1)S(1)} %copy-done.3, ...), custom_call_target="tpu_custom_call" | custom-call | flops 300000000 | bytes 3000000 | tf_op jit(solution)/shard_map/pallas_call | solution.py:395
  176.6 4.7 %collective-permute-start.10 = (bf16[8,128,128]{2,1,0:T(8,128)(2,1)}, bf16[8,128,128]{2,1,0:T(8,128)(2,1)S(1)}, u32[]{:S(2)}, u32[]{:S(2)}) collective-permute-start(bf16[8,128,128]{2,1,0:T(8,128)(2,1)} %get-tuple-element.28), channel_id=1, source_target_pairs={{0,3},{1,2},{2,1},{3,0},{4,7},{5,6},{6,5},{7,4},{8,11},{9,10},{10,... | collective-permute-start | bytes 786440 | tf_op jit(solution)/shard_map/ppermute | solution.py:287
  181.3 2.2 collective-permute-start.11
  183.5 2.2 collective-permute-start.9
  185.7 0.4 copy.22
  186.2 0.7 fusion.16
  186.9 0.1 copy.19
  186.9 0.1 concatenate.44
  187.0 5.7 %collective-permute-done.10 = bf16[8,128,128]{2,1,0:T(8,128)(2,1)S(1)} collective-permute-done((bf16[8,128,128]{2,1,0:T(8,128)(2,1)}, bf16[8,128,128]{2,1,0:T(8,128)(2,1)S(1)}, u32[]{:S(2)}, u32[]{:S(2)}) %collective-permute-start.10) | collective-permute-done | bytes 262176 | tf_op jit(solution)/shard_map/ppermute | solution.py:287
  192.7 3.0 %collective-permute-done.9 = bf16[8,128,128]{2,1,0:T(8,128)(2,1)S(1)} collective-permute-done((bf16[8,128,128]{2,1,0:T(8,128)(2,1)}, bf16[8,128,128]{2,1,0:T(8,128)(2,1)S(1)}, u32[]{:S(2)}, u32[]{:S(2)}) %collective-permute-start.9) | collective-permute-done | bytes 262176 | tf_op jit(solution)/shard_map/ppermute | solution.py:287
  195.7 0.1 add_convert_fusion.1
  195.9 2.4 collective-permute-start.12
  198.3 3.6 %collective-permute-done.12 = bf16[4,128,128]{2,1,0:T(8,128)(2,1)S(1)} collective-permute-done((bf16[4,128,128]{2,1,0:T(8,128)(2,1)S(1)}, bf16[4,128,128]{2,1,0:T(8,128)(2,1)S(1)}, u32[]{:S(2)}, u32[]{:S(2)}) %collective-permute-start.12) | collective-permute-done | bytes 131104 | tf_op jit(solution)/shard_map/ppermute | solution.py:287
  202.0 4.2 %collective-permute-start.13 = (bf16[2,128,128]{2,1,0:T(8,128)(2,1)S(1)}, bf16[2,128,128]{2,1,0:T(8,128)(2,1)S(1)}, u32[]{:S(2)}, u32[]{:S(2)}) collective-permute-start(bf16[2,128,128]{2,1,0:T(8,128)(2,1)S(1)} %dynamic-slice_bitcast_fusion.2), channel_id=1, source_target_pairs={{0,16},{1,17},{2,18},{3,19},{4,20},{5,21},{6,22},{7,23},{8,24},{9,... | collective-permute-start | bytes 196616 | tf_op jit(solution)/shard_map/ppermute | solution.py:287
  206.2 0.1 concatenate.45
  206.3 4.7 %collective-permute-done.13 = bf16[2,128,128]{2,1,0:T(8,128)(2,1)S(1)} collective-permute-done((bf16[2,128,128]{2,1,0:T(8,128)(2,1)S(1)}, bf16[2,128,128]{2,1,0:T(8,128)(2,1)S(1)}, u32[]{:S(2)}, u32[]{:S(2)}) %collective-permute-start.13) | collective-permute-done | bytes 65568 | tf_op jit(solution)/shard_map/ppermute | solution.py:287
  211.0 13.7 %collective-permute-start.14 = (bf16[128,128]{1,0:T(8,128)(2,1)S(1)}, bf16[128,128]{1,0:T(8,128)(2,1)S(1)}, u32[]{:S(2)}, u32[]{:S(2)}) collective-permute-start(bf16[128,128]{1,0:T(8,128)(2,1)S(1)} %get-tuple-element.43), channel_id=1, source_target_pairs={{0,256},{1,257},{2,288},{3,289},{4,320},{5,321},{6,352},{7,353},{8... | collective-permute-start | bytes 98312 | tf_op jit(solution)/shard_map/ppermute | solution.py:304
  224.7 1.9 collective-permute-start.15
  226.6 0.6 broadcast_select_fusion
  227.2 7.2 %collective-permute-done.15 = bf16[128,128]{1,0:T(8,128)(2,1)S(1)} collective-permute-done((bf16[128,128]{1,0:T(8,128)(2,1)S(1)}, bf16[128,128]{1,0:T(8,128)(2,1)S(1)}, u32[]{:S(2)}, u32[]{:S(2)}) %collective-permute-start.15) | collective-permute-done | bytes 32800 | tf_op jit(solution)/shard_map/ppermute | solution.py:305
  234.5 0.6 slice_bitcast_fusion
  235.1 1.2 shard_map.97
  (48 shorter events, 0.7 us)
Async XLA Ops:
  0.6 0.7 copy-start
  2.8 17.6 %collective-permute-start = (bf16[128,128]{1,0:T(8,128)(2,1)S(1)}, bf16[128,128]{1,0:T(8,128)(2,1)S(1)}, u32[]{:S(2)}, u32[]{:S(2)}) collective-permute-start(bf16[128,128]{1,0:T(8,128)(2,1)S(1)} %pad_maximum_fusion.1), channel_id=1, source_target_pairs={{256,0},{257,1},{288,2},{289,3},{320,4},{321,5},{352,6},{353,7},{3... | collective-permute-start | bytes 98312 | tf_op jit(solution)/shard_map/ppermute | solution.py:319
  22.0 43.5 %all-to-all-start = ((bf16[32,192,128]{2,1,0:T(8,128)(2,1)}), bf16[32,192,128]{2,1,0:T(8,128)(2,1)S(1)}, u32[]{:S(2)}, u32[]{:S(2)}) async-start(bf16[32,192,128]{2,1,0:T(8,128)(2,1)} %pad_maximum_fusion), calls=%async_computation | async-start | bytes 3145728 | tf_op jit(solution)/shard_map/all_to_all | solution.py:283
  29.2 43.0 %copy-start.2 = (bf16[128,256]{1,0:T(8,128)(2,1)S(1)}, bf16[128,256]{1,0:T(8,128)(2,1)}, u32[]{:S(2)}) copy-start(bf16[128,256]{1,0:T(8,128)(2,1)} %x_ref.5) | copy-start | bytes 196612
  29.2 43.0 %copy-start.3 = (bf16[128,256]{1,0:T(8,128)(2,1)S(1)}, bf16[128,256]{1,0:T(8,128)(2,1)}, u32[]{:S(2)}) copy-start(bf16[128,256]{1,0:T(8,128)(2,1)} %g_ref.3) | copy-start | bytes 196612
  66.5 9.3 %collective-permute-start.1 = (bf16[16,1152]{1,0:T(8,128)(2,1)S(1)}, bf16[16,1152]{1,0:T(8,128)(2,1)S(1)}, u32[]{:S(2)}, u32[]{:S(2)}) collective-permute-start(bf16[16,1152]{1,0:T(8,128)(2,1)S(1)} %get-tuple-element.18), channel_id=1, source_target_pairs={{0,32},{32,0},{64,96},{96,64},{128,160},{160,128},{192,224},{224,1... | collective-permute-start | bytes 110600 | tf_op jit(solution)/shard_map/ppermute | solution.py:348
  73.9 9.4 %collective-permute-start.2 = (bf16[64,3712]{1,0:T(8,128)(2,1)S(1)}, bf16[64,3712]{1,0:T(8,128)(2,1)S(1)}, u32[]{:S(2)}, u32[]{:S(2)}) collective-permute-start(bf16[64,3712]{1,0:T(8,128)(2,1)S(1)} %get-tuple-element.23), channel_id=1, source_target_pairs={{0,32},{32,0},{64,96},{96,64},{128,160},{160,128},{192,224},{224,1... | collective-permute-start | bytes 1425416 | tf_op jit(solution)/shard_map/ppermute | solution.py:361
  76.6 18.4 %all-to-all-start.1 = ((bf16[8,16,1152]{2,1,0:T(8,128)(2,1)}), bf16[8,16,1152]{2,1,0:T(8,128)(2,1)S(1)}, u32[]{:S(2)}, u32[]{:S(2)}) async-start(bf16[8,16,1152]{2,1,0:T(8,128)(2,1)} %broadcast_in_dim.129), calls=%async_computation.1 | async-start | bytes 589824 | tf_op jit(solution)/shard_map/all_to_all | solution.py:283
  83.5 18.3 %collective-permute-start.3 = (bf16[4,8,3712]{2,1,0:T(8,128)(2,1)S(1)}, bf16[4,8,3712]{2,1,0:T(8,128)(2,1)S(1)}, u32[]{:S(2)}, u32[]{:S(2)}) collective-permute-start(bf16[4,8,3712]{2,1,0:T(8,128)(2,1)S(1)} %dynamic-slice_bitcast_fusion), channel_id=1, source_target_pairs={{0,64},{32,96},{64,0},{96,32},{128,192},{160,224},{192,128},{224,1... | collective-permute-start | bytes 712712 | tf_op jit(solution)/shard_map/ppermute | solution.py:365
  96.2 32.8 %all-to-all-start.2 = ((bf16[32,16,1152]{2,1,0:T(8,128)(2,1)}), bf16[32,16,1152]{2,1,0:T(8,128)(2,1)S(1)}, u32[]{:S(2)}, u32[]{:S(2)}) async-start(bf16[32,16,1152]{2,1,0:T(8,128)(2,1)} %broadcast_in_dim.130), calls=%async_computation.2 | async-start | bytes 2359296 | tf_op jit(solution)/shard_map/all_to_all | solution.py:283
  101.8 11.4 %collective-permute-start.4 = (bf16[8,3712]{1,0:T(8,128)(2,1)S(1)}, bf16[8,3712]{1,0:T(8,128)(2,1)S(1)}, u32[]{:S(2)}, u32[]{:S(2)}) collective-permute-start(bf16[8,3712]{1,0:T(8,128)(2,1)S(1)} %get-tuple-element.38), channel_id=1, source_target_pairs={{0,128},{32,160},{64,192},{96,224},{128,0},{160,32},{192,64},{224,... | collective-permute-start | bytes 178184 | tf_op jit(solution)/shard_map/ppermute | solution.py:371
  103.7 9.5 %collective-permute-start.5 = (bf16[8,3712]{1,0:T(8,128)(2,1)S(1)}, bf16[8,3712]{1,0:T(8,128)(2,1)S(1)}, u32[]{:S(2)}, u32[]{:S(2)}) collective-permute-start(bf16[8,3712]{1,0:T(8,128)(2,1)S(1)} %get-tuple-element.40), channel_id=1, source_target_pairs={{0,256},{32,288},{64,320},{96,352},{128,384},{160,416},{192,448},{... | collective-permute-start | bytes 178184 | tf_op jit(solution)/shard_map/ppermute | solution.py:371
  108.3 7.3 %collective-permute-start.6 = (bf16[8,3712]{1,0:T(8,128)(2,1)S(1)}, bf16[8,3712]{1,0:T(8,128)(2,1)S(1)}, u32[]{:S(2)}, u32[]{:S(2)}) collective-permute-start(bf16[8,3712]{1,0:T(8,128)(2,1)S(1)} %get-tuple-element.39), channel_id=1, source_target_pairs={{0,384},{32,416},{64,448},{96,480},{128,256},{160,288},{192,320},{... | collective-permute-start | bytes 178184 | tf_op jit(solution)/shard_map/ppermute | solution.py:371
  129.0 8.8 %collective-permute-start.7 = (bf16[32,16,1152]{2,1,0:T(8,128)(2,1)S(1)}, bf16[32,16,1152]{2,1,0:T(8,128)(2,1)S(1)}, u32[]{:S(2)}, u32[]{:S(2)}) collective-permute-start(bf16[32,16,1152]{2,1,0:T(8,128)(2,1)S(1)} %all-to-all-done.2.mine_ref), channel_id=1, source_target_pairs={{0,32},{32,0},{64,96},{96,64},{128,160},{160,128},{192,224},{224,1... | collective-permute-start | bytes 3538952 | tf_op jit(solution)/shard_map/ppermute | solution.py:373
  163.6 4.2 %collective-permute-start.8 = (bf16[64,2432]{1,0:T(8,128)(2,1)S(1)}, bf16[64,2432]{1,0:T(8,128)(2,1)S(1)}, u32[]{:S(2)}, u32[]{:S(2)}) collective-permute-start(bf16[64,2432]{1,0:T(8,128)(2,1)S(1)} %bitcast.83), channel_id=1, source_target_pairs={{0,32},{32,0},{64,96},{96,64},{128,160},{160,128},{192,224},{224,1... | collective-permute-start | bytes 933896 | tf_op jit(solution)/shard_map/ppermute | solution.py:393
  167.8 6.0 %copy-start.4 = (bf16[16,8,384]{2,1,0:T(8,128)(2,1)}, bf16[16,8,384]{2,1,0:T(8,128)(2,1)S(1)}, u32[]{:S(2)}) copy-start(bf16[16,8,384]{2,1,0:T(8,128)(2,1)S(1)} %fusion.5) | copy-start | bytes 294916
  169.0 1.1 copy-start.1
  170.1 65.0 %all-to-all-start.4 = ((bf16[16,160,256]{2,1,0:T(8,128)(2,1)}), bf16[16,160,256]{2,1,0:T(8,128)(2,1)S(1)}, u32[]{:S(2)}, u32[]{:S(2)}) async-start(bf16[16,160,256]{2,1,0:T(8,128)(2,1)} %copy-done.1), calls=%async_computation.4 | async-start | bytes 2621440 | tf_op jit(solution)/shard_map/all_to_all | solution.py:283
  173.8 11.9 %slice-start = ((bf16[16,8,384]{2,1,0:T(8,128)(2,1)}), bf16[16,8,128]{2,1,0:T(8,128)(2,1)S(1)}, s32[]{:S(2)}) async-start(bf16[16,8,384]{2,1,0:T(8,128)(2,1)} %copy-done.4), calls=%async_computation.5 | async-start | bytes 65536 | tf_op jit(solution)/shard_map/slice | solution.py:429
  176.6 16.1 %collective-permute-start.10 = (bf16[8,128,128]{2,1,0:T(8,128)(2,1)}, bf16[8,128,128]{2,1,0:T(8,128)(2,1)S(1)}, u32[]{:S(2)}, u32[]{:S(2)}) collective-permute-start(bf16[8,128,128]{2,1,0:T(8,128)(2,1)} %get-tuple-element.28), channel_id=1, source_target_pairs={{0,3},{1,2},{2,1},{3,0},{4,7},{5,6},{6,5},{7,4},{8,11},{9,10},{10,... | collective-permute-start | bytes 786440 | tf_op jit(solution)/shard_map/ppermute | solution.py:287
  181.3 11.4 %collective-permute-start.11 = (bf16[8,128,128]{2,1,0:T(8,128)(2,1)}, bf16[8,128,128]{2,1,0:T(8,128)(2,1)S(1)}, u32[]{:S(2)}, u32[]{:S(2)}) collective-permute-start(bf16[8,128,128]{2,1,0:T(8,128)(2,1)} %get-tuple-element.29), channel_id=1, source_target_pairs={{0,2},{1,3},{2,0},{3,1},{4,6},{5,7},{6,4},{7,5},{8,10},{9,11},{10,... | collective-permute-start | bytes 786440 | tf_op jit(solution)/shard_map/ppermute | solution.py:287
  183.5 12.2 %collective-permute-start.9 = (bf16[8,128,128]{2,1,0:T(8,128)(2,1)}, bf16[8,128,128]{2,1,0:T(8,128)(2,1)S(1)}, u32[]{:S(2)}, u32[]{:S(2)}) collective-permute-start(bf16[8,128,128]{2,1,0:T(8,128)(2,1)} %get-tuple-element.27), channel_id=1, source_target_pairs={{0,1},{1,0},{2,3},{3,2},{4,5},{5,4},{6,7},{7,6},{8,9},{9,8},{10,11... | collective-permute-start | bytes 786440 | tf_op jit(solution)/shard_map/ppermute | solution.py:287
  195.9 6.0 %collective-permute-start.12 = (bf16[4,128,128]{2,1,0:T(8,128)(2,1)S(1)}, bf16[4,128,128]{2,1,0:T(8,128)(2,1)S(1)}, u32[]{:S(2)}, u32[]{:S(2)}) collective-permute-start(bf16[4,128,128]{2,1,0:T(8,128)(2,1)S(1)} %dynamic-slice_bitcast_fusion.1), channel_id=1, source_target_pairs={{0,4},{1,5},{2,6},{3,7},{4,0},{5,1},{6,2},{7,3},{8,12},{9,13},{10,... | collective-permute-start | bytes 393224 | tf_op jit(solution)/shard_map/ppermute | solution.py:287
  202.0 9.0 %collective-permute-start.13 = (bf16[2,128,128]{2,1,0:T(8,128)(2,1)S(1)}, bf16[2,128,128]{2,1,0:T(8,128)(2,1)S(1)}, u32[]{:S(2)}, u32[]{:S(2)}) collective-permute-start(bf16[2,128,128]{2,1,0:T(8,128)(2,1)S(1)} %dynamic-slice_bitcast_fusion.2), channel_id=1, source_target_pairs={{0,16},{1,17},{2,18},{3,19},{4,20},{5,21},{6,22},{7,23},{8,24},{9,... | collective-permute-start | bytes 196616 | tf_op jit(solution)/shard_map/ppermute | solution.py:287
  211.0 16.3 %collective-permute-start.14 = (bf16[128,128]{1,0:T(8,128)(2,1)S(1)}, bf16[128,128]{1,0:T(8,128)(2,1)S(1)}, u32[]{:S(2)}, u32[]{:S(2)}) collective-permute-start(bf16[128,128]{1,0:T(8,128)(2,1)S(1)} %get-tuple-element.43), channel_id=1, source_target_pairs={{0,256},{1,257},{2,288},{3,289},{4,320},{5,321},{6,352},{7,353},{8... | collective-permute-start | bytes 98312 | tf_op jit(solution)/shard_map/ppermute | solution.py:304
  224.7 9.8 %collective-permute-start.15 = (bf16[128,128]{1,0:T(8,128)(2,1)S(1)}, bf16[128,128]{1,0:T(8,128)(2,1)S(1)}, u32[]{:S(2)}, u32[]{:S(2)}) collective-permute-start(bf16[128,128]{1,0:T(8,128)(2,1)S(1)} %get-tuple-element.44), channel_id=1, source_target_pairs={{0,384},{1,385},{2,416},{3,417},{4,448},{5,449},{6,480},{7,481},{8... | collective-permute-start | bytes 98312 | tf_op jit(solution)/shard_map/ppermute | solution.py:305

commit v4 on v3

--- a/solution.py
+++ b/solution.py
@@ -230,7 +230,7 @@
     return out
 
 
-def grads_kernel(ints, x_ref, g_ref, mine_ref, other_ref, wc_ref, o0, o1, o2, o3, back_ref, xs_ref, ht_ref, zt_ref):
+def grads_kernel(ints, x_ref, g_ref, mine_ref, other_ref, wc_ref, keep_ref, send_ref, back_ref, xs_ref, ht_ref, zt_ref):
     gather_rows(ints[0], mine_ref, other_ref, back_ref)
     along = ints[1]
     ht_ref[...] = back_ref[:, 0:1024].T
@@ -251,8 +251,9 @@
         for h in range(2):
             blocks[2 * (s % 2) + h] = both[:, 128 * h : 128 * h + 128]
         if s % 2 == 0:
-            for k, ref in enumerate((o0, o1, o2, o3)):
-                ref[s // 2 ^ 4] = pick(blocks, along ^ k)
+            for ref, flips in ((keep_ref, (0, 3)), (send_ref, (1, 2))):
+                for k in range(2):
+                    ref[k, s // 2 ^ 4] = pick(blocks, along ^ flips[k])
         if s:
             z = back_ref[:, 1024 + 64 * s : 1024 + 64 * s + 64]
             g = g + dot(z, wc_ref[128 * s : 128 * s + 64, :], NN) - betas[:, s : s + 1] * xs.astype(F32)
@@ -287,10 +288,9 @@
     return lax.ppermute(value, "dp", [(i, i ^ bits) for i in range(DP)])
 
 
-def scatter_sum(own, arrived, me):
-    value = own.astype(F32)
-    for part in arrived:
-        value = value + part.astype(F32)
+def scatter_sum(keep, send, me):
+    value = keep.astype(F32) + flip(send, 1).astype(F32)
+    value = value[0] + flip(value[1].astype(BF), 3).astype(F32)
     for b in (2, 4, 3):
         blocks = value.astype(BF).reshape((-1, 2, 128, 128))
         if b == 4:
@@ -395,7 +395,7 @@
     blocks = call(
         grads_kernel,
         5,
-        (shape(8, 128, 128),) * 4,
+        (shape(2, 8, 128, 128),) * 2,
         [
             pltpu.VMEM((ROWS, BACK), BF),
             pltpu.VMEM((SECT, ROWS, F), BF),
@@ -405,7 +405,6 @@
         3 * 10**8,
         3 * 10**6,
     )(jnp.stack([core, me % 4]).astype(jnp.int32), x, g, back, back_other, wc)
-    arrived = [flip(blocks[k], k) for k in (1, 3, 2)]
 
     small, small_other = back[:, 2048:2432], back_other[:, 2048:2432]
     small = jnp.where(
@@ -423,7 +422,7 @@
         3 * 10**6,
     )(jnp.stack([own_at, pair_at, alive.astype(jnp.int32), core]).astype(jnp.int32), x, pair, back, back_other, extra_h, wc)
     saved = exchange(rows_out, "section")
-    grads = scatter_sum(blocks[0], arrived, me)
+    grads = scatter_sum(*blocks, me)
     saved = call(join_kernel, 1, shape(1, 1, ROWS + PAIR, D), [], 0, 3 * 10**6, False)(saved)
 
     misc = small[:, :, 256:384].astype(F32)

time: 239 us -> 235 us (0.983)
  starting transfers between devices: 100 us -> 96 us
    ppermute x1, starting transfers between devices: 13.7 us -> 9.47 us  [scatter_sum(): lax.ppermute(keep[0], both, [(a, owner(a // DP, a % DP)) for a in range(S...]
    ppermute x5 -> x4, waiting for transfers between devices: 16.9 us -> 15.2 us  [flip(): return lax.ppermute(value, 'dp', [(i, i ^ bits) for i in range(DP)])]
    ppermute x5 -> x4, starting transfers between devices: 15.7 us -> 14.6 us  [flip(): return lax.ppermute(value, 'dp', [(i, i ^ bits) for i in range(DP)])]
  transfers between devices with their start and end apart: 20 -> 19, of which waited for: 10 -> 11; matrix products, arithmetic and copies ran while one was open for 4% -> 5% of each run, Pallas kernels for 2% -> 2%
where the time goes in v4:
time: 235 us; the launch traced here: 232 us
  starting transfers between devices  96 us (41%)
  waiting for transfers between devices  81.8 us (35%)
  Pallas kernels  18.3 us (8%)
  blocking collectives  15.4 us (7%)
  other arithmetic  9 us (4%)
  local copies, waits for them, and re-layouts  7.45 us (3%)
  between operations  3.84 us (2%)
    all_to_all x4, waiting for transfers between devices, exchange(): lax.all_to_all(value, axis, 0, 0, tiled=True, axis_index_groups=groups)  53.1 us
    all_to_all x4, starting transfers between devices, exchange(): lax.all_to_all(value, axis, 0, 0, tiled=True, axis_index_groups=groups)  23.5 us
    all_to_all x1, blocking collectives, exchange(): lax.all_to_all(value, axis, 0, 0, tiled=True, axis_index_groups=groups)  15.4 us
    ppermute x4, waiting for transfers between devices, flip(): return lax.ppermute(value, 'dp', [(i, i ^ bits) for i in range(DP)])  15.2 us
    ppermute x4, starting transfers between devices, flip(): return lax.ppermute(value, 'dp', [(i, i ^ bits) for i in range(DP)])  14.6 us
    ppermute x1, starting transfers between devices, body(): lax.ppermute(block, ('section', 'dp'), [(owner(a // DP, a % DP), a) for a...  14.5 us
    ppermute x3, starting transfers between devices, body(): lax.ppermute(send, 'section', [(i, i ^ 4 * k) for i in range(SECT)])  11.4 us
    pallas_call x1, Pallas kernels, body(): call(recur_kernel, 3, shape(8, BACK), [pltpu.VMEM((1024, GW), BF), pltpu....  10.4 us
  transfers between devices with their start and end apart: 19, of which 11 were waited for; matrix products, arithmetic and copies ran while one was open for 5% of the time, Pallas kernels for 2%

profile of v4, /device:TPU:1, one launch (start us, length us, event | category | flops | bytes accessed | tf_op | source)
XLA Modules:
  0.0 231.7 jit_solution(3027454702561947625)
XLA Ops:
  0.7 0.7 copy-done
  1.4 0.7 fusion.10
  2.1 0.7 pad_maximum_fusion.1
  2.8 14.5 %collective-permute-start = (bf16[128,128]{1,0:T(8,128)(2,1)S(1)}, bf16[128,128]{1,0:T(8,128)(2,1)S(1)}, u32[]{:S(2)}, u32[]{:S(2)}) collective-permute-start(bf16[128,128]{1,0:T(8,128)(2,1)S(1)} %pad_maximum_fusion.1), channel_id=1, source_target_pairs={{256,0},{257,1},{288,2},{289,3},{320,4},{321,5},{352,6},{353,7},{3... | collective-permute-start | bytes 98312 | tf_op jit(solution)/shard_map/ppermute | solution.py:319
  17.3 0.7 slice.74
  18.0 0.2 fusion.23
  18.2 0.5 slice.75
  19.3 0.1 fusion.20
  19.4 0.8 fusion.26
  20.2 0.2 select_select_fusion
  20.4 0.2 broadcast_in_dim.111
  20.7 1.3 pad_maximum_fusion
  22.0 7.2 %all-to-all-start = ((bf16[32,192,128]{2,1,0:T(8,128)(2,1)}), bf16[32,192,128]{2,1,0:T(8,128)(2,1)S(1)}, u32[]{:S(2)}, u32[]{:S(2)}) async-start(bf16[32,192,128]{2,1,0:T(8,128)(2,1)} %pad_maximum_fusion), calls=%async_computation | async-start | bytes 3145728 | tf_op jit(solution)/shard_map/all_to_all | solution.py:284
  29.3 0.6 fusion.22
  30.6 0.6 select_reduce_fusion
  31.2 0.7 stack.49.ints
  32.0 33.5 %all-to-all-done.w_ref = bf16[32,192,128]{2,1,0:T(8,128)(2,1)S(1)} async-done(((bf16[32,192,128]{2,1,0:T(8,128)(2,1)}), bf16[32,192,128]{2,1,0:T(8,128)(2,1)S(1)}, u32[]{:S(2)}, u32[]{:S(2)}) %all-to-all-start) | async-done | bytes 1572896 | tf_op jit(solution)/shard_map/all_to_all | solution.py:284
  65.5 1.1 shard_map.93
  66.5 5.7 %collective-permute-start.1 = (bf16[16,1152]{1,0:T(8,128)(2,1)S(1)}, bf16[16,1152]{1,0:T(8,128)(2,1)S(1)}, u32[]{:S(2)}, u32[]{:S(2)}) collective-permute-start(bf16[16,1152]{1,0:T(8,128)(2,1)S(1)} %get-tuple-element.16), channel_id=1, source_target_pairs={{0,32},{32,0},{64,96},{96,64},{128,160},{160,128},{192,224},{224,1... | collective-permute-start | bytes 110600 | tf_op jit(solution)/shard_map/ppermute | solution.py:348
  72.3 1.6 shard_map.94
  73.9 1.9 collective-permute-start.2
  75.9 0.7 broadcast_in_dim.129
  76.6 6.7 %all-to-all-start.1 = ((bf16[8,16,1152]{2,1,0:T(8,128)(2,1)}), bf16[8,16,1152]{2,1,0:T(8,128)(2,1)S(1)}, u32[]{:S(2)}, u32[]{:S(2)}) async-start(bf16[8,16,1152]{2,1,0:T(8,128)(2,1)} %broadcast_in_dim.129), calls=%async_computation.1 | async-start | bytes 589824 | tf_op jit(solution)/shard_map/all_to_all | solution.py:284
  83.3 1.1 add_convert_fusion
  84.5 3.4 %collective-permute-start.3 = (bf16[4,8,3712]{2,1,0:T(8,128)(2,1)S(1)}, bf16[4,8,3712]{2,1,0:T(8,128)(2,1)S(1)}, u32[]{:S(2)}, u32[]{:S(2)}) collective-permute-start(bf16[4,8,3712]{2,1,0:T(8,128)(2,1)S(1)} %dynamic-slice_bitcast_fusion), channel_id=1, source_target_pairs={{0,64},{32,96},{64,0},{96,32},{128,192},{160,224},{192,128},{224,1... | collective-permute-start | bytes 712712 | tf_op jit(solution)/shard_map/ppermute | solution.py:365
  87.9 7.0 %all-to-all-done.1 = bf16[8,16,1152]{2,1,0:T(8,128)(2,1)S(1)} async-done(((bf16[8,16,1152]{2,1,0:T(8,128)(2,1)}), bf16[8,16,1152]{2,1,0:T(8,128)(2,1)S(1)}, u32[]{:S(2)}, u32[]{:S(2)}) %all-to-all-start.1) | async-done | bytes 294944 | tf_op jit(solution)/shard_map/all_to_all | solution.py:284
  94.9 1.1 broadcast_in_dim.130
  96.0 5.5 %all-to-all-start.2 = ((bf16[32,16,1152]{2,1,0:T(8,128)(2,1)}), bf16[32,16,1152]{2,1,0:T(8,128)(2,1)S(1)}, u32[]{:S(2)}, u32[]{:S(2)}) async-start(bf16[32,16,1152]{2,1,0:T(8,128)(2,1)} %broadcast_in_dim.130), calls=%async_computation.2 | async-start | bytes 2359296 | tf_op jit(solution)/shard_map/all_to_all | solution.py:284
  101.6 1.9 collective-permute-start.4
  103.5 4.8 %collective-permute-start.5 = (bf16[8,3712]{1,0:T(8,128)(2,1)S(1)}, bf16[8,3712]{1,0:T(8,128)(2,1)S(1)}, u32[]{:S(2)}, u32[]{:S(2)}) collective-permute-start(bf16[8,3712]{1,0:T(8,128)(2,1)S(1)} %get-tuple-element.36), channel_id=1, source_target_pairs={{0,256},{32,288},{64,320},{96,352},{128,384},{160,416},{192,448},{... | collective-permute-start | bytes 178184 | tf_op jit(solution)/shard_map/ppermute | solution.py:371
  108.4 4.6 %collective-permute-start.6 = (bf16[8,3712]{1,0:T(8,128)(2,1)S(1)}, bf16[8,3712]{1,0:T(8,128)(2,1)S(1)}, u32[]{:S(2)}, u32[]{:S(2)}) collective-permute-start(bf16[8,3712]{1,0:T(8,128)(2,1)S(1)} %get-tuple-element.35), channel_id=1, source_target_pairs={{0,384},{32,416},{64,448},{96,480},{128,256},{160,288},{192,320},{... | collective-permute-start | bytes 178184 | tf_op jit(solution)/shard_map/ppermute | solution.py:371
  113.1 2.7 %collective-permute-done.6 = bf16[8,3712]{1,0:T(8,128)(2,1)S(1)} collective-permute-done((bf16[8,3712]{1,0:T(8,128)(2,1)S(1)}, bf16[8,3712]{1,0:T(8,128)(2,1)S(1)}, u32[]{:S(2)}, u32[]{:S(2)}) %collective-permute-start.6) | collective-permute-done | bytes 59424 | tf_op jit(solution)/shard_map/ppermute | solution.py:371
  115.8 12.6 %all-to-all-done.2.mine_ref = bf16[32,16,1152]{2,1,0:T(8,128)(2,1)S(1)} async-done(((bf16[32,16,1152]{2,1,0:T(8,128)(2,1)}), bf16[32,16,1152]{2,1,0:T(8,128)(2,1)S(1)}, u32[]{:S(2)}, u32[]{:S(2)}) %all-to-all-start.2) | async-done | bytes 1179680 | tf_op jit(solution)/shard_map/all_to_all | solution.py:284
  128.4 6.8 %collective-permute-start.7 = (bf16[32,16,1152]{2,1,0:T(8,128)(2,1)S(1)}, bf16[32,16,1152]{2,1,0:T(8,128)(2,1)S(1)}, u32[]{:S(2)}, u32[]{:S(2)}) collective-permute-start(bf16[32,16,1152]{2,1,0:T(8,128)(2,1)S(1)} %all-to-all-done.2.mine_ref), channel_id=1, source_target_pairs={{0,32},{32,0},{64,96},{96,64},{128,160},{160,128},{192,224},{224,1... | collective-permute-start | bytes 3538952 | tf_op jit(solution)/shard_map/ppermute | solution.py:373
  135.2 2.5 %collective-permute-done.7.other_ref = bf16[32,16,1152]{2,1,0:T(8,128)(2,1)S(1)} collective-permute-done((bf16[32,16,1152]{2,1,0:T(8,128)(2,1)S(1)}, bf16[32,16,1152]{2,1,0:T(8,128)(2,1)S(1)}, u32[]{:S(2)}, u32[]{:S(2)}) %collective-permute-start.7) | collective-permute-done | bytes 1179680 | tf_op jit(solution)/shard_map/ppermute | solution.py:373
  137.6 10.4 %shard_map.95 = bf16[8,2432]{1,0:T(8,128)(2,1)S(1)} custom-call(s32[1]{0:T(128)} %bitcast.ints, f32[8,3712]{1,0:T(8,128)S(1)} %fusion.7.sum_ref, bf16[32,16,1152]{2,1,0:T(8,128)(2,1)S(1)} %all-to-all-done.2.mine_ref, bf16[32,16,1152]{2,1,0:T(8,128)(2,1)S(1)} %collective-permute-done.7.other_ref), custom_call_target="tpu_custom_call" | custom-call | flops 200000000 | bytes 3000000 | tf_op jit(solution)/shard_map/pallas_call | solution.py:375
  148.0 15.4 %all_to_all.25 = bf16[8,8,2432]{2,1,0:T(8,128)(2,1)S(1)} all-to-all(bf16[8,8,2432]{2,1,0:T(8,128)(2,1)S(1)} %broadcast_in_dim.131), channel_id=1, replica_groups={{0,64,128,192,256,320,384,448},{32,96,160,224,288,352,416,480},{1,65,12..., dimensions={0} | all-to-all | bytes 622592 | tf_op jit(solution)/shard_map/all_to_all | solution.py:284
  163.4 2.8 %collective-permute-start.8 = (bf16[64,2432]{1,0:T(8,128)(2,1)S(1)}, bf16[64,2432]{1,0:T(8,128)(2,1)S(1)}, u32[]{:S(2)}, u32[]{:S(2)}) collective-permute-start(bf16[64,2432]{1,0:T(8,128)(2,1)S(1)} %bitcast.91), channel_id=1, source_target_pairs={{0,32},{32,0},{64,96},{96,64},{128,160},{160,128},{192,224},{224,1... | collective-permute-start | bytes 933896 | tf_op jit(solution)/shard_map/ppermute | solution.py:393
  166.2 0.1 pad_add_fusion.1.ints
  166.3 1.1 collective-permute-done.8.other_ref
  167.4 1.9 shard_map.98
  169.3 3.1 %collective-permute-start.9 = (bf16[2,8,128,128]{3,2,1,0:T(8,128)(2,1)S(1)}, bf16[2,8,128,128]{3,2,1,0:T(8,128)(2,1)}, u32[]{:S(2)}, u32[]{:S(2)}) collective-permute-start(bf16[2,8,128,128]{3,2,1,0:T(8,128)(2,1)S(1)} %get-tuple-element.25), channel_id=1, source_target_pairs={{0,1},{1,0},{2,3},{3,2},{4,5},{5,4},{6,7},{7,6},{8,9},{9,8},{10,11... | collective-permute-start | bytes 1572872 | tf_op jit(solution)/shard_map/ppermute | solution.py:288
  173.7 0.1 pad_add_fusion.ints
  174.0 2.1 shard_map.96
  176.1 4.1 %all-to-all-start.4 = ((bf16[16,160,256]{2,1,0:T(8,128)(2,1)}), bf16[16,160,256]{2,1,0:T(8,128)(2,1)S(1)}, u32[]{:S(2)}, u32[]{:S(2)}) async-start(bf16[16,160,256]{2,1,0:T(8,128)(2,1)} %shard_map.96), calls=%async_computation.4 | async-start | bytes 2621440 | tf_op jit(solution)/shard_map/all_to_all | solution.py:284
  180.3 1.2 copy.22
  181.5 3.0 %collective-permute-done.9 = bf16[2,8,128,128]{3,2,1,0:T(8,128)(2,1)} collective-permute-done((bf16[2,8,128,128]{3,2,1,0:T(8,128)(2,1)S(1)}, bf16[2,8,128,128]{3,2,1,0:T(8,128)(2,1)}, u32[]{:S(2)}, u32[]{:S(2)}) %collective-permute-start.9) | collective-permute-done | bytes 524320 | tf_op jit(solution)/shard_map/ppermute | solution.py:288
  184.5 1.2 convert_add_fusion
  185.7 4.4 %collective-permute-start.10 = (bf16[8,128,128]{2,1,0:T(8,128)(2,1)S(1)}, bf16[8,128,128]{2,1,0:T(8,128)(2,1)S(1)}, u32[]{:S(2)}, u32[]{:S(2)}) collective-permute-start(bf16[8,128,128]{2,1,0:T(8,128)(2,1)S(1)} %fusion.3), channel_id=1, source_target_pairs={{0,3},{1,2},{2,1},{3,0},{4,7},{5,6},{6,5},{7,4},{8,11},{9,10},{10,... | collective-permute-start | bytes 786440 | tf_op jit(solution)/shard_map/ppermute | solution.py:288
  190.2 0.7 fusion.19
  190.8 0.1 copy.19
  190.9 0.1 concatenate.44
  191.0 4.5 %collective-permute-done.10 = bf16[8,128,128]{2,1,0:T(8,128)(2,1)S(1)} collective-permute-done((bf16[8,128,128]{2,1,0:T(8,128)(2,1)S(1)}, bf16[8,128,128]{2,1,0:T(8,128)(2,1)S(1)}, u32[]{:S(2)}, u32[]{:S(2)}) %collective-permute-start.10) | collective-permute-done | bytes 262176 | tf_op jit(solution)/shard_map/ppermute | solution.py:288
  195.6 2.6 %collective-permute-start.11 = (bf16[4,128,128]{2,1,0:T(8,128)(2,1)S(1)}, bf16[4,128,128]{2,1,0:T(8,128)(2,1)S(1)}, u32[]{:S(2)}, u32[]{:S(2)}) collective-permute-start(bf16[4,128,128]{2,1,0:T(8,128)(2,1)S(1)} %dynamic-slice_bitcast_fusion.1), channel_id=1, source_target_pairs={{0,4},{1,5},{2,6},{3,7},{4,0},{5,1},{6,2},{7,3},{8,12},{9,13},{10,... | collective-permute-start | bytes 393224 | tf_op jit(solution)/shard_map/ppermute | solution.py:288
  198.3 3.3 %collective-permute-done.11 = bf16[4,128,128]{2,1,0:T(8,128)(2,1)S(1)} collective-permute-done((bf16[4,128,128]{2,1,0:T(8,128)(2,1)S(1)}, bf16[4,128,128]{2,1,0:T(8,128)(2,1)S(1)}, u32[]{:S(2)}, u32[]{:S(2)}) %collective-permute-start.11) | collective-permute-done | bytes 131104 | tf_op jit(solution)/shard_map/ppermute | solution.py:288
  201.7 4.4 %collective-permute-start.12 = (bf16[2,128,128]{2,1,0:T(8,128)(2,1)S(1)}, bf16[2,128,128]{2,1,0:T(8,128)(2,1)S(1)}, u32[]{:S(2)}, u32[]{:S(2)}) collective-permute-start(bf16[2,128,128]{2,1,0:T(8,128)(2,1)S(1)} %dynamic-slice_bitcast_fusion.2), channel_id=1, source_target_pairs={{0,16},{1,17},{2,18},{3,19},{4,20},{5,21},{6,22},{7,23},{8,24},{9,... | collective-permute-start | bytes 196616 | tf_op jit(solution)/shard_map/ppermute | solution.py:288
  206.2 0.1 concatenate.45
  206.2 4.4 %collective-permute-done.12 = bf16[2,128,128]{2,1,0:T(8,128)(2,1)S(1)} collective-permute-done((bf16[2,128,128]{2,1,0:T(8,128)(2,1)S(1)}, bf16[2,128,128]{2,1,0:T(8,128)(2,1)S(1)}, u32[]{:S(2)}, u32[]{:S(2)}) %collective-permute-start.12) | collective-permute-done | bytes 65568 | tf_op jit(solution)/shard_map/ppermute | solution.py:288
  210.7 9.5 %collective-permute-start.13 = (bf16[128,128]{1,0:T(8,128)(2,1)S(1)}, bf16[128,128]{1,0:T(8,128)(2,1)S(1)}, u32[]{:S(2)}, u32[]{:S(2)}) collective-permute-start(bf16[128,128]{1,0:T(8,128)(2,1)S(1)} %get-tuple-element.39), channel_id=1, source_target_pairs={{0,256},{1,257},{2,288},{3,289},{4,320},{5,321},{6,352},{7,353},{8... | collective-permute-start | bytes 98312 | tf_op jit(solution)/shard_map/ppermute | solution.py:304
  220.1 1.9 collective-permute-start.14
  222.1 0.6 broadcast_select_fusion
  222.7 7.2 %collective-permute-done.14 = bf16[128,128]{1,0:T(8,128)(2,1)S(1)} collective-permute-done((bf16[128,128]{1,0:T(8,128)(2,1)S(1)}, bf16[128,128]{1,0:T(8,128)(2,1)S(1)}, u32[]{:S(2)}, u32[]{:S(2)}) %collective-permute-start.14) | collective-permute-done | bytes 32800 | tf_op jit(solution)/shard_map/ppermute | solution.py:305
  229.9 0.6 slice_bitcast_fusion.1
  230.5 1.2 shard_map.97
  (47 shorter events, 0.7 us)
Async XLA Ops:
  0.6 0.7 copy-start
  2.8 17.6 %collective-permute-start = (bf16[128,128]{1,0:T(8,128)(2,1)S(1)}, bf16[128,128]{1,0:T(8,128)(2,1)S(1)}, u32[]{:S(2)}, u32[]{:S(2)}) collective-permute-start(bf16[128,128]{1,0:T(8,128)(2,1)S(1)} %pad_maximum_fusion.1), channel_id=1, source_target_pairs={{256,0},{257,1},{288,2},{289,3},{320,4},{321,5},{352,6},{353,7},{3... | collective-permute-start | bytes 98312 | tf_op jit(solution)/shard_map/ppermute | solution.py:319
  22.0 43.5 %all-to-all-start = ((bf16[32,192,128]{2,1,0:T(8,128)(2,1)}), bf16[32,192,128]{2,1,0:T(8,128)(2,1)S(1)}, u32[]{:S(2)}, u32[]{:S(2)}) async-start(bf16[32,192,128]{2,1,0:T(8,128)(2,1)} %pad_maximum_fusion), calls=%async_computation | async-start | bytes 3145728 | tf_op jit(solution)/shard_map/all_to_all | solution.py:284
  29.2 43.1 %copy-start.1 = (bf16[128,256]{1,0:T(8,128)(2,1)S(1)}, bf16[128,256]{1,0:T(8,128)(2,1)}, u32[]{:S(2)}) copy-start(bf16[128,256]{1,0:T(8,128)(2,1)} %x_ref.5) | copy-start | bytes 196612
  29.2 43.0 %copy-start.2 = (bf16[128,256]{1,0:T(8,128)(2,1)S(1)}, bf16[128,256]{1,0:T(8,128)(2,1)}, u32[]{:S(2)}) copy-start(bf16[128,256]{1,0:T(8,128)(2,1)} %g_ref.3) | copy-start | bytes 196612
  66.5 9.3 %collective-permute-start.1 = (bf16[16,1152]{1,0:T(8,128)(2,1)S(1)}, bf16[16,1152]{1,0:T(8,128)(2,1)S(1)}, u32[]{:S(2)}, u32[]{:S(2)}) collective-permute-start(bf16[16,1152]{1,0:T(8,128)(2,1)S(1)} %get-tuple-element.16), channel_id=1, source_target_pairs={{0,32},{32,0},{64,96},{96,64},{128,160},{160,128},{192,224},{224,1... | collective-permute-start | bytes 110600 | tf_op jit(solution)/shard_map/ppermute | solution.py:348
  73.9 9.4 %collective-permute-start.2 = (bf16[64,3712]{1,0:T(8,128)(2,1)S(1)}, bf16[64,3712]{1,0:T(8,128)(2,1)}, u32[]{:S(2)}, u32[]{:S(2)}) collective-permute-start(bf16[64,3712]{1,0:T(8,128)(2,1)S(1)} %get-tuple-element.21), channel_id=1, source_target_pairs={{0,32},{32,0},{64,96},{96,64},{128,160},{160,128},{192,224},{224,1... | collective-permute-start | bytes 1425416 | tf_op jit(solution)/shard_map/ppermute | solution.py:361
  76.6 18.3 %all-to-all-start.1 = ((bf16[8,16,1152]{2,1,0:T(8,128)(2,1)}), bf16[8,16,1152]{2,1,0:T(8,128)(2,1)S(1)}, u32[]{:S(2)}, u32[]{:S(2)}) async-start(bf16[8,16,1152]{2,1,0:T(8,128)(2,1)} %broadcast_in_dim.129), calls=%async_computation.1 | async-start | bytes 589824 | tf_op jit(solution)/shard_map/all_to_all | solution.py:284
  84.5 17.0 %collective-permute-start.3 = (bf16[4,8,3712]{2,1,0:T(8,128)(2,1)S(1)}, bf16[4,8,3712]{2,1,0:T(8,128)(2,1)S(1)}, u32[]{:S(2)}, u32[]{:S(2)}) collective-permute-start(bf16[4,8,3712]{2,1,0:T(8,128)(2,1)S(1)} %dynamic-slice_bitcast_fusion), channel_id=1, source_target_pairs={{0,64},{32,96},{64,0},{96,32},{128,192},{160,224},{192,128},{224,1... | collective-permute-start | bytes 712712 | tf_op jit(solution)/shard_map/ppermute | solution.py:365
  96.0 32.3 %all-to-all-start.2 = ((bf16[32,16,1152]{2,1,0:T(8,128)(2,1)}), bf16[32,16,1152]{2,1,0:T(8,128)(2,1)S(1)}, u32[]{:S(2)}, u32[]{:S(2)}) async-start(bf16[32,16,1152]{2,1,0:T(8,128)(2,1)} %broadcast_in_dim.130), calls=%async_computation.2 | async-start | bytes 2359296 | tf_op jit(solution)/shard_map/all_to_all | solution.py:284
  101.6 11.4 %collective-permute-start.4 = (bf16[8,3712]{1,0:T(8,128)(2,1)S(1)}, bf16[8,3712]{1,0:T(8,128)(2,1)S(1)}, u32[]{:S(2)}, u32[]{:S(2)}) collective-permute-start(bf16[8,3712]{1,0:T(8,128)(2,1)S(1)} %get-tuple-element.34), channel_id=1, source_target_pairs={{0,128},{32,160},{64,192},{96,224},{128,0},{160,32},{192,64},{224,... | collective-permute-start | bytes 178184 | tf_op jit(solution)/shard_map/ppermute | solution.py:371
  103.5 9.5 %collective-permute-start.5 = (bf16[8,3712]{1,0:T(8,128)(2,1)S(1)}, bf16[8,3712]{1,0:T(8,128)(2,1)S(1)}, u32[]{:S(2)}, u32[]{:S(2)}) collective-permute-start(bf16[8,3712]{1,0:T(8,128)(2,1)S(1)} %get-tuple-element.36), channel_id=1, source_target_pairs={{0,256},{32,288},{64,320},{96,352},{128,384},{160,416},{192,448},{... | collective-permute-start | bytes 178184 | tf_op jit(solution)/shard_map/ppermute | solution.py:371
  108.4 7.3 %collective-permute-start.6 = (bf16[8,3712]{1,0:T(8,128)(2,1)S(1)}, bf16[8,3712]{1,0:T(8,128)(2,1)S(1)}, u32[]{:S(2)}, u32[]{:S(2)}) collective-permute-start(bf16[8,3712]{1,0:T(8,128)(2,1)S(1)} %get-tuple-element.35), channel_id=1, source_target_pairs={{0,384},{32,416},{64,448},{96,480},{128,256},{160,288},{192,320},{... | collective-permute-start | bytes 178184 | tf_op jit(solution)/shard_map/ppermute | solution.py:371
  128.4 9.3 %collective-permute-start.7 = (bf16[32,16,1152]{2,1,0:T(8,128)(2,1)S(1)}, bf16[32,16,1152]{2,1,0:T(8,128)(2,1)S(1)}, u32[]{:S(2)}, u32[]{:S(2)}) collective-permute-start(bf16[32,16,1152]{2,1,0:T(8,128)(2,1)S(1)} %all-to-all-done.2.mine_ref), channel_id=1, source_target_pairs={{0,32},{32,0},{64,96},{96,64},{128,160},{160,128},{192,224},{224,1... | collective-permute-start | bytes 3538952 | tf_op jit(solution)/shard_map/ppermute | solution.py:373
  163.4 4.0 %collective-permute-start.8 = (bf16[64,2432]{1,0:T(8,128)(2,1)S(1)}, bf16[64,2432]{1,0:T(8,128)(2,1)S(1)}, u32[]{:S(2)}, u32[]{:S(2)}) collective-permute-start(bf16[64,2432]{1,0:T(8,128)(2,1)S(1)} %bitcast.91), channel_id=1, source_target_pairs={{0,32},{32,0},{64,96},{96,64},{128,160},{160,128},{192,224},{224,1... | collective-permute-start | bytes 933896 | tf_op jit(solution)/shard_map/ppermute | solution.py:393
  169.3 15.1 %collective-permute-start.9 = (bf16[2,8,128,128]{3,2,1,0:T(8,128)(2,1)S(1)}, bf16[2,8,128,128]{3,2,1,0:T(8,128)(2,1)}, u32[]{:S(2)}, u32[]{:S(2)}) collective-permute-start(bf16[2,8,128,128]{3,2,1,0:T(8,128)(2,1)S(1)} %get-tuple-element.25), channel_id=1, source_target_pairs={{0,1},{1,0},{2,3},{3,2},{4,5},{5,4},{6,7},{7,6},{8,9},{9,8},{10,11... | collective-permute-start | bytes 1572872 | tf_op jit(solution)/shard_map/ppermute | solution.py:288
  176.1 54.4 %all-to-all-start.4 = ((bf16[16,160,256]{2,1,0:T(8,128)(2,1)}), bf16[16,160,256]{2,1,0:T(8,128)(2,1)S(1)}, u32[]{:S(2)}, u32[]{:S(2)}) async-start(bf16[16,160,256]{2,1,0:T(8,128)(2,1)} %shard_map.96), calls=%async_computation.4 | async-start | bytes 2621440 | tf_op jit(solution)/shard_map/all_to_all | solution.py:284
  181.5 8.7 %copy-start.3 = (bf16[16,8,128]{1,0,2:T(8,128)(2,1)S(1)}, bf16[16,8,128]{1,0,2:T(8,128)(2,1)}, u32[]{:S(2)}) copy-start(bf16[16,8,128]{1,0,2:T(8,128)(2,1)} %copy.22) | copy-start | bytes 98308
  185.6 12.6 %copy-start.4 = (bf16[16,8,128]{1,0,2:T(8,128)(2,1)S(1)}, bf16[16,8,128]{1,0,2:T(8,128)(2,1)}, u32[]{:S(2)}) copy-start(bf16[16,8,128]{1,0,2:T(8,128)(2,1)} %copy.22) | copy-start | bytes 98308
  185.7 9.8 %collective-permute-start.10 = (bf16[8,128,128]{2,1,0:T(8,128)(2,1)S(1)}, bf16[8,128,128]{2,1,0:T(8,128)(2,1)S(1)}, u32[]{:S(2)}, u32[]{:S(2)}) collective-permute-start(bf16[8,128,128]{2,1,0:T(8,128)(2,1)S(1)} %fusion.3), channel_id=1, source_target_pairs={{0,3},{1,2},{2,1},{3,0},{4,7},{5,6},{6,5},{7,4},{8,11},{9,10},{10,... | collective-permute-start | bytes 786440 | tf_op jit(solution)/shard_map/ppermute | solution.py:288
  195.6 6.0 %collective-permute-start.11 = (bf16[4,128,128]{2,1,0:T(8,128)(2,1)S(1)}, bf16[4,128,128]{2,1,0:T(8,128)(2,1)S(1)}, u32[]{:S(2)}, u32[]{:S(2)}) collective-permute-start(bf16[4,128,128]{2,1,0:T(8,128)(2,1)S(1)} %dynamic-slice_bitcast_fusion.1), channel_id=1, source_target_pairs={{0,4},{1,5},{2,6},{3,7},{4,0},{5,1},{6,2},{7,3},{8,12},{9,13},{10,... | collective-permute-start | bytes 393224 | tf_op jit(solution)/shard_map/ppermute | solution.py:288
  201.7 8.9 %collective-permute-start.12 = (bf16[2,128,128]{2,1,0:T(8,128)(2,1)S(1)}, bf16[2,128,128]{2,1,0:T(8,128)(2,1)S(1)}, u32[]{:S(2)}, u32[]{:S(2)}) collective-permute-start(bf16[2,128,128]{2,1,0:T(8,128)(2,1)S(1)} %dynamic-slice_bitcast_fusion.2), channel_id=1, source_target_pairs={{0,16},{1,17},{2,18},{3,19},{4,20},{5,21},{6,22},{7,23},{8,24},{9,... | collective-permute-start | bytes 196616 | tf_op jit(solution)/shard_map/ppermute | solution.py:288
  210.7 12.0 %collective-permute-start.13 = (bf16[128,128]{1,0:T(8,128)(2,1)S(1)}, bf16[128,128]{1,0:T(8,128)(2,1)S(1)}, u32[]{:S(2)}, u32[]{:S(2)}) collective-permute-start(bf16[128,128]{1,0:T(8,128)(2,1)S(1)} %get-tuple-element.39), channel_id=1, source_target_pairs={{0,256},{1,257},{2,288},{3,289},{4,320},{5,321},{6,352},{7,353},{8... | collective-permute-start | bytes 98312 | tf_op jit(solution)/shard_map/ppermute | solution.py:304
  220.1 9.7 %collective-permute-start.14 = (bf16[128,128]{1,0:T(8,128)(2,1)S(1)}, bf16[128,128]{1,0:T(8,128)(2,1)S(1)}, u32[]{:S(2)}, u32[]{:S(2)}) collective-permute-start(bf16[128,128]{1,0:T(8,128)(2,1)S(1)} %get-tuple-element.40), channel_id=1, source_target_pairs={{0,384},{1,385},{2,416},{3,417},{4,448},{5,449},{6,480},{7,481},{8... | collective-permute-start | bytes 98312 | tf_op jit(solution)/shard_map/ppermute | solution.py:305

commit v5 on v4

--- a/solution.py
+++ b/solution.py
@@ -30,6 +30,7 @@
 
 
 def hi_lo(v):
+    v = jnp.minimum(v, 3.0e38)
     hi = v.astype(BF).astype(F32)
     return hi, v - hi
 
@@ -46,7 +47,7 @@
     taking = ints[4] > 0
     for s in range(SECT):
         for h in range(2):
-            block = w_ref[2 * (s ^ 8) + h, 0:128, :]
+            block = w_ref[4 * place_z(s) + 2 * (s % 2) + h, 0:128, :]
             lanes = slice(128 * h, 128 * h + 128)
             wc_ref[128 * s : 128 * s + 128, lanes] = block
             uc_ref[64 * s : 64 * s + 64, lanes] = block[64:128]
@@ -73,7 +74,7 @@
         gref[...] = gr_ref[pl.ds(pl.multiple_of(16 * part, 16), 16), :].astype(BF)
 
 
-def project_kernel(ints, x_ref, pair_ref, g_ref, wc_ref, uc_ref, keep_ref, send_ref, res_ref, ex_ref):
+def project_kernel(ints, x_ref, pair_ref, g_ref, wc_ref, uc_ref, o0, o1, o2, o3, res_ref, ex_ref):
     core, sec = ints[2], ints[5]
     x = x_ref[...]
     pair = pair_ref[...]
@@ -100,8 +101,12 @@
     lane = lax.broadcasted_iota(jnp.int32, (ROWS, 128), 1) - 4 * sec
     own_part = jnp.where(lane == 0, own_hi, 0.0) + jnp.where(lane == 1, own_lo, 0.0)
     res_ref[:, 3584:3712] = ex_ref[0:ROWS, :] + own_part
-    for ref, part in ((keep_ref, core), (send_ref, 1 - core)):
-        ref[...] = res_ref[pl.ds(pl.multiple_of(64 * part, 64), 64), :].astype(BF)
+    for k, ref in enumerate((o0, o1, o2, o3)):
+        first = 64 * (core ^ (k % 2)) + 8 * (((sec >> 1) & 1) ^ (k // 2))
+        for j in range(2):
+            low = res_ref[pl.ds(pl.multiple_of(first + 32 * j, 8), 8), :]
+            high = res_ref[pl.ds(pl.multiple_of(first + 32 * j + 16, 8), 8), :]
+            ref[16 * j : 16 * j + 16, :] = jnp.concatenate([low, high], axis=0).astype(BF)
 
 
 def slab_place(s):
@@ -253,7 +258,7 @@
         if s % 2 == 0:
             for ref, flips in ((keep_ref, (0, 3)), (send_ref, (1, 2))):
                 for k in range(2):
-                    ref[k, s // 2 ^ 4] = pick(blocks, along ^ flips[k])
+                    ref[k, place_z(s)] = pick(blocks, along ^ flips[k])
         if s:
             z = back_ref[:, 1024 + 64 * s : 1024 + 64 * s + 64]
             g = g + dot(z, wc_ref[128 * s : 128 * s + 64, :], NN) - betas[:, s : s + 1] * xs.astype(F32)
@@ -288,26 +293,30 @@
     return lax.ppermute(value, "dp", [(i, i ^ bits) for i in range(DP)])
 
 
-def scatter_sum(keep, send, me):
+def scatter_sum(keep, send, me, later):
     value = keep.astype(F32) + flip(send, 1).astype(F32)
     value = value[0] + flip(value[1].astype(BF), 3).astype(F32)
-    for b in (2, 4, 3):
-        blocks = value.astype(BF).reshape((-1, 2, 128, 128))
-        if b == 4:
-            blocks = blocks.reshape(2, 2, 128, 128).swapaxes(0, 1)
-        bit = (me >> b) & 1
-        keep = lax.dynamic_index_in_dim(blocks, bit, 1, keepdims=False)
-        send = lax.dynamic_index_in_dim(blocks, 1 - bit, 1, keepdims=False)
-        if b != 3:
-            value = keep.astype(F32) + flip(send, 1 << b).astype(F32)
+    value, later = lax.optimization_barrier((value, later))
+    blocks = value.astype(BF).reshape(2, 4, 128, 128)
+    along = (me >> 2) & 3
+    value = lax.dynamic_index_in_dim(value.reshape(2, 4, 128, 128), along, 1, keepdims=False)
+    for k in (1, 2, 3):
+        value = value + flip(lax.dynamic_index_in_dim(blocks, along ^ k, 1, keepdims=False), 4 * k).astype(F32)
+    value = value.astype(BF)
+    keep = lax.dynamic_index_in_dim(value, me >> 4, 0, keepdims=False)
+    send = lax.dynamic_index_in_dim(value, 1 - (me >> 4), 0, keepdims=False)
     both = ("section", "dp")
-    mine = lax.ppermute(keep[0], both, [(a, owner(a // DP, a % DP)) for a in range(SECT * DP)])
-    theirs = lax.ppermute(send[0], both, [(a, owner(a // DP, a % DP ^ 8)) for a in range(SECT * DP)])
-    return mine.astype(F32) + theirs.astype(F32)
+    mine = lax.ppermute(keep, both, [(a, owner(a // DP, a % DP)) for a in range(SECT * DP)])
+    theirs = lax.ppermute(send, both, [(a, owner(a // DP, a % DP ^ 16)) for a in range(SECT * DP)])
+    return mine, theirs, later
+
+
+def place_z(s):
+    return (s // 2 - 2) % 8
 
 
 def owner(sec, q):
-    return (q // 2 ^ 8) * DP + 2 * sec + q % 2
+    return (2 * ((q // 4 + 2) % 8) + q // 2 % 2) * DP + 2 * sec + q % 2
 
 
 def body(x, g, worker, gain, narrow, widen):
@@ -346,10 +355,10 @@
     )(ints, weights)
     swap = [(i, i ^ 1) for i in range(SECT)]
     share = (gkeep.astype(F32) + lax.ppermute(gsend, "section", swap).astype(F32)).astype(BF)
-    keep, send = call(
+    parts = call(
         project_kernel,
         5,
-        (shape(64, PIECE), shape(64, PIECE)),
+        (shape(32, PIECE),) * 4,
         [pltpu.VMEM((ROWS, PIECE), F32), pltpu.VMEM((4 * ROWS, 128), F32)],
         3 * 10**8,
         3 * 10**6,
@@ -358,12 +367,10 @@
     share = jnp.sum(share.astype(F32), axis=0).astype(BF)
     half = exchange(jnp.broadcast_to(share[None], (DP, 16, GW)), "dp")
 
-    rows = (keep.astype(F32) + lax.ppermute(send, "section", swap).astype(F32)).astype(BF).reshape(8, 8, PIECE)
-    bit = (sec >> 1) & 1
-    both = rows.reshape(4, 2, 8, PIECE)
-    send = lax.dynamic_index_in_dim(both, 1 - bit, 1, keepdims=False)
-    send = lax.ppermute(send, "section", [(i, i ^ 2) for i in range(SECT)])
-    rows = (lax.dynamic_index_in_dim(both, bit, 1, keepdims=False).astype(F32) + send.astype(F32)).astype(BF)
+    rows = parts[0].astype(F32)
+    for k in range(1, 4):
+        rows = rows + lax.ppermute(parts[k], "section", [(i, i ^ k) for i in range(SECT)]).astype(F32)
+    rows = rows.astype(BF).reshape(4, 8, PIECE)
     here = sec // 4
     total = lax.dynamic_index_in_dim(rows, here, 0, keepdims=False).astype(F32)
     for k in range(1, 4):
@@ -422,10 +429,14 @@
         3 * 10**6,
     )(jnp.stack([own_at, pair_at, alive.astype(jnp.int32), core]).astype(jnp.int32), x, pair, back, back_other, extra_h, wc)
     saved = exchange(rows_out, "section")
-    grads = scatter_sum(*blocks, me)
+    misc = small[:, :, 256:384]
+    mine_sum, other_sum, misc = scatter_sum(*blocks, me, misc)
     saved = call(join_kernel, 1, shape(1, 1, ROWS + PAIR, D), [], 0, 3 * 10**6, False)(saved)
 
-    misc = small[:, :, 256:384].astype(F32)
+    saved, mine_sum, other_sum = lax.optimization_barrier((saved, mine_sum, other_sum))
+    grads = mine_sum.astype(F32) + other_sum.astype(F32)
+
+    misc = misc.astype(F32)
     own_inv = misc[:, :, 16:32] + misc[:, :, 32:48]
     pair_inv = misc[:, 0:2, 48:64] + misc[:, 0:2, 64:80]
     own_inv = lax.dynamic_index_in_dim(own_inv, sec, 2, keepdims=False).reshape(ROWS)

time: 235 us -> 230 us (0.979)
  the two profiles are of different devices: /device:TPU:1 before, /device:TPU:35 now
where the time goes in v5:
time: 230 us; the launch traced here: 229 us
  starting transfers between devices  97.2 us (42%)
  waiting for transfers between devices  78.5 us (34%)
  Pallas kernels  19.1 us (8%)
  blocking collectives  14 us (6%)
  other arithmetic  9.83 us (4%)
  local copies, waits for them, and re-layouts  6.63 us (3%)
  between operations  3.8 us (2%)
    all_to_all x4, waiting for transfers between devices, exchange(): lax.all_to_all(value, axis, 0, 0, tiled=True, axis_index_groups=groups)  45.9 us
    all_to_all x4, starting transfers between devices, exchange(): lax.all_to_all(value, axis, 0, 0, tiled=True, axis_index_groups=groups)  31.7 us
    ppermute x5, starting transfers between devices, flip(): return lax.ppermute(value, 'dp', [(i, i ^ bits) for i in range(DP)])  14.8 us
    all_to_all x1, blocking collectives, exchange(): lax.all_to_all(value, axis, 0, 0, tiled=True, axis_index_groups=groups)  14 us
    ppermute x3, starting transfers between devices, body(): lax.ppermute(send, 'section', [(i, i ^ 4 * k) for i in range(SECT)])  11.4 us
    ppermute x1, waiting for transfers between devices, scatter_sum(): lax.ppermute(send, both, [(a, owner(a // DP, a % DP ^ 16)) for a in range...  10.8 us
    pallas_call x1, Pallas kernels, body(): call(recur_kernel, 3, shape(8, BACK), [pltpu.VMEM((1024, GW), BF), pltpu....  10.4 us
    ppermute x1, starting transfers between devices, scatter_sum(): lax.ppermute(keep, both, [(a, owner(a // DP, a % DP)) for a in range(SECT...  10.1 us
  transfers between devices with their start and end apart: 21, of which 14 were waited for; matrix products, arithmetic and copies ran while one was open for 5% of the time, Pallas kernels for 3%

profile of v5, /device:TPU:35, one launch (start us, length us, event | category | flops | bytes accessed | tf_op | source)
XLA Modules:
  0.0 229.0 jit_solution(7841911406573372511)
XLA Ops:
  0.7 0.7 copy-done
  1.4 0.7 fusion.10
  2.1 0.7 pad_maximum_fusion.1
  2.8 7.5 %collective-permute-start = (bf16[128,128]{1,0:T(8,128)(2,1)S(1)}, bf16[128,128]{1,0:T(8,128)(2,1)S(1)}, u32[]{:S(2)}, u32[]{:S(2)}) collective-permute-start(bf16[128,128]{1,0:T(8,128)(2,1)S(1)} %pad_maximum_fusion.1), channel_id=1, source_target_pairs={{128,0},{129,1},{160,2},{161,3},{192,4},{193,5},{224,6},{225,7},{2... | collective-permute-start | bytes 98312 | tf_op jit(solution)/shard_map/ppermute | solution.py:328
  10.3 0.7 slice.74
  11.0 0.2 fusion.23
  11.2 0.5 slice.75
  12.4 0.8 fusion.26
  13.2 0.2 select_select_fusion
  13.4 3.9 %collective-permute-done = bf16[128,128]{1,0:T(8,128)(2,1)S(1)} collective-permute-done((bf16[128,128]{1,0:T(8,128)(2,1)S(1)}, bf16[128,128]{1,0:T(8,128)(2,1)S(1)}, u32[]{:S(2)}, u32[]{:S(2)}) %collective-permute-start) | collective-permute-done | bytes 32800 | tf_op jit(solution)/shard_map/ppermute | solution.py:328
  17.3 0.2 broadcast_in_dim.111
  17.6 1.3 pad_maximum_fusion
  18.9 10.5 %all-to-all-start = ((bf16[32,192,128]{2,1,0:T(8,128)(2,1)}), bf16[32,192,128]{2,1,0:T(8,128)(2,1)S(1)}, u32[]{:S(2)}, u32[]{:S(2)}) async-start(bf16[32,192,128]{2,1,0:T(8,128)(2,1)} %pad_maximum_fusion), calls=%async_computation | async-start | bytes 3145728 | tf_op jit(solution)/shard_map/all_to_all | solution.py:289
  29.4 0.6 fusion.22
  30.8 0.6 select_reduce_fusion
  31.4 0.7 stack.53.ints
  32.1 35.2 %all-to-all-done.w_ref = bf16[32,192,128]{2,1,0:T(8,128)(2,1)S(1)} async-done(((bf16[32,192,128]{2,1,0:T(8,128)(2,1)}), bf16[32,192,128]{2,1,0:T(8,128)(2,1)S(1)}, u32[]{:S(2)}, u32[]{:S(2)}) %all-to-all-start) | async-done | bytes 1572896 | tf_op jit(solution)/shard_map/all_to_all | solution.py:289
  67.3 1.1 shard_map.93
  68.4 4.0 %collective-permute-start.1 = (bf16[16,1152]{1,0:T(8,128)(2,1)S(1)}, bf16[16,1152]{1,0:T(8,128)(2,1)S(1)}, u32[]{:S(2)}, u32[]{:S(2)}) collective-permute-start(bf16[16,1152]{1,0:T(8,128)(2,1)S(1)} %get-tuple-element.23), channel_id=1, source_target_pairs={{0,32},{32,0},{64,96},{96,64},{128,160},{160,128},{192,224},{224,1... | collective-permute-start | bytes 110600 | tf_op jit(solution)/shard_map/ppermute | solution.py:357
  72.4 0.8 collective-permute-done.1
  73.2 0.7 broadcast_in_dim.129
  74.0 6.6 %all-to-all-start.1 = ((bf16[8,16,1152]{2,1,0:T(8,128)(2,1)}), bf16[8,16,1152]{2,1,0:T(8,128)(2,1)S(1)}, u32[]{:S(2)}, u32[]{:S(2)}) async-start(bf16[8,16,1152]{2,1,0:T(8,128)(2,1)} %broadcast_in_dim.129), calls=%async_computation.1 | async-start | bytes 589824 | tf_op jit(solution)/shard_map/all_to_all | solution.py:289
  80.6 2.4 %shard_map.94 = (bf16[32,3712]{1,0:T(8,128)(2,1)S(1)}, bf16[32,3712]{1,0:T(8,128)(2,1)S(1)}, bf16[32,3712]{1,0:T(8,128)(2,1)}, bf16[32,3712]{1,0:T(8,128)(2,1)}) custom-call(s32[6]{0:T(128)S(1)} %stack.53.ints, bf16[128,256]{1,0:T(8,128)(2,1)S(1)} %copy-done.1, bf16[32,256]{1,0:T(8,128)(2,1)S(1)} %get-tuple-element.24.pair_ref, ...), custom_call_target="tpu_custom_call" | custom-call | flops 300000000 | bytes 3000000 | tf_op jit(solution)/shard_map/pallas_call | solution.py:358
  83.0 3.0 %collective-permute-start.4 = (bf16[32,3712]{1,0:T(8,128)(2,1)}, bf16[32,3712]{1,0:T(8,128)(2,1)S(1)}, u32[]{:S(2)}, u32[]{:S(2)}) collective-permute-start(bf16[32,3712]{1,0:T(8,128)(2,1)} %get-tuple-element.30), channel_id=1, source_target_pairs={{0,96},{32,64},{64,32},{96,0},{128,224},{160,192},{192,160},{224,1... | collective-permute-start | bytes 712712 | tf_op jit(solution)/shard_map/ppermute | solution.py:372
  86.0 3.1 %collective-permute-start.3 = (bf16[32,3712]{1,0:T(8,128)(2,1)}, bf16[32,3712]{1,0:T(8,128)(2,1)S(1)}, u32[]{:S(2)}, u32[]{:S(2)}) collective-permute-start(bf16[32,3712]{1,0:T(8,128)(2,1)} %get-tuple-element.29), channel_id=1, source_target_pairs={{0,64},{32,96},{64,0},{96,32},{128,192},{160,224},{192,128},{224,1... | collective-permute-start | bytes 712712 | tf_op jit(solution)/shard_map/ppermute | solution.py:372
  89.1 1.9 collective-permute-start.2
  91.1 1.1 broadcast_in_dim.130
  92.2 5.5 %all-to-all-start.2 = ((bf16[32,16,1152]{2,1,0:T(8,128)(2,1)}), bf16[32,16,1152]{2,1,0:T(8,128)(2,1)S(1)}, u32[]{:S(2)}, u32[]{:S(2)}) async-start(bf16[32,16,1152]{2,1,0:T(8,128)(2,1)} %broadcast_in_dim.130), calls=%async_computation.2 | async-start | bytes 2359296 | tf_op jit(solution)/shard_map/all_to_all | solution.py:289
  97.8 1.1 collective-permute-done.3
  98.9 1.1 fusion.2
  100.0 3.9 %collective-permute-start.7 = (bf16[8,3712]{1,0:T(8,128)(2,1)S(1)}, bf16[8,3712]{1,0:T(8,128)(2,1)S(1)}, u32[]{:S(2)}, u32[]{:S(2)}) collective-permute-start(bf16[8,3712]{1,0:T(8,128)(2,1)S(1)} %get-tuple-element.52), channel_id=1, source_target_pairs={{0,384},{32,416},{64,448},{96,480},{128,256},{160,288},{192,320},{... | collective-permute-start | bytes 178184 | tf_op jit(solution)/shard_map/ppermute | solution.py:378
  103.9 3.7 %collective-permute-start.6 = (bf16[8,3712]{1,0:T(8,128)(2,1)S(1)}, bf16[8,3712]{1,0:T(8,128)(2,1)S(1)}, u32[]{:S(2)}, u32[]{:S(2)}) collective-permute-start(bf16[8,3712]{1,0:T(8,128)(2,1)S(1)} %get-tuple-element.53), channel_id=1, source_target_pairs={{0,256},{32,288},{64,320},{96,352},{128,384},{160,416},{192,448},{... | collective-permute-start | bytes 178184 | tf_op jit(solution)/shard_map/ppermute | solution.py:378
  107.6 3.8 %collective-permute-start.5 = (bf16[8,3712]{1,0:T(8,128)(2,1)S(1)}, bf16[8,3712]{1,0:T(8,128)(2,1)S(1)}, u32[]{:S(2)}, u32[]{:S(2)}) collective-permute-start(bf16[8,3712]{1,0:T(8,128)(2,1)S(1)} %get-tuple-element.51), channel_id=1, source_target_pairs={{0,128},{32,160},{64,192},{96,224},{128,0},{160,32},{192,64},{224,... | collective-permute-start | bytes 178184 | tf_op jit(solution)/shard_map/ppermute | solution.py:378
  111.4 1.6 collective-permute-done.6
  113.0 3.4 %collective-permute-done.5 = bf16[8,3712]{1,0:T(8,128)(2,1)S(1)} collective-permute-done((bf16[8,3712]{1,0:T(8,128)(2,1)S(1)}, bf16[8,3712]{1,0:T(8,128)(2,1)S(1)}, u32[]{:S(2)}, u32[]{:S(2)}) %collective-permute-start.5) | collective-permute-done | bytes 59424 | tf_op jit(solution)/shard_map/ppermute | solution.py:378
  116.5 10.6 %all-to-all-done.2.mine_ref = bf16[32,16,1152]{2,1,0:T(8,128)(2,1)S(1)} async-done(((bf16[32,16,1152]{2,1,0:T(8,128)(2,1)}), bf16[32,16,1152]{2,1,0:T(8,128)(2,1)S(1)}, u32[]{:S(2)}, u32[]{:S(2)}) %all-to-all-start.2) | async-done | bytes 1179680 | tf_op jit(solution)/shard_map/all_to_all | solution.py:289
  127.1 4.7 %collective-permute-start.8 = (bf16[32,16,1152]{2,1,0:T(8,128)(2,1)S(1)}, bf16[32,16,1152]{2,1,0:T(8,128)(2,1)S(1)}, u32[]{:S(2)}, u32[]{:S(2)}) collective-permute-start(bf16[32,16,1152]{2,1,0:T(8,128)(2,1)S(1)} %all-to-all-done.2.mine_ref), channel_id=1, source_target_pairs={{0,32},{32,0},{64,96},{96,64},{128,160},{160,128},{192,224},{224,1... | collective-permute-start | bytes 3538952 | tf_op jit(solution)/shard_map/ppermute | solution.py:380
  131.8 2.5 %collective-permute-done.8.other_ref = bf16[32,16,1152]{2,1,0:T(8,128)(2,1)S(1)} collective-permute-done((bf16[32,16,1152]{2,1,0:T(8,128)(2,1)S(1)}, bf16[32,16,1152]{2,1,0:T(8,128)(2,1)S(1)}, u32[]{:S(2)}, u32[]{:S(2)}) %collective-permute-start.8) | collective-permute-done | bytes 1179680 | tf_op jit(solution)/shard_map/ppermute | solution.py:380
  134.2 10.4 %shard_map.95 = bf16[8,2432]{1,0:T(8,128)(2,1)S(1)} custom-call(s32[1]{0:T(128)} %bitcast.ints, f32[8,3712]{1,0:T(8,128)S(1)} %fusion.7.sum_ref, bf16[32,16,1152]{2,1,0:T(8,128)(2,1)S(1)} %all-to-all-done.2.mine_ref, bf16[32,16,1152]{2,1,0:T(8,128)(2,1)S(1)} %collective-permute-done.8.other_ref), custom_call_target="tpu_custom_call" | custom-call | flops 200000000 | bytes 3000000 | tf_op jit(solution)/shard_map/pallas_call | solution.py:382
  144.6 14.0 %all_to_all.25 = bf16[8,8,2432]{2,1,0:T(8,128)(2,1)S(1)} all-to-all(bf16[8,8,2432]{2,1,0:T(8,128)(2,1)S(1)} %broadcast_in_dim.131), channel_id=1, replica_groups={{0,64,128,192,256,320,384,448},{32,96,160,224,288,352,416,480},{1,65,12..., dimensions={0} | all-to-all | bytes 622592 | tf_op jit(solution)/shard_map/all_to_all | solution.py:289
  158.6 3.1 %collective-permute-start.9 = (bf16[64,2432]{1,0:T(8,128)(2,1)S(1)}, bf16[64,2432]{1,0:T(8,128)(2,1)S(1)}, u32[]{:S(2)}, u32[]{:S(2)}) collective-permute-start(bf16[64,2432]{1,0:T(8,128)(2,1)S(1)} %bitcast.89), channel_id=1, source_target_pairs={{0,32},{32,0},{64,96},{96,64},{128,160},{160,128},{192,224},{224,1... | collective-permute-start | bytes 933896 | tf_op jit(solution)/shard_map/ppermute | solution.py:400
  161.8 1.1 collective-permute-done.9.other_ref
  163.0 1.9 shard_map.96
  164.9 1.9 collective-permute-start.10
  168.4 2.1 shard_map.97
  170.5 9.1 %all-to-all-start.4 = ((bf16[16,160,256]{2,1,0:T(8,128)(2,1)}), bf16[16,160,256]{2,1,0:T(8,128)(2,1)S(1)}, u32[]{:S(2)}, u32[]{:S(2)}) async-start(bf16[16,160,256]{2,1,0:T(8,128)(2,1)} %shard_map.97), calls=%async_computation.4 | async-start | bytes 2621440 | tf_op jit(solution)/shard_map/all_to_all | solution.py:289
  179.6 0.4 collective-permute-done.10
  180.0 1.2 convert_add_fusion
  181.2 3.7 %collective-permute-start.11 = (bf16[8,128,128]{2,1,0:T(8,128)(2,1)S(1)}, bf16[8,128,128]{2,1,0:T(8,128)(2,1)}, u32[]{:S(2)}, u32[]{:S(2)}) collective-permute-start(bf16[8,128,128]{2,1,0:T(8,128)(2,1)S(1)} %fusion.1), channel_id=1, source_target_pairs={{0,3},{1,2},{2,1},{3,0},{4,7},{5,6},{6,5},{7,4},{8,11},{9,10},{10,... | collective-permute-start | bytes 786440 | tf_op jit(solution)/shard_map/ppermute | solution.py:293
  184.9 0.4 copy.20
  185.4 5.1 %collective-permute-done.11 = bf16[8,128,128]{2,1,0:T(8,128)(2,1)} collective-permute-done((bf16[8,128,128]{2,1,0:T(8,128)(2,1)S(1)}, bf16[8,128,128]{2,1,0:T(8,128)(2,1)}, u32[]{:S(2)}, u32[]{:S(2)}) %collective-permute-start.11) | collective-permute-done | bytes 262176 | tf_op jit(solution)/shard_map/ppermute | solution.py:293
  190.4 1.0 fusion
  191.6 3.8 %collective-permute-start.14 = (bf16[2,128,128]{2,1,0:T(8,128)(2,1)S(1)}, bf16[2,128,128]{2,1,0:T(8,128)(2,1)S(1)}, u32[]{:S(2)}, u32[]{:S(2)}) collective-permute-start(bf16[2,128,128]{2,1,0:T(8,128)(2,1)S(1)} %get-tuple-element.49), channel_id=1, source_target_pairs={{0,12},{1,13},{2,14},{3,15},{4,8},{5,9},{6,10},{7,11},{8,4},{9,5},... | collective-permute-start | bytes 196616 | tf_op jit(solution)/shard_map/ppermute | solution.py:293
  195.4 2.4 %collective-permute-start.13 = (bf16[2,128,128]{2,1,0:T(8,128)(2,1)S(1)}, bf16[2,128,128]{2,1,0:T(8,128)(2,1)S(1)}, u32[]{:S(2)}, u32[]{:S(2)}) collective-permute-start(bf16[2,128,128]{2,1,0:T(8,128)(2,1)S(1)} %get-tuple-element.50), channel_id=1, source_target_pairs={{0,8},{1,9},{2,10},{3,11},{4,12},{5,13},{6,14},{7,15},{8,0},{9,1},... | collective-permute-start | bytes 196616 | tf_op jit(solution)/shard_map/ppermute | solution.py:293
  197.8 3.1 %collective-permute-start.12 = (bf16[2,128,128]{2,1,0:T(8,128)(2,1)S(1)}, bf16[2,128,128]{2,1,0:T(8,128)(2,1)S(1)}, u32[]{:S(2)}, u32[]{:S(2)}) collective-permute-start(bf16[2,128,128]{2,1,0:T(8,128)(2,1)S(1)} %get-tuple-element.48), channel_id=1, source_target_pairs={{0,4},{1,5},{2,6},{3,7},{4,0},{5,1},{6,2},{7,3},{8,12},{9,13},{10,... | collective-permute-start | bytes 196616 | tf_op jit(solution)/shard_map/ppermute | solution.py:293
  201.0 0.7 fusion.19
  201.8 0.6 collective-permute-done.13
  202.4 1.2 collective-permute-done.12
  203.7 10.1 %collective-permute-start.15 = (bf16[128,128]{1,0:T(8,128)(2,1)S(1)}, bf16[128,128]{1,0:T(8,128)(2,1)S(1)}, u32[]{:S(2)}, u32[]{:S(2)}) collective-permute-start(bf16[128,128]{1,0:T(8,128)(2,1)S(1)} %get-tuple-element.57), channel_id=1, source_target_pairs={{0,128},{1,129},{2,160},{3,161},{4,192},{5,193},{6,224},{7,225},{8... | collective-permute-start | bytes 98312 | tf_op jit(solution)/shard_map/ppermute | solution.py:309
  213.8 1.9 collective-permute-start.16
  215.8 0.6 broadcast_select_fusion
  216.4 1.2 shard_map.98
  217.6 10.8 %collective-permute-done.16 = bf16[128,128]{1,0:T(8,128)(2,1)S(1)} collective-permute-done((bf16[128,128]{1,0:T(8,128)(2,1)S(1)}, bf16[128,128]{1,0:T(8,128)(2,1)S(1)}, u32[]{:S(2)}, u32[]{:S(2)}) %collective-permute-start.16) | collective-permute-done | bytes 32800 | tf_op jit(solution)/shard_map/ppermute | solution.py:310
  228.4 0.6 slice_bitcast_fusion.1
  (44 shorter events, 1.0 us)
Async XLA Ops:
  0.6 0.7 copy-start
  2.8 14.5 %collective-permute-start = (bf16[128,128]{1,0:T(8,128)(2,1)S(1)}, bf16[128,128]{1,0:T(8,128)(2,1)S(1)}, u32[]{:S(2)}, u32[]{:S(2)}) collective-permute-start(bf16[128,128]{1,0:T(8,128)(2,1)S(1)} %pad_maximum_fusion.1), channel_id=1, source_target_pairs={{128,0},{129,1},{160,2},{161,3},{192,4},{193,5},{224,6},{225,7},{2... | collective-permute-start | bytes 98312 | tf_op jit(solution)/shard_map/ppermute | solution.py:328
  18.9 48.5 %all-to-all-start = ((bf16[32,192,128]{2,1,0:T(8,128)(2,1)}), bf16[32,192,128]{2,1,0:T(8,128)(2,1)S(1)}, u32[]{:S(2)}, u32[]{:S(2)}) async-start(bf16[32,192,128]{2,1,0:T(8,128)(2,1)} %pad_maximum_fusion), calls=%async_computation | async-start | bytes 3145728 | tf_op jit(solution)/shard_map/all_to_all | solution.py:289
  29.4 51.3 %copy-start.1 = (bf16[128,256]{1,0:T(8,128)(2,1)S(1)}, bf16[128,256]{1,0:T(8,128)(2,1)}, u32[]{:S(2)}) copy-start(bf16[128,256]{1,0:T(8,128)(2,1)} %x_ref.5) | copy-start | bytes 196612
  29.4 51.2 %copy-start.2 = (bf16[128,256]{1,0:T(8,128)(2,1)S(1)}, bf16[128,256]{1,0:T(8,128)(2,1)}, u32[]{:S(2)}) copy-start(bf16[128,256]{1,0:T(8,128)(2,1)} %g_ref.3) | copy-start | bytes 196612
  68.4 4.8 %collective-permute-start.1 = (bf16[16,1152]{1,0:T(8,128)(2,1)S(1)}, bf16[16,1152]{1,0:T(8,128)(2,1)S(1)}, u32[]{:S(2)}, u32[]{:S(2)}) collective-permute-start(bf16[16,1152]{1,0:T(8,128)(2,1)S(1)} %get-tuple-element.23), channel_id=1, source_target_pairs={{0,32},{32,0},{64,96},{96,64},{128,160},{160,128},{192,224},{224,1... | collective-permute-start | bytes 110600 | tf_op jit(solution)/shard_map/ppermute | solution.py:357
  74.0 17.1 %all-to-all-start.1 = ((bf16[8,16,1152]{2,1,0:T(8,128)(2,1)}), bf16[8,16,1152]{2,1,0:T(8,128)(2,1)S(1)}, u32[]{:S(2)}, u32[]{:S(2)}) async-start(bf16[8,16,1152]{2,1,0:T(8,128)(2,1)} %broadcast_in_dim.129), calls=%async_computation.1 | async-start | bytes 589824 | tf_op jit(solution)/shard_map/all_to_all | solution.py:289
  83.0 14.7 %collective-permute-start.4 = (bf16[32,3712]{1,0:T(8,128)(2,1)}, bf16[32,3712]{1,0:T(8,128)(2,1)S(1)}, u32[]{:S(2)}, u32[]{:S(2)}) collective-permute-start(bf16[32,3712]{1,0:T(8,128)(2,1)} %get-tuple-element.30), channel_id=1, source_target_pairs={{0,96},{32,64},{64,32},{96,0},{128,224},{160,192},{192,160},{224,1... | collective-permute-start | bytes 712712 | tf_op jit(solution)/shard_map/ppermute | solution.py:372
  86.0 12.9 %collective-permute-start.3 = (bf16[32,3712]{1,0:T(8,128)(2,1)}, bf16[32,3712]{1,0:T(8,128)(2,1)S(1)}, u32[]{:S(2)}, u32[]{:S(2)}) collective-permute-start(bf16[32,3712]{1,0:T(8,128)(2,1)} %get-tuple-element.29), channel_id=1, source_target_pairs={{0,64},{32,96},{64,0},{96,32},{128,192},{160,224},{192,128},{224,1... | collective-permute-start | bytes 712712 | tf_op jit(solution)/shard_map/ppermute | solution.py:372
  89.1 9.8 %collective-permute-start.2 = (bf16[32,3712]{1,0:T(8,128)(2,1)S(1)}, bf16[32,3712]{1,0:T(8,128)(2,1)}, u32[]{:S(2)}, u32[]{:S(2)}) collective-permute-start(bf16[32,3712]{1,0:T(8,128)(2,1)S(1)} %get-tuple-element.28), channel_id=1, source_target_pairs={{0,32},{32,0},{64,96},{96,64},{128,160},{160,128},{192,224},{224,1... | collective-permute-start | bytes 712712 | tf_op jit(solution)/shard_map/ppermute | solution.py:372
  92.2 34.9 %all-to-all-start.2 = ((bf16[32,16,1152]{2,1,0:T(8,128)(2,1)}), bf16[32,16,1152]{2,1,0:T(8,128)(2,1)S(1)}, u32[]{:S(2)}, u32[]{:S(2)}) async-start(bf16[32,16,1152]{2,1,0:T(8,128)(2,1)} %broadcast_in_dim.130), calls=%async_computation.2 | async-start | bytes 2359296 | tf_op jit(solution)/shard_map/all_to_all | solution.py:289
  100.0 11.4 %collective-permute-start.7 = (bf16[8,3712]{1,0:T(8,128)(2,1)S(1)}, bf16[8,3712]{1,0:T(8,128)(2,1)S(1)}, u32[]{:S(2)}, u32[]{:S(2)}) collective-permute-start(bf16[8,3712]{1,0:T(8,128)(2,1)S(1)} %get-tuple-element.52), channel_id=1, source_target_pairs={{0,384},{32,416},{64,448},{96,480},{128,256},{160,288},{192,320},{... | collective-permute-start | bytes 178184 | tf_op jit(solution)/shard_map/ppermute | solution.py:378
  103.9 9.1 %collective-permute-start.6 = (bf16[8,3712]{1,0:T(8,128)(2,1)S(1)}, bf16[8,3712]{1,0:T(8,128)(2,1)S(1)}, u32[]{:S(2)}, u32[]{:S(2)}) collective-permute-start(bf16[8,3712]{1,0:T(8,128)(2,1)S(1)} %get-tuple-element.53), channel_id=1, source_target_pairs={{0,256},{32,288},{64,320},{96,352},{128,384},{160,416},{192,448},{... | collective-permute-start | bytes 178184 | tf_op jit(solution)/shard_map/ppermute | solution.py:378
  107.6 8.9 %collective-permute-start.5 = (bf16[8,3712]{1,0:T(8,128)(2,1)S(1)}, bf16[8,3712]{1,0:T(8,128)(2,1)S(1)}, u32[]{:S(2)}, u32[]{:S(2)}) collective-permute-start(bf16[8,3712]{1,0:T(8,128)(2,1)S(1)} %get-tuple-element.51), channel_id=1, source_target_pairs={{0,128},{32,160},{64,192},{96,224},{128,0},{160,32},{192,64},{224,... | collective-permute-start | bytes 178184 | tf_op jit(solution)/shard_map/ppermute | solution.py:378
  127.1 7.1 %collective-permute-start.8 = (bf16[32,16,1152]{2,1,0:T(8,128)(2,1)S(1)}, bf16[32,16,1152]{2,1,0:T(8,128)(2,1)S(1)}, u32[]{:S(2)}, u32[]{:S(2)}) collective-permute-start(bf16[32,16,1152]{2,1,0:T(8,128)(2,1)S(1)} %all-to-all-done.2.mine_ref), channel_id=1, source_target_pairs={{0,32},{32,0},{64,96},{96,64},{128,160},{160,128},{192,224},{224,1... | collective-permute-start | bytes 3538952 | tf_op jit(solution)/shard_map/ppermute | solution.py:380
  158.6 4.4 %collective-permute-start.9 = (bf16[64,2432]{1,0:T(8,128)(2,1)S(1)}, bf16[64,2432]{1,0:T(8,128)(2,1)S(1)}, u32[]{:S(2)}, u32[]{:S(2)}) collective-permute-start(bf16[64,2432]{1,0:T(8,128)(2,1)S(1)} %bitcast.89), channel_id=1, source_target_pairs={{0,32},{32,0},{64,96},{96,64},{128,160},{160,128},{192,224},{224,1... | collective-permute-start | bytes 933896 | tf_op jit(solution)/shard_map/ppermute | solution.py:400
  164.9 15.1 %collective-permute-start.10 = (bf16[2,8,128,128]{3,2,1,0:T(8,128)(2,1)S(1)}, bf16[2,8,128,128]{3,2,1,0:T(8,128)(2,1)}, u32[]{:S(2)}, u32[]{:S(2)}) collective-permute-start(bf16[2,8,128,128]{3,2,1,0:T(8,128)(2,1)S(1)} %get-tuple-element.34), channel_id=1, source_target_pairs={{0,1},{1,0},{2,3},{3,2},{4,5},{5,4},{6,7},{7,6},{8,9},{9,8},{10,11... | collective-permute-start | bytes 1572872 | tf_op jit(solution)/shard_map/ppermute | solution.py:293
  170.5 45.9 %all-to-all-start.4 = ((bf16[16,160,256]{2,1,0:T(8,128)(2,1)}), bf16[16,160,256]{2,1,0:T(8,128)(2,1)S(1)}, u32[]{:S(2)}, u32[]{:S(2)}) async-start(bf16[16,160,256]{2,1,0:T(8,128)(2,1)} %shard_map.97), calls=%async_computation.4 | async-start | bytes 2621440 | tf_op jit(solution)/shard_map/all_to_all | solution.py:289
  181.2 9.2 %collective-permute-start.11 = (bf16[8,128,128]{2,1,0:T(8,128)(2,1)S(1)}, bf16[8,128,128]{2,1,0:T(8,128)(2,1)}, u32[]{:S(2)}, u32[]{:S(2)}) collective-permute-start(bf16[8,128,128]{2,1,0:T(8,128)(2,1)S(1)} %fusion.1), channel_id=1, source_target_pairs={{0,3},{1,2},{2,1},{3,0},{4,7},{5,6},{6,5},{7,4},{8,11},{9,10},{10,... | collective-permute-start | bytes 786440 | tf_op jit(solution)/shard_map/ppermute | solution.py:293
  191.6 10.2 %collective-permute-start.14 = (bf16[2,128,128]{2,1,0:T(8,128)(2,1)S(1)}, bf16[2,128,128]{2,1,0:T(8,128)(2,1)S(1)}, u32[]{:S(2)}, u32[]{:S(2)}) collective-permute-start(bf16[2,128,128]{2,1,0:T(8,128)(2,1)S(1)} %get-tuple-element.49), channel_id=1, source_target_pairs={{0,12},{1,13},{2,14},{3,15},{4,8},{5,9},{6,10},{7,11},{8,4},{9,5},... | collective-permute-start | bytes 196616 | tf_op jit(solution)/shard_map/ppermute | solution.py:293
  195.4 7.0 %collective-permute-start.13 = (bf16[2,128,128]{2,1,0:T(8,128)(2,1)S(1)}, bf16[2,128,128]{2,1,0:T(8,128)(2,1)S(1)}, u32[]{:S(2)}, u32[]{:S(2)}) collective-permute-start(bf16[2,128,128]{2,1,0:T(8,128)(2,1)S(1)} %get-tuple-element.50), channel_id=1, source_target_pairs={{0,8},{1,9},{2,10},{3,11},{4,12},{5,13},{6,14},{7,15},{8,0},{9,1},... | collective-permute-start | bytes 196616 | tf_op jit(solution)/shard_map/ppermute | solution.py:293
  197.8 5.9 %collective-permute-start.12 = (bf16[2,128,128]{2,1,0:T(8,128)(2,1)S(1)}, bf16[2,128,128]{2,1,0:T(8,128)(2,1)S(1)}, u32[]{:S(2)}, u32[]{:S(2)}) collective-permute-start(bf16[2,128,128]{2,1,0:T(8,128)(2,1)S(1)} %get-tuple-element.48), channel_id=1, source_target_pairs={{0,4},{1,5},{2,6},{3,7},{4,0},{5,1},{6,2},{7,3},{8,12},{9,13},{10,... | collective-permute-start | bytes 196616 | tf_op jit(solution)/shard_map/ppermute | solution.py:293
  203.7 13.9 %collective-permute-start.15 = (bf16[128,128]{1,0:T(8,128)(2,1)S(1)}, bf16[128,128]{1,0:T(8,128)(2,1)S(1)}, u32[]{:S(2)}, u32[]{:S(2)}) collective-permute-start(bf16[128,128]{1,0:T(8,128)(2,1)S(1)} %get-tuple-element.57), channel_id=1, source_target_pairs={{0,128},{1,129},{2,160},{3,161},{4,192},{5,193},{6,224},{7,225},{8... | collective-permute-start | bytes 98312 | tf_op jit(solution)/shard_map/ppermute | solution.py:309
  213.8 14.6 %collective-permute-start.16 = (bf16[128,128]{1,0:T(8,128)(2,1)S(1)}, bf16[128,128]{1,0:T(8,128)(2,1)S(1)}, u32[]{:S(2)}, u32[]{:S(2)}) collective-permute-start(bf16[128,128]{1,0:T(8,128)(2,1)S(1)} %get-tuple-element.56), channel_id=1, source_target_pairs={{0,384},{1,385},{2,416},{3,417},{4,448},{5,449},{6,480},{7,481},{8... | collective-permute-start | bytes 98312 | tf_op jit(solution)/shard_map/ppermute | solution.py:310

commit v6 on v5

--- a/solution.py
+++ b/solution.py
@@ -21,7 +21,7 @@
 BF = jnp.bfloat16
 NT = (((1,), (1,)), ((), ()))
 NN = (((1,), (0,)), ((), ()))
-Y_GROUPS = [[2 * y + c for y in range(8)] for c in range(2)]
+Y_GROUPS = [[2 * (2 * k + low) + c for low in range(2) for k in range(4)] for c in range(2)]
 VMEM_LIMIT = 48 * 1024 * 1024
 
 
@@ -102,11 +102,8 @@
     own_part = jnp.where(lane == 0, own_hi, 0.0) + jnp.where(lane == 1, own_lo, 0.0)
     res_ref[:, 3584:3712] = ex_ref[0:ROWS, :] + own_part
     for k, ref in enumerate((o0, o1, o2, o3)):
-        first = 64 * (core ^ (k % 2)) + 8 * (((sec >> 1) & 1) ^ (k // 2))
-        for j in range(2):
-            low = res_ref[pl.ds(pl.multiple_of(first + 32 * j, 8), 8), :]
-            high = res_ref[pl.ds(pl.multiple_of(first + 32 * j + 16, 8), 8), :]
-            ref[16 * j : 16 * j + 16, :] = jnp.concatenate([low, high], axis=0).astype(BF)
+        first = 64 * (core ^ (k % 2)) + 32 * (((sec >> 1) & 1) ^ (k // 2))
+        ref[...] = res_ref[pl.ds(pl.multiple_of(first, 32), 32), :].astype(BF)
 
 
 def slab_place(s):
@@ -294,15 +291,20 @@
 
 
 def scatter_sum(keep, send, me, later):
-    value = keep.astype(F32) + flip(send, 1).astype(F32)
-    value = value[0] + flip(value[1].astype(BF), 3).astype(F32)
+    first = flip(send, 1)
+    low = (me >> 2) & 1
+    arrived = 0.0
+    for e, b in ((1, 0), (0, 1), (1, 1)):
+        part = keep[e].astype(F32) + first[e].astype(F32)
+        part = lax.dynamic_index_in_dim(part.astype(BF).reshape(4, 2, 128, 128), low ^ b, 1, keepdims=False)
+        arrived = arrived + flip(part, 3 * e | 4 * b).astype(F32)
+    own = (keep[0].astype(F32) + first[0].astype(F32)).reshape(4, 2, 128, 128)
+    value = lax.dynamic_index_in_dim(own, low, 1, keepdims=False) + arrived
     value, later = lax.optimization_barrier((value, later))
-    blocks = value.astype(BF).reshape(2, 4, 128, 128)
-    along = (me >> 2) & 3
-    value = lax.dynamic_index_in_dim(value.reshape(2, 4, 128, 128), along, 1, keepdims=False)
-    for k in (1, 2, 3):
-        value = value + flip(lax.dynamic_index_in_dim(blocks, along ^ k, 1, keepdims=False), 4 * k).astype(F32)
-    value = value.astype(BF)
+    middle = (me >> 3) & 1
+    value = value.reshape(2, 2, 128, 128)
+    send = lax.dynamic_index_in_dim(value, 1 - middle, 1, keepdims=False).astype(BF)
+    value = (lax.dynamic_index_in_dim(value, middle, 1, keepdims=False) + flip(send, 8).astype(F32)).astype(BF)
     keep = lax.dynamic_index_in_dim(value, me >> 4, 0, keepdims=False)
     send = lax.dynamic_index_in_dim(value, 1 - (me >> 4), 0, keepdims=False)
     both = ("section", "dp")

time: 230 us -> 229 us (level)
    ppermute x5, starting transfers between devices: 14.8 us -> 12.2 us  [flip(): return lax.ppermute(value, 'dp', [(i, i ^ bits) for i in range(DP)])]
    ppermute x5, waiting for transfers between devices: 7.39 us -> 9.8 us  [flip(): return lax.ppermute(value, 'dp', [(i, i ^ bits) for i in range(DP)])]
  transfers between devices with their start and end apart: 21 -> 21, of which waited for: 14 -> 13; matrix products, arithmetic and copies ran while one was open for 5% -> 5% of each run, Pallas kernels for 3% -> 3%
where the time goes in v6:
time: 229 us; the launch traced here: 228 us
  starting transfers between devices  95.6 us (42%)
  waiting for transfers between devices  79.8 us (35%)
  Pallas kernels  19.1 us (8%)
  blocking collectives  13.8 us (6%)
  other arithmetic  8.83 us (4%)
  local copies, waits for them, and re-layouts  6.65 us (3%)
  between operations  3.77 us (2%)
    all_to_all x4, waiting for transfers between devices, exchange(): lax.all_to_all(value, axis, 0, 0, tiled=True, axis_index_groups=groups)  45.9 us
    all_to_all x4, starting transfers between devices, exchange(): lax.all_to_all(value, axis, 0, 0, tiled=True, axis_index_groups=groups)  31.4 us
    all_to_all x1, blocking collectives, exchange(): lax.all_to_all(value, axis, 0, 0, tiled=True, axis_index_groups=groups)  13.8 us
    ppermute x5, starting transfers between devices, flip(): return lax.ppermute(value, 'dp', [(i, i ^ bits) for i in range(DP)])  12.2 us
    ppermute x3, starting transfers between devices, body(): lax.ppermute(send, 'section', [(i, i ^ 4 * k) for i in range(SECT)])  11.4 us
    ppermute x1, starting transfers between devices, scatter_sum(): lax.ppermute(keep, both, [(a, owner(a // DP, a % DP)) for a in range(SECT...  11.3 us
    ppermute x1, waiting for transfers between devices, scatter_sum(): lax.ppermute(send, both, [(a, owner(a // DP, a % DP ^ 16)) for a in range...  10.8 us
    pallas_call x1, Pallas kernels, body(): call(recur_kernel, 3, shape(8, BACK), [pltpu.VMEM((1024, GW), BF), pltpu....  10.4 us
  transfers between devices with their start and end apart: 21, of which 13 were waited for; matrix products, arithmetic and copies ran while one was open for 5% of the time, Pallas kernels for 3%

profile of v6, /device:TPU:35, one launch (start us, length us, event | category | flops | bytes accessed | tf_op | source)
XLA Modules:
  0.0 227.5 jit_solution(2242035526526815559)
XLA Ops:
  0.7 0.7 copy-done
  1.4 0.7 fusion.8
  2.1 0.7 pad_maximum_fusion.1
  2.8 7.5 %collective-permute-start = (bf16[128,128]{1,0:T(8,128)(2,1)S(1)}, bf16[128,128]{1,0:T(8,128)(2,1)S(1)}, u32[]{:S(2)}, u32[]{:S(2)}) collective-permute-start(bf16[128,128]{1,0:T(8,128)(2,1)S(1)} %pad_maximum_fusion.1), channel_id=1, source_target_pairs={{128,0},{129,1},{160,2},{161,3},{192,4},{193,5},{224,6},{225,7},{2... | collective-permute-start | bytes 98312 | tf_op jit(solution)/shard_map/ppermute | solution.py:330
  10.3 0.7 slice.83
  11.0 0.2 fusion.21
  11.2 0.5 slice.84
  12.4 0.8 fusion.24
  13.2 0.2 select_select_fusion
  13.4 3.9 %collective-permute-done = bf16[128,128]{1,0:T(8,128)(2,1)S(1)} collective-permute-done((bf16[128,128]{1,0:T(8,128)(2,1)S(1)}, bf16[128,128]{1,0:T(8,128)(2,1)S(1)}, u32[]{:S(2)}, u32[]{:S(2)}) %collective-permute-start) | collective-permute-done | bytes 32800 | tf_op jit(solution)/shard_map/ppermute | solution.py:330
  17.3 0.2 broadcast_in_dim.111
  17.6 1.3 pad_maximum_fusion
  18.9 10.5 %all-to-all-start = ((bf16[32,192,128]{2,1,0:T(8,128)(2,1)}), bf16[32,192,128]{2,1,0:T(8,128)(2,1)S(1)}, u32[]{:S(2)}, u32[]{:S(2)}) async-start(bf16[32,192,128]{2,1,0:T(8,128)(2,1)} %pad_maximum_fusion), calls=%async_computation | async-start | bytes 3145728 | tf_op jit(solution)/shard_map/all_to_all | solution.py:286
  29.4 0.6 fusion.20
  30.7 0.6 select_reduce_fusion
  31.4 0.7 stack.53.ints
  32.1 35.2 %all-to-all-done.w_ref = bf16[32,192,128]{2,1,0:T(8,128)(2,1)S(1)} async-done(((bf16[32,192,128]{2,1,0:T(8,128)(2,1)}), bf16[32,192,128]{2,1,0:T(8,128)(2,1)S(1)}, u32[]{:S(2)}, u32[]{:S(2)}) %all-to-all-start) | async-done | bytes 1572896 | tf_op jit(solution)/shard_map/all_to_all | solution.py:286
  67.3 1.1 shard_map.93
  68.4 4.0 %collective-permute-start.1 = (bf16[16,1152]{1,0:T(8,128)(2,1)S(1)}, bf16[16,1152]{1,0:T(8,128)(2,1)S(1)}, u32[]{:S(2)}, u32[]{:S(2)}) collective-permute-start(bf16[16,1152]{1,0:T(8,128)(2,1)S(1)} %get-tuple-element.23), channel_id=1, source_target_pairs={{0,32},{32,0},{64,96},{96,64},{128,160},{160,128},{192,224},{224,1... | collective-permute-start | bytes 110600 | tf_op jit(solution)/shard_map/ppermute | solution.py:359
  72.4 0.8 collective-permute-done.1
  73.2 0.7 broadcast_in_dim.129
  74.0 6.6 %all-to-all-start.1 = ((bf16[8,16,1152]{2,1,0:T(8,128)(2,1)}), bf16[8,16,1152]{2,1,0:T(8,128)(2,1)S(1)}, u32[]{:S(2)}, u32[]{:S(2)}) async-start(bf16[8,16,1152]{2,1,0:T(8,128)(2,1)} %broadcast_in_dim.129), calls=%async_computation.1 | async-start | bytes 589824 | tf_op jit(solution)/shard_map/all_to_all | solution.py:286
  80.6 2.4 %shard_map.94 = (bf16[32,3712]{1,0:T(8,128)(2,1)S(1)}, bf16[32,3712]{1,0:T(8,128)(2,1)S(1)}, bf16[32,3712]{1,0:T(8,128)(2,1)}, bf16[32,3712]{1,0:T(8,128)(2,1)}) custom-call(s32[6]{0:T(128)S(1)} %stack.53.ints, bf16[128,256]{1,0:T(8,128)(2,1)S(1)} %copy-done.1, bf16[32,256]{1,0:T(8,128)(2,1)S(1)} %get-tuple-element.24.pair_ref, ...), custom_call_target="tpu_custom_call" | custom-call | flops 300000000 | bytes 3000000 | tf_op jit(solution)/shard_map/pallas_call | solution.py:360
  83.0 3.0 %collective-permute-start.4 = (bf16[32,3712]{1,0:T(8,128)(2,1)}, bf16[32,3712]{1,0:T(8,128)(2,1)S(1)}, u32[]{:S(2)}, u32[]{:S(2)}) collective-permute-start(bf16[32,3712]{1,0:T(8,128)(2,1)} %get-tuple-element.30), channel_id=1, source_target_pairs={{0,96},{32,64},{64,32},{96,0},{128,224},{160,192},{192,160},{224,1... | collective-permute-start | bytes 712712 | tf_op jit(solution)/shard_map/ppermute | solution.py:374
  86.0 3.1 %collective-permute-start.3 = (bf16[32,3712]{1,0:T(8,128)(2,1)}, bf16[32,3712]{1,0:T(8,128)(2,1)S(1)}, u32[]{:S(2)}, u32[]{:S(2)}) collective-permute-start(bf16[32,3712]{1,0:T(8,128)(2,1)} %get-tuple-element.29), channel_id=1, source_target_pairs={{0,64},{32,96},{64,0},{96,32},{128,192},{160,224},{192,128},{224,1... | collective-permute-start | bytes 712712 | tf_op jit(solution)/shard_map/ppermute | solution.py:374
  89.1 1.9 collective-permute-start.2
  91.1 1.1 broadcast_in_dim.130
  92.2 5.5 %all-to-all-start.2 = ((bf16[32,16,1152]{2,1,0:T(8,128)(2,1)}), bf16[32,16,1152]{2,1,0:T(8,128)(2,1)S(1)}, u32[]{:S(2)}, u32[]{:S(2)}) async-start(bf16[32,16,1152]{2,1,0:T(8,128)(2,1)} %broadcast_in_dim.130), calls=%async_computation.2 | async-start | bytes 2359296 | tf_op jit(solution)/shard_map/all_to_all | solution.py:286
  97.8 1.1 collective-permute-done.3
  98.9 1.1 fusion
  100.0 3.4 %collective-permute-start.7 = (bf16[8,3712]{1,0:T(8,128)(2,1)S(1)}, bf16[8,3712]{1,0:T(8,128)(2,1)S(1)}, u32[]{:S(2)}, u32[]{:S(2)}) collective-permute-start(bf16[8,3712]{1,0:T(8,128)(2,1)S(1)} %get-tuple-element.53), channel_id=1, source_target_pairs={{0,384},{32,416},{64,448},{96,480},{128,256},{160,288},{192,320},{... | collective-permute-start | bytes 178184 | tf_op jit(solution)/shard_map/ppermute | solution.py:380
  103.3 3.9 %collective-permute-start.6 = (bf16[8,3712]{1,0:T(8,128)(2,1)S(1)}, bf16[8,3712]{1,0:T(8,128)(2,1)S(1)}, u32[]{:S(2)}, u32[]{:S(2)}) collective-permute-start(bf16[8,3712]{1,0:T(8,128)(2,1)S(1)} %get-tuple-element.54), channel_id=1, source_target_pairs={{0,256},{32,288},{64,320},{96,352},{128,384},{160,416},{192,448},{... | collective-permute-start | bytes 178184 | tf_op jit(solution)/shard_map/ppermute | solution.py:380
  107.2 4.2 %collective-permute-start.5 = (bf16[8,3712]{1,0:T(8,128)(2,1)S(1)}, bf16[8,3712]{1,0:T(8,128)(2,1)S(1)}, u32[]{:S(2)}, u32[]{:S(2)}) collective-permute-start(bf16[8,3712]{1,0:T(8,128)(2,1)S(1)} %get-tuple-element.52), channel_id=1, source_target_pairs={{0,128},{32,160},{64,192},{96,224},{128,0},{160,32},{192,64},{224,... | collective-permute-start | bytes 178184 | tf_op jit(solution)/shard_map/ppermute | solution.py:380
  111.4 1.1 collective-permute-done.6
  112.5 3.9 %collective-permute-done.5 = bf16[8,3712]{1,0:T(8,128)(2,1)S(1)} collective-permute-done((bf16[8,3712]{1,0:T(8,128)(2,1)S(1)}, bf16[8,3712]{1,0:T(8,128)(2,1)S(1)}, u32[]{:S(2)}, u32[]{:S(2)}) %collective-permute-start.5) | collective-permute-done | bytes 59424 | tf_op jit(solution)/shard_map/ppermute | solution.py:380
  116.4 10.7 %all-to-all-done.2.mine_ref = bf16[32,16,1152]{2,1,0:T(8,128)(2,1)S(1)} async-done(((bf16[32,16,1152]{2,1,0:T(8,128)(2,1)}), bf16[32,16,1152]{2,1,0:T(8,128)(2,1)S(1)}, u32[]{:S(2)}, u32[]{:S(2)}) %all-to-all-start.2) | async-done | bytes 1179680 | tf_op jit(solution)/shard_map/all_to_all | solution.py:286
  127.1 4.7 %collective-permute-start.8 = (bf16[32,16,1152]{2,1,0:T(8,128)(2,1)S(1)}, bf16[32,16,1152]{2,1,0:T(8,128)(2,1)S(1)}, u32[]{:S(2)}, u32[]{:S(2)}) collective-permute-start(bf16[32,16,1152]{2,1,0:T(8,128)(2,1)S(1)} %all-to-all-done.2.mine_ref), channel_id=1, source_target_pairs={{0,32},{32,0},{64,96},{96,64},{128,160},{160,128},{192,224},{224,1... | collective-permute-start | bytes 3538952 | tf_op jit(solution)/shard_map/ppermute | solution.py:382
  131.8 2.5 %collective-permute-done.8.other_ref = bf16[32,16,1152]{2,1,0:T(8,128)(2,1)S(1)} collective-permute-done((bf16[32,16,1152]{2,1,0:T(8,128)(2,1)S(1)}, bf16[32,16,1152]{2,1,0:T(8,128)(2,1)S(1)}, u32[]{:S(2)}, u32[]{:S(2)}) %collective-permute-start.8) | collective-permute-done | bytes 1179680 | tf_op jit(solution)/shard_map/ppermute | solution.py:382
  134.2 10.4 %shard_map.95 = bf16[8,2432]{1,0:T(8,128)(2,1)S(1)} custom-call(s32[1]{0:T(128)} %bitcast.ints, f32[8,3712]{1,0:T(8,128)S(1)} %fusion.4.sum_ref, bf16[32,16,1152]{2,1,0:T(8,128)(2,1)S(1)} %all-to-all-done.2.mine_ref, bf16[32,16,1152]{2,1,0:T(8,128)(2,1)S(1)} %collective-permute-done.8.other_ref), custom_call_target="tpu_custom_call" | custom-call | flops 200000000 | bytes 3000000 | tf_op jit(solution)/shard_map/pallas_call | solution.py:384
  144.6 13.8 %all_to_all.25 = bf16[8,8,2432]{2,1,0:T(8,128)(2,1)S(1)} all-to-all(bf16[8,8,2432]{2,1,0:T(8,128)(2,1)S(1)} %broadcast_in_dim.131), channel_id=1, replica_groups={{0,128,256,384,64,192,320,448},{32,160,288,416,96,224,352,480},{1,129,2..., dimensions={0} | all-to-all | bytes 622592 | tf_op jit(solution)/shard_map/all_to_all | solution.py:286
  158.4 3.3 %collective-permute-start.9 = (bf16[64,2432]{1,0:T(8,128)(2,1)S(1)}, bf16[64,2432]{1,0:T(8,128)(2,1)S(1)}, u32[]{:S(2)}, u32[]{:S(2)}) collective-permute-start(bf16[64,2432]{1,0:T(8,128)(2,1)S(1)} %bitcast.84), channel_id=1, source_target_pairs={{0,32},{32,0},{64,96},{96,64},{128,160},{160,128},{192,224},{224,1... | collective-permute-start | bytes 933896 | tf_op jit(solution)/shard_map/ppermute | solution.py:402
  163.1 1.9 shard_map.96
  165.1 1.9 collective-permute-start.10
  167.2 2.1 shard_map.97
  169.4 8.7 %all-to-all-start.4 = ((bf16[16,160,256]{2,1,0:T(8,128)(2,1)}), bf16[16,160,256]{2,1,0:T(8,128)(2,1)S(1)}, u32[]{:S(2)}, u32[]{:S(2)}) async-start(bf16[16,160,256]{2,1,0:T(8,128)(2,1)} %shard_map.97), calls=%async_computation.4 | async-start | bytes 2621440 | tf_op jit(solution)/shard_map/all_to_all | solution.py:286
  178.1 2.3 %collective-permute-done.10 = bf16[2,8,128,128]{3,2,1,0:T(8,128)(2,1)} collective-permute-done((bf16[2,8,128,128]{3,2,1,0:T(8,128)(2,1)S(1)}, bf16[2,8,128,128]{3,2,1,0:T(8,128)(2,1)}, u32[]{:S(2)}, u32[]{:S(2)}) %collective-permute-start.10) | collective-permute-done | bytes 524320 | tf_op jit(solution)/shard_map/ppermute | solution.py:290
  180.4 1.2 convert_add_fusion
  181.6 3.1 %collective-permute-start.13 = (bf16[4,128,128]{2,1,0:T(8,128)(2,1)S(1)}, bf16[4,128,128]{2,1,0:T(8,128)(2,1)S(1)}, u32[]{:S(2)}, u32[]{:S(2)}) collective-permute-start(bf16[4,128,128]{2,1,0:T(8,128)(2,1)S(1)} %get-tuple-element.51), channel_id=1, source_target_pairs={{0,7},{1,6},{2,5},{3,4},{4,3},{5,2},{6,1},{7,0},{8,15},{9,14},{10,... | collective-permute-start | bytes 393224 | tf_op jit(solution)/shard_map/ppermute | solution.py:290
  184.7 3.1 %collective-permute-start.12 = (bf16[4,128,128]{2,1,0:T(8,128)(2,1)S(1)}, bf16[4,128,128]{2,1,0:T(8,128)(2,1)S(1)}, u32[]{:S(2)}, u32[]{:S(2)}) collective-permute-start(bf16[4,128,128]{2,1,0:T(8,128)(2,1)S(1)} %fusion.1), channel_id=1, source_target_pairs={{0,4},{1,5},{2,6},{3,7},{4,0},{5,1},{6,2},{7,3},{8,12},{9,13},{10,... | collective-permute-start | bytes 393224 | tf_op jit(solution)/shard_map/ppermute | solution.py:290
  187.8 2.2 collective-permute-start.11
  190.0 0.4 copy.20
  190.5 1.1 collective-permute-done.12
  191.6 2.3 collective-permute-done.11
  193.9 0.1 concatenate.45
  194.1 1.9 collective-permute-start.14
  196.0 0.7 fusion.17
  196.8 0.1 concatenate.44
  196.8 4.1 %collective-permute-done.14 = bf16[2,128,128]{2,1,0:T(8,128)(2,1)S(1)} collective-permute-done((bf16[2,128,128]{2,1,0:T(8,128)(2,1)S(1)}, bf16[2,128,128]{2,1,0:T(8,128)(2,1)S(1)}, u32[]{:S(2)}, u32[]{:S(2)}) %collective-permute-start.14) | collective-permute-done | bytes 65568 | tf_op jit(solution)/shard_map/ppermute | solution.py:290
  201.0 11.3 %collective-permute-start.15 = (bf16[128,128]{1,0:T(8,128)(2,1)S(1)}, bf16[128,128]{1,0:T(8,128)(2,1)S(1)}, u32[]{:S(2)}, u32[]{:S(2)}) collective-permute-start(bf16[128,128]{1,0:T(8,128)(2,1)S(1)} %get-tuple-element.58), channel_id=1, source_target_pairs={{0,128},{1,129},{2,160},{3,161},{4,192},{5,193},{6,224},{7,225},{8... | collective-permute-start | bytes 98312 | tf_op jit(solution)/shard_map/ppermute | solution.py:311
  212.3 1.9 collective-permute-start.16
  214.3 0.6 broadcast_select_fusion
  214.9 1.2 shard_map.98
  216.1 10.8 %collective-permute-done.16 = bf16[128,128]{1,0:T(8,128)(2,1)S(1)} collective-permute-done((bf16[128,128]{1,0:T(8,128)(2,1)S(1)}, bf16[128,128]{1,0:T(8,128)(2,1)S(1)}, u32[]{:S(2)}, u32[]{:S(2)}) %collective-permute-start.16) | collective-permute-done | bytes 32800 | tf_op jit(solution)/shard_map/ppermute | solution.py:312
  226.9 0.6 slice_bitcast_fusion
  (44 shorter events, 0.9 us)
Async XLA Ops:
  0.6 0.7 copy-start
  2.8 14.5 %collective-permute-start = (bf16[128,128]{1,0:T(8,128)(2,1)S(1)}, bf16[128,128]{1,0:T(8,128)(2,1)S(1)}, u32[]{:S(2)}, u32[]{:S(2)}) collective-permute-start(bf16[128,128]{1,0:T(8,128)(2,1)S(1)} %pad_maximum_fusion.1), channel_id=1, source_target_pairs={{128,0},{129,1},{160,2},{161,3},{192,4},{193,5},{224,6},{225,7},{2... | collective-permute-start | bytes 98312 | tf_op jit(solution)/shard_map/ppermute | solution.py:330
  18.9 48.5 %all-to-all-start = ((bf16[32,192,128]{2,1,0:T(8,128)(2,1)}), bf16[32,192,128]{2,1,0:T(8,128)(2,1)S(1)}, u32[]{:S(2)}, u32[]{:S(2)}) async-start(bf16[32,192,128]{2,1,0:T(8,128)(2,1)} %pad_maximum_fusion), calls=%async_computation | async-start | bytes 3145728 | tf_op jit(solution)/shard_map/all_to_all | solution.py:286
  29.4 51.3 %copy-start.1 = (bf16[128,256]{1,0:T(8,128)(2,1)S(1)}, bf16[128,256]{1,0:T(8,128)(2,1)}, u32[]{:S(2)}) copy-start(bf16[128,256]{1,0:T(8,128)(2,1)} %x_ref.5) | copy-start | bytes 196612
  29.4 51.2 %copy-start.2 = (bf16[128,256]{1,0:T(8,128)(2,1)S(1)}, bf16[128,256]{1,0:T(8,128)(2,1)}, u32[]{:S(2)}) copy-start(bf16[128,256]{1,0:T(8,128)(2,1)} %g_ref.3) | copy-start | bytes 196612
  68.4 4.8 %collective-permute-start.1 = (bf16[16,1152]{1,0:T(8,128)(2,1)S(1)}, bf16[16,1152]{1,0:T(8,128)(2,1)S(1)}, u32[]{:S(2)}, u32[]{:S(2)}) collective-permute-start(bf16[16,1152]{1,0:T(8,128)(2,1)S(1)} %get-tuple-element.23), channel_id=1, source_target_pairs={{0,32},{32,0},{64,96},{96,64},{128,160},{160,128},{192,224},{224,1... | collective-permute-start | bytes 110600 | tf_op jit(solution)/shard_map/ppermute | solution.py:359
  74.0 17.1 %all-to-all-start.1 = ((bf16[8,16,1152]{2,1,0:T(8,128)(2,1)}), bf16[8,16,1152]{2,1,0:T(8,128)(2,1)S(1)}, u32[]{:S(2)}, u32[]{:S(2)}) async-start(bf16[8,16,1152]{2,1,0:T(8,128)(2,1)} %broadcast_in_dim.129), calls=%async_computation.1 | async-start | bytes 589824 | tf_op jit(solution)/shard_map/all_to_all | solution.py:286
  83.0 14.7 %collective-permute-start.4 = (bf16[32,3712]{1,0:T(8,128)(2,1)}, bf16[32,3712]{1,0:T(8,128)(2,1)S(1)}, u32[]{:S(2)}, u32[]{:S(2)}) collective-permute-start(bf16[32,3712]{1,0:T(8,128)(2,1)} %get-tuple-element.30), channel_id=1, source_target_pairs={{0,96},{32,64},{64,32},{96,0},{128,224},{160,192},{192,160},{224,1... | collective-permute-start | bytes 712712 | tf_op jit(solution)/shard_map/ppermute | solution.py:374
  86.0 12.9 %collective-permute-start.3 = (bf16[32,3712]{1,0:T(8,128)(2,1)}, bf16[32,3712]{1,0:T(8,128)(2,1)S(1)}, u32[]{:S(2)}, u32[]{:S(2)}) collective-permute-start(bf16[32,3712]{1,0:T(8,128)(2,1)} %get-tuple-element.29), channel_id=1, source_target_pairs={{0,64},{32,96},{64,0},{96,32},{128,192},{160,224},{192,128},{224,1... | collective-permute-start | bytes 712712 | tf_op jit(solution)/shard_map/ppermute | solution.py:374
  89.1 9.8 %collective-permute-start.2 = (bf16[32,3712]{1,0:T(8,128)(2,1)S(1)}, bf16[32,3712]{1,0:T(8,128)(2,1)}, u32[]{:S(2)}, u32[]{:S(2)}) collective-permute-start(bf16[32,3712]{1,0:T(8,128)(2,1)S(1)} %get-tuple-element.28), channel_id=1, source_target_pairs={{0,32},{32,0},{64,96},{96,64},{128,160},{160,128},{192,224},{224,1... | collective-permute-start | bytes 712712 | tf_op jit(solution)/shard_map/ppermute | solution.py:374
  92.2 34.9 %all-to-all-start.2 = ((bf16[32,16,1152]{2,1,0:T(8,128)(2,1)}), bf16[32,16,1152]{2,1,0:T(8,128)(2,1)S(1)}, u32[]{:S(2)}, u32[]{:S(2)}) async-start(bf16[32,16,1152]{2,1,0:T(8,128)(2,1)} %broadcast_in_dim.130), calls=%async_computation.2 | async-start | bytes 2359296 | tf_op jit(solution)/shard_map/all_to_all | solution.py:286
  100.0 11.4 %collective-permute-start.7 = (bf16[8,3712]{1,0:T(8,128)(2,1)S(1)}, bf16[8,3712]{1,0:T(8,128)(2,1)S(1)}, u32[]{:S(2)}, u32[]{:S(2)}) collective-permute-start(bf16[8,3712]{1,0:T(8,128)(2,1)S(1)} %get-tuple-element.53), channel_id=1, source_target_pairs={{0,384},{32,416},{64,448},{96,480},{128,256},{160,288},{192,320},{... | collective-permute-start | bytes 178184 | tf_op jit(solution)/shard_map/ppermute | solution.py:380
  103.3 9.1 %collective-permute-start.6 = (bf16[8,3712]{1,0:T(8,128)(2,1)S(1)}, bf16[8,3712]{1,0:T(8,128)(2,1)S(1)}, u32[]{:S(2)}, u32[]{:S(2)}) collective-permute-start(bf16[8,3712]{1,0:T(8,128)(2,1)S(1)} %get-tuple-element.54), channel_id=1, source_target_pairs={{0,256},{32,288},{64,320},{96,352},{128,384},{160,416},{192,448},{... | collective-permute-start | bytes 178184 | tf_op jit(solution)/shard_map/ppermute | solution.py:380
  107.2 9.2 %collective-permute-start.5 = (bf16[8,3712]{1,0:T(8,128)(2,1)S(1)}, bf16[8,3712]{1,0:T(8,128)(2,1)S(1)}, u32[]{:S(2)}, u32[]{:S(2)}) collective-permute-start(bf16[8,3712]{1,0:T(8,128)(2,1)S(1)} %get-tuple-element.52), channel_id=1, source_target_pairs={{0,128},{32,160},{64,192},{96,224},{128,0},{160,32},{192,64},{224,... | collective-permute-start | bytes 178184 | tf_op jit(solution)/shard_map/ppermute | solution.py:380
  127.1 7.1 %collective-permute-start.8 = (bf16[32,16,1152]{2,1,0:T(8,128)(2,1)S(1)}, bf16[32,16,1152]{2,1,0:T(8,128)(2,1)S(1)}, u32[]{:S(2)}, u32[]{:S(2)}) collective-permute-start(bf16[32,16,1152]{2,1,0:T(8,128)(2,1)S(1)} %all-to-all-done.2.mine_ref), channel_id=1, source_target_pairs={{0,32},{32,0},{64,96},{96,64},{128,160},{160,128},{192,224},{224,1... | collective-permute-start | bytes 3538952 | tf_op jit(solution)/shard_map/ppermute | solution.py:382
  158.4 4.7 %collective-permute-start.9 = (bf16[64,2432]{1,0:T(8,128)(2,1)S(1)}, bf16[64,2432]{1,0:T(8,128)(2,1)S(1)}, u32[]{:S(2)}, u32[]{:S(2)}) collective-permute-start(bf16[64,2432]{1,0:T(8,128)(2,1)S(1)} %bitcast.84), channel_id=1, source_target_pairs={{0,32},{32,0},{64,96},{96,64},{128,160},{160,128},{192,224},{224,1... | collective-permute-start | bytes 933896 | tf_op jit(solution)/shard_map/ppermute | solution.py:402
  165.1 15.3 %collective-permute-start.10 = (bf16[2,8,128,128]{3,2,1,0:T(8,128)(2,1)S(1)}, bf16[2,8,128,128]{3,2,1,0:T(8,128)(2,1)}, u32[]{:S(2)}, u32[]{:S(2)}) collective-permute-start(bf16[2,8,128,128]{3,2,1,0:T(8,128)(2,1)S(1)} %get-tuple-element.34), channel_id=1, source_target_pairs={{0,1},{1,0},{2,3},{3,2},{4,5},{5,4},{6,7},{7,6},{8,9},{9,8},{10,11... | collective-permute-start | bytes 1572872 | tf_op jit(solution)/shard_map/ppermute | solution.py:290
  169.4 45.5 %all-to-all-start.4 = ((bf16[16,160,256]{2,1,0:T(8,128)(2,1)}), bf16[16,160,256]{2,1,0:T(8,128)(2,1)S(1)}, u32[]{:S(2)}, u32[]{:S(2)}) async-start(bf16[16,160,256]{2,1,0:T(8,128)(2,1)} %shard_map.97), calls=%async_computation.4 | async-start | bytes 2621440 | tf_op jit(solution)/shard_map/all_to_all | solution.py:286
  181.6 8.9 %collective-permute-start.13 = (bf16[4,128,128]{2,1,0:T(8,128)(2,1)S(1)}, bf16[4,128,128]{2,1,0:T(8,128)(2,1)S(1)}, u32[]{:S(2)}, u32[]{:S(2)}) collective-permute-start(bf16[4,128,128]{2,1,0:T(8,128)(2,1)S(1)} %get-tuple-element.51), channel_id=1, source_target_pairs={{0,7},{1,6},{2,5},{3,4},{4,3},{5,2},{6,1},{7,0},{8,15},{9,14},{10,... | collective-permute-start | bytes 393224 | tf_op jit(solution)/shard_map/ppermute | solution.py:290
  184.7 6.8 %collective-permute-start.12 = (bf16[4,128,128]{2,1,0:T(8,128)(2,1)S(1)}, bf16[4,128,128]{2,1,0:T(8,128)(2,1)S(1)}, u32[]{:S(2)}, u32[]{:S(2)}) collective-permute-start(bf16[4,128,128]{2,1,0:T(8,128)(2,1)S(1)} %fusion.1), channel_id=1, source_target_pairs={{0,4},{1,5},{2,6},{3,7},{4,0},{5,1},{6,2},{7,3},{8,12},{9,13},{10,... | collective-permute-start | bytes 393224 | tf_op jit(solution)/shard_map/ppermute | solution.py:290
  187.8 6.0 %collective-permute-start.11 = (bf16[4,128,128]{2,1,0:T(8,128)(2,1)S(1)}, bf16[4,128,128]{2,1,0:T(8,128)(2,1)S(1)}, u32[]{:S(2)}, u32[]{:S(2)}) collective-permute-start(bf16[4,128,128]{2,1,0:T(8,128)(2,1)S(1)} %get-tuple-element.50), channel_id=1, source_target_pairs={{0,3},{1,2},{2,1},{3,0},{4,7},{5,6},{6,5},{7,4},{8,11},{9,10},{10,... | collective-permute-start | bytes 393224 | tf_op jit(solution)/shard_map/ppermute | solution.py:290
  194.1 6.9 %collective-permute-start.14 = (bf16[2,128,128]{2,1,0:T(8,128)(2,1)S(1)}, bf16[2,128,128]{2,1,0:T(8,128)(2,1)S(1)}, u32[]{:S(2)}, u32[]{:S(2)}) collective-permute-start(bf16[2,128,128]{2,1,0:T(8,128)(2,1)S(1)} %fusion.6), channel_id=1, source_target_pairs={{0,8},{1,9},{2,10},{3,11},{4,12},{5,13},{6,14},{7,15},{8,0},{9,1},... | collective-permute-start | bytes 196616 | tf_op jit(solution)/shard_map/ppermute | solution.py:290
  201.0 15.1 %collective-permute-start.15 = (bf16[128,128]{1,0:T(8,128)(2,1)S(1)}, bf16[128,128]{1,0:T(8,128)(2,1)S(1)}, u32[]{:S(2)}, u32[]{:S(2)}) collective-permute-start(bf16[128,128]{1,0:T(8,128)(2,1)S(1)} %get-tuple-element.58), channel_id=1, source_target_pairs={{0,128},{1,129},{2,160},{3,161},{4,192},{5,193},{6,224},{7,225},{8... | collective-permute-start | bytes 98312 | tf_op jit(solution)/shard_map/ppermute | solution.py:311
  212.3 14.6 %collective-permute-start.16 = (bf16[128,128]{1,0:T(8,128)(2,1)S(1)}, bf16[128,128]{1,0:T(8,128)(2,1)S(1)}, u32[]{:S(2)}, u32[]{:S(2)}) collective-permute-start(bf16[128,128]{1,0:T(8,128)(2,1)S(1)} %get-tuple-element.57), channel_id=1, source_target_pairs={{0,384},{1,385},{2,416},{3,417},{4,448},{5,449},{6,480},{7,481},{8... | collective-permute-start | bytes 98312 | tf_op jit(solution)/shard_map/ppermute | solution.py:312

commit v7 on v6

--- a/solution.py
+++ b/solution.py
@@ -290,7 +290,7 @@
     return lax.ppermute(value, "dp", [(i, i ^ bits) for i in range(DP)])
 
 
-def scatter_sum(keep, send, me, later):
+def scatter_sum(keep, send, me, later, finish):
     first = flip(send, 1)
     low = (me >> 2) & 1
     arrived = 0.0
@@ -301,10 +301,12 @@
     own = (keep[0].astype(F32) + first[0].astype(F32)).reshape(4, 2, 128, 128)
     value = lax.dynamic_index_in_dim(own, low, 1, keepdims=False) + arrived
     value, later = lax.optimization_barrier((value, later))
+    later = finish(later)
     middle = (me >> 3) & 1
     value = value.reshape(2, 2, 128, 128)
     send = lax.dynamic_index_in_dim(value, 1 - middle, 1, keepdims=False).astype(BF)
     value = (lax.dynamic_index_in_dim(value, middle, 1, keepdims=False) + flip(send, 8).astype(F32)).astype(BF)
+    value, later = lax.optimization_barrier((value, later))
     keep = lax.dynamic_index_in_dim(value, me >> 4, 0, keepdims=False)
     send = lax.dynamic_index_in_dim(value, 1 - (me >> 4), 0, keepdims=False)
     both = ("section", "dp")
@@ -431,23 +433,24 @@
         3 * 10**6,
     )(jnp.stack([own_at, pair_at, alive.astype(jnp.int32), core]).astype(jnp.int32), x, pair, back, back_other, extra_h, wc)
     saved = exchange(rows_out, "section")
-    misc = small[:, :, 256:384]
-    mine_sum, other_sum, misc = scatter_sum(*blocks, me, misc)
+    def slot_rstd(misc):
+        misc = misc.astype(F32)
+        own_inv = misc[:, :, 16:32] + misc[:, :, 32:48]
+        pair_inv = misc[:, 0:2, 48:64] + misc[:, 0:2, 64:80]
+        own_inv = lax.dynamic_index_in_dim(own_inv, sec, 2, keepdims=False).reshape(ROWS)
+        pair_inv = lax.dynamic_index_in_dim(pair_inv, sec, 2, keepdims=False).T.reshape(PAIR)
+        own_inv = jnp.where(alive, own_inv, 0.0)
+        pair_inv = jnp.where(taking, pair_inv, 0.0)
+        return jnp.where(
+            pair_first, jnp.concatenate([pair_inv, own_inv]), jnp.concatenate([own_inv, pair_inv])
+        ).reshape(1, 1, ROWS + PAIR)
+
+    mine_sum, other_sum, rstd = scatter_sum(*blocks, me, small[:, :, 256:384], slot_rstd)
     saved = call(join_kernel, 1, shape(1, 1, ROWS + PAIR, D), [], 0, 3 * 10**6, False)(saved)
 
     saved, mine_sum, other_sum = lax.optimization_barrier((saved, mine_sum, other_sum))
     grads = mine_sum.astype(F32) + other_sum.astype(F32)
 
-    misc = misc.astype(F32)
-    own_inv = misc[:, :, 16:32] + misc[:, :, 32:48]
-    pair_inv = misc[:, 0:2, 48:64] + misc[:, 0:2, 64:80]
-    own_inv = lax.dynamic_index_in_dim(own_inv, sec, 2, keepdims=False).reshape(ROWS)
-    pair_inv = lax.dynamic_index_in_dim(pair_inv, sec, 2, keepdims=False).T.reshape(PAIR)
-    own_inv = jnp.where(alive, own_inv, 0.0)
-    pair_inv = jnp.where(taking, pair_inv, 0.0)
-    rstd = jnp.where(
-        pair_first, jnp.concatenate([pair_inv, own_inv]), jnp.concatenate([own_inv, pair_inv])
-    ).reshape(1, 1, ROWS + PAIR)
     return rstd, saved, (grads[64:128] * gain_here)[None], grads[0:64][None]
 
 

time: 229 us -> 229 us (level)
  no operation moved by 1% of the time
where the time goes in v7:
time: 229 us; the launch traced here: 227 us
  starting transfers between devices  95.6 us (42%)
  waiting for transfers between devices  79.6 us (35%)
  Pallas kernels  19.1 us (8%)
  blocking collectives  13.8 us (6%)
  other arithmetic  8.83 us (4%)
  local copies, waits for them, and re-layouts  6.65 us (3%)
  between operations  3.79 us (2%)
    all_to_all x4, waiting for transfers between devices, exchange(): lax.all_to_all(value, axis, 0, 0, tiled=True, axis_index_groups=groups)  45.9 us
    all_to_all x4, starting transfers between devices, exchange(): lax.all_to_all(value, axis, 0, 0, tiled=True, axis_index_groups=groups)  31.4 us
    all_to_all x1, blocking collectives, exchange(): lax.all_to_all(value, axis, 0, 0, tiled=True, axis_index_groups=groups)  13.8 us
    ppermute x5, starting transfers between devices, flip(): return lax.ppermute(value, 'dp', [(i, i ^ bits) for i in range(DP)])  12.2 us
    ppermute x1, waiting for transfers between devices, scatter_sum(): lax.ppermute(send, both, [(a, owner(a // DP, a % DP ^ 16)) for a in range...  11.4 us
    ppermute x3, starting transfers between devices, body(): lax.ppermute(send, 'section', [(i, i ^ 4 * k) for i in range(SECT)])  11.4 us
    ppermute x1, starting transfers between devices, scatter_sum(): lax.ppermute(keep, both, [(a, owner(a // DP, a % DP)) for a in range(SECT...  11.3 us
    pallas_call x1, Pallas kernels, body(): call(recur_kernel, 3, shape(8, BACK), [pltpu.VMEM((1024, GW), BF), pltpu....  10.4 us
  transfers between devices with their start and end apart: 21, of which 13 were waited for; matrix products, arithmetic and copies ran while one was open for 5% of the time, Pallas kernels for 3%

profile of v7, /device:TPU:35, one launch (start us, length us, event | category | flops | bytes accessed | tf_op | source)
XLA Modules:
  0.0 227.4 jit_solution(5958442961545409069)
XLA Ops:
  0.7 0.7 copy-done
  1.4 0.7 fusion.8
  2.1 0.7 pad_maximum_fusion.1
  2.8 7.5 %collective-permute-start = (bf16[128,128]{1,0:T(8,128)(2,1)S(1)}, bf16[128,128]{1,0:T(8,128)(2,1)S(1)}, u32[]{:S(2)}, u32[]{:S(2)}) collective-permute-start(bf16[128,128]{1,0:T(8,128)(2,1)S(1)} %pad_maximum_fusion.1), channel_id=1, source_target_pairs={{128,0},{129,1},{160,2},{161,3},{192,4},{193,5},{224,6},{225,7},{2... | collective-permute-start | bytes 98312 | tf_op jit(solution)/shard_map/ppermute | solution.py:332
  10.3 0.7 slice.83
  11.0 0.2 fusion.21
  11.2 0.5 slice.84
  12.4 0.8 fusion.24
  13.2 0.2 select_select_fusion
  13.4 3.9 %collective-permute-done = bf16[128,128]{1,0:T(8,128)(2,1)S(1)} collective-permute-done((bf16[128,128]{1,0:T(8,128)(2,1)S(1)}, bf16[128,128]{1,0:T(8,128)(2,1)S(1)}, u32[]{:S(2)}, u32[]{:S(2)}) %collective-permute-start) | collective-permute-done | bytes 32800 | tf_op jit(solution)/shard_map/ppermute | solution.py:332
  17.3 0.2 broadcast_in_dim.111
  17.6 1.3 pad_maximum_fusion
  18.9 10.5 %all-to-all-start = ((bf16[32,192,128]{2,1,0:T(8,128)(2,1)}), bf16[32,192,128]{2,1,0:T(8,128)(2,1)S(1)}, u32[]{:S(2)}, u32[]{:S(2)}) async-start(bf16[32,192,128]{2,1,0:T(8,128)(2,1)} %pad_maximum_fusion), calls=%async_computation | async-start | bytes 3145728 | tf_op jit(solution)/shard_map/all_to_all | solution.py:286
  29.4 0.6 fusion.20
  30.7 0.6 select_reduce_fusion
  31.4 0.7 stack.53.ints
  32.1 35.2 %all-to-all-done.w_ref = bf16[32,192,128]{2,1,0:T(8,128)(2,1)S(1)} async-done(((bf16[32,192,128]{2,1,0:T(8,128)(2,1)}), bf16[32,192,128]{2,1,0:T(8,128)(2,1)S(1)}, u32[]{:S(2)}, u32[]{:S(2)}) %all-to-all-start) | async-done | bytes 1572896 | tf_op jit(solution)/shard_map/all_to_all | solution.py:286
  67.3 1.1 shard_map.93
  68.4 4.0 %collective-permute-start.1 = (bf16[16,1152]{1,0:T(8,128)(2,1)S(1)}, bf16[16,1152]{1,0:T(8,128)(2,1)S(1)}, u32[]{:S(2)}, u32[]{:S(2)}) collective-permute-start(bf16[16,1152]{1,0:T(8,128)(2,1)S(1)} %get-tuple-element.25), channel_id=1, source_target_pairs={{0,32},{32,0},{64,96},{96,64},{128,160},{160,128},{192,224},{224,1... | collective-permute-start | bytes 110600 | tf_op jit(solution)/shard_map/ppermute | solution.py:361
  72.4 0.8 collective-permute-done.1
  73.2 0.7 broadcast_in_dim.129
  74.0 6.6 %all-to-all-start.1 = ((bf16[8,16,1152]{2,1,0:T(8,128)(2,1)}), bf16[8,16,1152]{2,1,0:T(8,128)(2,1)S(1)}, u32[]{:S(2)}, u32[]{:S(2)}) async-start(bf16[8,16,1152]{2,1,0:T(8,128)(2,1)} %broadcast_in_dim.129), calls=%async_computation.1 | async-start | bytes 589824 | tf_op jit(solution)/shard_map/all_to_all | solution.py:286
  80.6 2.4 %shard_map.94 = (bf16[32,3712]{1,0:T(8,128)(2,1)S(1)}, bf16[32,3712]{1,0:T(8,128)(2,1)S(1)}, bf16[32,3712]{1,0:T(8,128)(2,1)}, bf16[32,3712]{1,0:T(8,128)(2,1)}) custom-call(s32[6]{0:T(128)S(1)} %stack.53.ints, bf16[128,256]{1,0:T(8,128)(2,1)S(1)} %copy-done.1, bf16[32,256]{1,0:T(8,128)(2,1)S(1)} %get-tuple-element.26.pair_ref, ...), custom_call_target="tpu_custom_call" | custom-call | flops 300000000 | bytes 3000000 | tf_op jit(solution)/shard_map/pallas_call | solution.py:362
  83.0 3.0 %collective-permute-start.4 = (bf16[32,3712]{1,0:T(8,128)(2,1)}, bf16[32,3712]{1,0:T(8,128)(2,1)S(1)}, u32[]{:S(2)}, u32[]{:S(2)}) collective-permute-start(bf16[32,3712]{1,0:T(8,128)(2,1)} %get-tuple-element.32), channel_id=1, source_target_pairs={{0,96},{32,64},{64,32},{96,0},{128,224},{160,192},{192,160},{224,1... | collective-permute-start | bytes 712712 | tf_op jit(solution)/shard_map/ppermute | solution.py:376
  86.0 3.1 %collective-permute-start.3 = (bf16[32,3712]{1,0:T(8,128)(2,1)}, bf16[32,3712]{1,0:T(8,128)(2,1)S(1)}, u32[]{:S(2)}, u32[]{:S(2)}) collective-permute-start(bf16[32,3712]{1,0:T(8,128)(2,1)} %get-tuple-element.31), channel_id=1, source_target_pairs={{0,64},{32,96},{64,0},{96,32},{128,192},{160,224},{192,128},{224,1... | collective-permute-start | bytes 712712 | tf_op jit(solution)/shard_map/ppermute | solution.py:376
  89.1 1.9 collective-permute-start.2
  91.1 1.1 broadcast_in_dim.130
  92.2 5.5 %all-to-all-start.2 = ((bf16[32,16,1152]{2,1,0:T(8,128)(2,1)}), bf16[32,16,1152]{2,1,0:T(8,128)(2,1)S(1)}, u32[]{:S(2)}, u32[]{:S(2)}) async-start(bf16[32,16,1152]{2,1,0:T(8,128)(2,1)} %broadcast_in_dim.130), calls=%async_computation.2 | async-start | bytes 2359296 | tf_op jit(solution)/shard_map/all_to_all | solution.py:286
  97.8 1.1 collective-permute-done.3
  98.9 1.1 fusion
  100.0 3.4 %collective-permute-start.7 = (bf16[8,3712]{1,0:T(8,128)(2,1)S(1)}, bf16[8,3712]{1,0:T(8,128)(2,1)S(1)}, u32[]{:S(2)}, u32[]{:S(2)}) collective-permute-start(bf16[8,3712]{1,0:T(8,128)(2,1)S(1)} %get-tuple-element.57), channel_id=1, source_target_pairs={{0,384},{32,416},{64,448},{96,480},{128,256},{160,288},{192,320},{... | collective-permute-start | bytes 178184 | tf_op jit(solution)/shard_map/ppermute | solution.py:382
  103.3 3.9 %collective-permute-start.6 = (bf16[8,3712]{1,0:T(8,128)(2,1)S(1)}, bf16[8,3712]{1,0:T(8,128)(2,1)S(1)}, u32[]{:S(2)}, u32[]{:S(2)}) collective-permute-start(bf16[8,3712]{1,0:T(8,128)(2,1)S(1)} %get-tuple-element.58), channel_id=1, source_target_pairs={{0,256},{32,288},{64,320},{96,352},{128,384},{160,416},{192,448},{... | collective-permute-start | bytes 178184 | tf_op jit(solution)/shard_map/ppermute | solution.py:382
  107.2 4.2 %collective-permute-start.5 = (bf16[8,3712]{1,0:T(8,128)(2,1)S(1)}, bf16[8,3712]{1,0:T(8,128)(2,1)S(1)}, u32[]{:S(2)}, u32[]{:S(2)}) collective-permute-start(bf16[8,3712]{1,0:T(8,128)(2,1)S(1)} %get-tuple-element.56), channel_id=1, source_target_pairs={{0,128},{32,160},{64,192},{96,224},{128,0},{160,32},{192,64},{224,... | collective-permute-start | bytes 178184 | tf_op jit(solution)/shard_map/ppermute | solution.py:382
  111.4 1.1 collective-permute-done.6
  112.5 3.9 %collective-permute-done.5 = bf16[8,3712]{1,0:T(8,128)(2,1)S(1)} collective-permute-done((bf16[8,3712]{1,0:T(8,128)(2,1)S(1)}, bf16[8,3712]{1,0:T(8,128)(2,1)S(1)}, u32[]{:S(2)}, u32[]{:S(2)}) %collective-permute-start.5) | collective-permute-done | bytes 59424 | tf_op jit(solution)/shard_map/ppermute | solution.py:382
  116.4 10.7 %all-to-all-done.2.mine_ref = bf16[32,16,1152]{2,1,0:T(8,128)(2,1)S(1)} async-done(((bf16[32,16,1152]{2,1,0:T(8,128)(2,1)}), bf16[32,16,1152]{2,1,0:T(8,128)(2,1)S(1)}, u32[]{:S(2)}, u32[]{:S(2)}) %all-to-all-start.2) | async-done | bytes 1179680 | tf_op jit(solution)/shard_map/all_to_all | solution.py:286
  127.1 4.7 %collective-permute-start.8 = (bf16[32,16,1152]{2,1,0:T(8,128)(2,1)S(1)}, bf16[32,16,1152]{2,1,0:T(8,128)(2,1)S(1)}, u32[]{:S(2)}, u32[]{:S(2)}) collective-permute-start(bf16[32,16,1152]{2,1,0:T(8,128)(2,1)S(1)} %all-to-all-done.2.mine_ref), channel_id=1, source_target_pairs={{0,32},{32,0},{64,96},{96,64},{128,160},{160,128},{192,224},{224,1... | collective-permute-start | bytes 3538952 | tf_op jit(solution)/shard_map/ppermute | solution.py:384
  131.8 2.5 %collective-permute-done.8.other_ref = bf16[32,16,1152]{2,1,0:T(8,128)(2,1)S(1)} collective-permute-done((bf16[32,16,1152]{2,1,0:T(8,128)(2,1)S(1)}, bf16[32,16,1152]{2,1,0:T(8,128)(2,1)S(1)}, u32[]{:S(2)}, u32[]{:S(2)}) %collective-permute-start.8) | collective-permute-done | bytes 1179680 | tf_op jit(solution)/shard_map/ppermute | solution.py:384
  134.2 10.4 %shard_map.95 = bf16[8,2432]{1,0:T(8,128)(2,1)S(1)} custom-call(s32[1]{0:T(128)} %bitcast.ints, f32[8,3712]{1,0:T(8,128)S(1)} %fusion.4.sum_ref, bf16[32,16,1152]{2,1,0:T(8,128)(2,1)S(1)} %all-to-all-done.2.mine_ref, bf16[32,16,1152]{2,1,0:T(8,128)(2,1)S(1)} %collective-permute-done.8.other_ref), custom_call_target="tpu_custom_call" | custom-call | flops 200000000 | bytes 3000000 | tf_op jit(solution)/shard_map/pallas_call | solution.py:386
  144.6 13.8 %all_to_all.25 = bf16[8,8,2432]{2,1,0:T(8,128)(2,1)S(1)} all-to-all(bf16[8,8,2432]{2,1,0:T(8,128)(2,1)S(1)} %broadcast_in_dim.131), channel_id=1, replica_groups={{0,128,256,384,64,192,320,448},{32,160,288,416,96,224,352,480},{1,129,2..., dimensions={0} | all-to-all | bytes 622592 | tf_op jit(solution)/shard_map/all_to_all | solution.py:286
  158.4 3.3 %collective-permute-start.9 = (bf16[64,2432]{1,0:T(8,128)(2,1)S(1)}, bf16[64,2432]{1,0:T(8,128)(2,1)S(1)}, u32[]{:S(2)}, u32[]{:S(2)}) collective-permute-start(bf16[64,2432]{1,0:T(8,128)(2,1)S(1)} %bitcast.84), channel_id=1, source_target_pairs={{0,32},{32,0},{64,96},{96,64},{128,160},{160,128},{192,224},{224,1... | collective-permute-start | bytes 933896 | tf_op jit(solution)/shard_map/ppermute | solution.py:404
  163.1 1.9 shard_map.96
  165.1 1.9 collective-permute-start.10
  167.2 2.1 shard_map.97
  169.4 8.7 %all-to-all-start.4 = ((bf16[16,160,256]{2,1,0:T(8,128)(2,1)}), bf16[16,160,256]{2,1,0:T(8,128)(2,1)S(1)}, u32[]{:S(2)}, u32[]{:S(2)}) async-start(bf16[16,160,256]{2,1,0:T(8,128)(2,1)} %shard_map.97), calls=%async_computation.4 | async-start | bytes 2621440 | tf_op jit(solution)/shard_map/all_to_all | solution.py:286
  178.1 2.3 %collective-permute-done.10 = bf16[2,8,128,128]{3,2,1,0:T(8,128)(2,1)} collective-permute-done((bf16[2,8,128,128]{3,2,1,0:T(8,128)(2,1)S(1)}, bf16[2,8,128,128]{3,2,1,0:T(8,128)(2,1)}, u32[]{:S(2)}, u32[]{:S(2)}) %collective-permute-start.10) | collective-permute-done | bytes 524320 | tf_op jit(solution)/shard_map/ppermute | solution.py:290
  180.4 1.2 convert_add_fusion
  181.6 3.1 %collective-permute-start.13 = (bf16[4,128,128]{2,1,0:T(8,128)(2,1)S(1)}, bf16[4,128,128]{2,1,0:T(8,128)(2,1)S(1)}, u32[]{:S(2)}, u32[]{:S(2)}) collective-permute-start(bf16[4,128,128]{2,1,0:T(8,128)(2,1)S(1)} %get-tuple-element.55), channel_id=1, source_target_pairs={{0,7},{1,6},{2,5},{3,4},{4,3},{5,2},{6,1},{7,0},{8,15},{9,14},{10,... | collective-permute-start | bytes 393224 | tf_op jit(solution)/shard_map/ppermute | solution.py:290
  184.8 3.1 %collective-permute-start.12 = (bf16[4,128,128]{2,1,0:T(8,128)(2,1)S(1)}, bf16[4,128,128]{2,1,0:T(8,128)(2,1)S(1)}, u32[]{:S(2)}, u32[]{:S(2)}) collective-permute-start(bf16[4,128,128]{2,1,0:T(8,128)(2,1)S(1)} %fusion.1), channel_id=1, source_target_pairs={{0,4},{1,5},{2,6},{3,7},{4,0},{5,1},{6,2},{7,3},{8,12},{9,13},{10,... | collective-permute-start | bytes 393224 | tf_op jit(solution)/shard_map/ppermute | solution.py:290
  187.8 2.2 collective-permute-start.11
  190.1 0.4 copy.20
  190.5 1.1 collective-permute-done.12
  191.6 2.3 collective-permute-done.11
  193.9 1.9 collective-permute-start.14
  195.9 0.1 concatenate.45
  196.0 0.7 fusion.17
  196.8 0.1 concatenate.44
  196.8 0.6 broadcast_select_fusion
  197.5 3.3 %collective-permute-done.14 = bf16[2,128,128]{2,1,0:T(8,128)(2,1)S(1)} collective-permute-done((bf16[2,128,128]{2,1,0:T(8,128)(2,1)S(1)}, bf16[2,128,128]{2,1,0:T(8,128)(2,1)S(1)}, u32[]{:S(2)}, u32[]{:S(2)}) %collective-permute-start.14) | collective-permute-done | bytes 65568 | tf_op jit(solution)/shard_map/ppermute | solution.py:290
  200.9 11.3 %collective-permute-start.15 = (bf16[128,128]{1,0:T(8,128)(2,1)S(1)}, bf16[128,128]{1,0:T(8,128)(2,1)S(1)}, u32[]{:S(2)}, u32[]{:S(2)}) collective-permute-start(bf16[128,128]{1,0:T(8,128)(2,1)S(1)} %get-tuple-element.62), channel_id=1, source_target_pairs={{0,128},{1,129},{2,160},{3,161},{4,192},{5,193},{6,224},{7,225},{8... | collective-permute-start | bytes 98312 | tf_op jit(solution)/shard_map/ppermute | solution.py:313
  212.2 1.9 collective-permute-start.16
  214.1 1.2 shard_map.98
  215.3 11.4 %collective-permute-done.16 = bf16[128,128]{1,0:T(8,128)(2,1)S(1)} collective-permute-done((bf16[128,128]{1,0:T(8,128)(2,1)S(1)}, bf16[128,128]{1,0:T(8,128)(2,1)S(1)}, u32[]{:S(2)}, u32[]{:S(2)}) %collective-permute-start.16) | collective-permute-done | bytes 32800 | tf_op jit(solution)/shard_map/ppermute | solution.py:314
  226.8 0.6 slice_bitcast_fusion
  (44 shorter events, 0.9 us)
Async XLA Ops:
  0.6 0.7 copy-start
  2.8 14.5 %collective-permute-start = (bf16[128,128]{1,0:T(8,128)(2,1)S(1)}, bf16[128,128]{1,0:T(8,128)(2,1)S(1)}, u32[]{:S(2)}, u32[]{:S(2)}) collective-permute-start(bf16[128,128]{1,0:T(8,128)(2,1)S(1)} %pad_maximum_fusion.1), channel_id=1, source_target_pairs={{128,0},{129,1},{160,2},{161,3},{192,4},{193,5},{224,6},{225,7},{2... | collective-permute-start | bytes 98312 | tf_op jit(solution)/shard_map/ppermute | solution.py:332
  18.9 48.5 %all-to-all-start = ((bf16[32,192,128]{2,1,0:T(8,128)(2,1)}), bf16[32,192,128]{2,1,0:T(8,128)(2,1)S(1)}, u32[]{:S(2)}, u32[]{:S(2)}) async-start(bf16[32,192,128]{2,1,0:T(8,128)(2,1)} %pad_maximum_fusion), calls=%async_computation | async-start | bytes 3145728 | tf_op jit(solution)/shard_map/all_to_all | solution.py:286
  29.4 51.3 %copy-start.1 = (bf16[128,256]{1,0:T(8,128)(2,1)S(1)}, bf16[128,256]{1,0:T(8,128)(2,1)}, u32[]{:S(2)}) copy-start(bf16[128,256]{1,0:T(8,128)(2,1)} %x_ref.5) | copy-start | bytes 196612
  29.4 51.2 %copy-start.2 = (bf16[128,256]{1,0:T(8,128)(2,1)S(1)}, bf16[128,256]{1,0:T(8,128)(2,1)}, u32[]{:S(2)}) copy-start(bf16[128,256]{1,0:T(8,128)(2,1)} %g_ref.3) | copy-start | bytes 196612
  68.4 4.8 %collective-permute-start.1 = (bf16[16,1152]{1,0:T(8,128)(2,1)S(1)}, bf16[16,1152]{1,0:T(8,128)(2,1)S(1)}, u32[]{:S(2)}, u32[]{:S(2)}) collective-permute-start(bf16[16,1152]{1,0:T(8,128)(2,1)S(1)} %get-tuple-element.25), channel_id=1, source_target_pairs={{0,32},{32,0},{64,96},{96,64},{128,160},{160,128},{192,224},{224,1... | collective-permute-start | bytes 110600 | tf_op jit(solution)/shard_map/ppermute | solution.py:361
  74.0 17.1 %all-to-all-start.1 = ((bf16[8,16,1152]{2,1,0:T(8,128)(2,1)}), bf16[8,16,1152]{2,1,0:T(8,128)(2,1)S(1)}, u32[]{:S(2)}, u32[]{:S(2)}) async-start(bf16[8,16,1152]{2,1,0:T(8,128)(2,1)} %broadcast_in_dim.129), calls=%async_computation.1 | async-start | bytes 589824 | tf_op jit(solution)/shard_map/all_to_all | solution.py:286
  83.0 14.7 %collective-permute-start.4 = (bf16[32,3712]{1,0:T(8,128)(2,1)}, bf16[32,3712]{1,0:T(8,128)(2,1)S(1)}, u32[]{:S(2)}, u32[]{:S(2)}) collective-permute-start(bf16[32,3712]{1,0:T(8,128)(2,1)} %get-tuple-element.32), channel_id=1, source_target_pairs={{0,96},{32,64},{64,32},{96,0},{128,224},{160,192},{192,160},{224,1... | collective-permute-start | bytes 712712 | tf_op jit(solution)/shard_map/ppermute | solution.py:376
  86.0 12.9 %collective-permute-start.3 = (bf16[32,3712]{1,0:T(8,128)(2,1)}, bf16[32,3712]{1,0:T(8,128)(2,1)S(1)}, u32[]{:S(2)}, u32[]{:S(2)}) collective-permute-start(bf16[32,3712]{1,0:T(8,128)(2,1)} %get-tuple-element.31), channel_id=1, source_target_pairs={{0,64},{32,96},{64,0},{96,32},{128,192},{160,224},{192,128},{224,1... | collective-permute-start | bytes 712712 | tf_op jit(solution)/shard_map/ppermute | solution.py:376
  89.1 9.8 %collective-permute-start.2 = (bf16[32,3712]{1,0:T(8,128)(2,1)S(1)}, bf16[32,3712]{1,0:T(8,128)(2,1)}, u32[]{:S(2)}, u32[]{:S(2)}) collective-permute-start(bf16[32,3712]{1,0:T(8,128)(2,1)S(1)} %get-tuple-element.30), channel_id=1, source_target_pairs={{0,32},{32,0},{64,96},{96,64},{128,160},{160,128},{192,224},{224,1... | collective-permute-start | bytes 712712 | tf_op jit(solution)/shard_map/ppermute | solution.py:376
  92.2 34.9 %all-to-all-start.2 = ((bf16[32,16,1152]{2,1,0:T(8,128)(2,1)}), bf16[32,16,1152]{2,1,0:T(8,128)(2,1)S(1)}, u32[]{:S(2)}, u32[]{:S(2)}) async-start(bf16[32,16,1152]{2,1,0:T(8,128)(2,1)} %broadcast_in_dim.130), calls=%async_computation.2 | async-start | bytes 2359296 | tf_op jit(solution)/shard_map/all_to_all | solution.py:286
  100.0 11.4 %collective-permute-start.7 = (bf16[8,3712]{1,0:T(8,128)(2,1)S(1)}, bf16[8,3712]{1,0:T(8,128)(2,1)S(1)}, u32[]{:S(2)}, u32[]{:S(2)}) collective-permute-start(bf16[8,3712]{1,0:T(8,128)(2,1)S(1)} %get-tuple-element.57), channel_id=1, source_target_pairs={{0,384},{32,416},{64,448},{96,480},{128,256},{160,288},{192,320},{... | collective-permute-start | bytes 178184 | tf_op jit(solution)/shard_map/ppermute | solution.py:382
  103.3 9.1 %collective-permute-start.6 = (bf16[8,3712]{1,0:T(8,128)(2,1)S(1)}, bf16[8,3712]{1,0:T(8,128)(2,1)S(1)}, u32[]{:S(2)}, u32[]{:S(2)}) collective-permute-start(bf16[8,3712]{1,0:T(8,128)(2,1)S(1)} %get-tuple-element.58), channel_id=1, source_target_pairs={{0,256},{32,288},{64,320},{96,352},{128,384},{160,416},{192,448},{... | collective-permute-start | bytes 178184 | tf_op jit(solution)/shard_map/ppermute | solution.py:382
  107.2 9.2 %collective-permute-start.5 = (bf16[8,3712]{1,0:T(8,128)(2,1)S(1)}, bf16[8,3712]{1,0:T(8,128)(2,1)S(1)}, u32[]{:S(2)}, u32[]{:S(2)}) collective-permute-start(bf16[8,3712]{1,0:T(8,128)(2,1)S(1)} %get-tuple-element.56), channel_id=1, source_target_pairs={{0,128},{32,160},{64,192},{96,224},{128,0},{160,32},{192,64},{224,... | collective-permute-start | bytes 178184 | tf_op jit(solution)/shard_map/ppermute | solution.py:382
  127.1 7.1 %collective-permute-start.8 = (bf16[32,16,1152]{2,1,0:T(8,128)(2,1)S(1)}, bf16[32,16,1152]{2,1,0:T(8,128)(2,1)S(1)}, u32[]{:S(2)}, u32[]{:S(2)}) collective-permute-start(bf16[32,16,1152]{2,1,0:T(8,128)(2,1)S(1)} %all-to-all-done.2.mine_ref), channel_id=1, source_target_pairs={{0,32},{32,0},{64,96},{96,64},{128,160},{160,128},{192,224},{224,1... | collective-permute-start | bytes 3538952 | tf_op jit(solution)/shard_map/ppermute | solution.py:384
  158.4 4.7 %collective-permute-start.9 = (bf16[64,2432]{1,0:T(8,128)(2,1)S(1)}, bf16[64,2432]{1,0:T(8,128)(2,1)S(1)}, u32[]{:S(2)}, u32[]{:S(2)}) collective-permute-start(bf16[64,2432]{1,0:T(8,128)(2,1)S(1)} %bitcast.84), channel_id=1, source_target_pairs={{0,32},{32,0},{64,96},{96,64},{128,160},{160,128},{192,224},{224,1... | collective-permute-start | bytes 933896 | tf_op jit(solution)/shard_map/ppermute | solution.py:404
  165.1 15.3 %collective-permute-start.10 = (bf16[2,8,128,128]{3,2,1,0:T(8,128)(2,1)S(1)}, bf16[2,8,128,128]{3,2,1,0:T(8,128)(2,1)}, u32[]{:S(2)}, u32[]{:S(2)}) collective-permute-start(bf16[2,8,128,128]{3,2,1,0:T(8,128)(2,1)S(1)} %get-tuple-element.36), channel_id=1, source_target_pairs={{0,1},{1,0},{2,3},{3,2},{4,5},{5,4},{6,7},{7,6},{8,9},{9,8},{10,11... | collective-permute-start | bytes 1572872 | tf_op jit(solution)/shard_map/ppermute | solution.py:290
  169.4 44.8 %all-to-all-start.4 = ((bf16[16,160,256]{2,1,0:T(8,128)(2,1)}), bf16[16,160,256]{2,1,0:T(8,128)(2,1)S(1)}, u32[]{:S(2)}, u32[]{:S(2)}) async-start(bf16[16,160,256]{2,1,0:T(8,128)(2,1)} %shard_map.97), calls=%async_computation.4 | async-start | bytes 2621440 | tf_op jit(solution)/shard_map/all_to_all | solution.py:286
  181.6 8.9 %collective-permute-start.13 = (bf16[4,128,128]{2,1,0:T(8,128)(2,1)S(1)}, bf16[4,128,128]{2,1,0:T(8,128)(2,1)S(1)}, u32[]{:S(2)}, u32[]{:S(2)}) collective-permute-start(bf16[4,128,128]{2,1,0:T(8,128)(2,1)S(1)} %get-tuple-element.55), channel_id=1, source_target_pairs={{0,7},{1,6},{2,5},{3,4},{4,3},{5,2},{6,1},{7,0},{8,15},{9,14},{10,... | collective-permute-start | bytes 393224 | tf_op jit(solution)/shard_map/ppermute | solution.py:290
  184.8 6.8 %collective-permute-start.12 = (bf16[4,128,128]{2,1,0:T(8,128)(2,1)S(1)}, bf16[4,128,128]{2,1,0:T(8,128)(2,1)S(1)}, u32[]{:S(2)}, u32[]{:S(2)}) collective-permute-start(bf16[4,128,128]{2,1,0:T(8,128)(2,1)S(1)} %fusion.1), channel_id=1, source_target_pairs={{0,4},{1,5},{2,6},{3,7},{4,0},{5,1},{6,2},{7,3},{8,12},{9,13},{10,... | collective-permute-start | bytes 393224 | tf_op jit(solution)/shard_map/ppermute | solution.py:290
  187.8 6.0 %collective-permute-start.11 = (bf16[4,128,128]{2,1,0:T(8,128)(2,1)S(1)}, bf16[4,128,128]{2,1,0:T(8,128)(2,1)S(1)}, u32[]{:S(2)}, u32[]{:S(2)}) collective-permute-start(bf16[4,128,128]{2,1,0:T(8,128)(2,1)S(1)} %get-tuple-element.54), channel_id=1, source_target_pairs={{0,3},{1,2},{2,1},{3,0},{4,7},{5,6},{6,5},{7,4},{8,11},{9,10},{10,... | collective-permute-start | bytes 393224 | tf_op jit(solution)/shard_map/ppermute | solution.py:290
  193.9 6.9 %collective-permute-start.14 = (bf16[2,128,128]{2,1,0:T(8,128)(2,1)S(1)}, bf16[2,128,128]{2,1,0:T(8,128)(2,1)S(1)}, u32[]{:S(2)}, u32[]{:S(2)}) collective-permute-start(bf16[2,128,128]{2,1,0:T(8,128)(2,1)S(1)} %fusion.6), channel_id=1, source_target_pairs={{0,8},{1,9},{2,10},{3,11},{4,12},{5,13},{6,14},{7,15},{8,0},{9,1},... | collective-permute-start | bytes 196616 | tf_op jit(solution)/shard_map/ppermute | solution.py:290
  200.9 14.5 %collective-permute-start.15 = (bf16[128,128]{1,0:T(8,128)(2,1)S(1)}, bf16[128,128]{1,0:T(8,128)(2,1)S(1)}, u32[]{:S(2)}, u32[]{:S(2)}) collective-permute-start(bf16[128,128]{1,0:T(8,128)(2,1)S(1)} %get-tuple-element.62), channel_id=1, source_target_pairs={{0,128},{1,129},{2,160},{3,161},{4,192},{5,193},{6,224},{7,225},{8... | collective-permute-start | bytes 98312 | tf_op jit(solution)/shard_map/ppermute | solution.py:313
  212.2 14.6 %collective-permute-start.16 = (bf16[128,128]{1,0:T(8,128)(2,1)S(1)}, bf16[128,128]{1,0:T(8,128)(2,1)S(1)}, u32[]{:S(2)}, u32[]{:S(2)}) collective-permute-start(bf16[128,128]{1,0:T(8,128)(2,1)S(1)} %get-tuple-element.61), channel_id=1, source_target_pairs={{0,384},{1,385},{2,416},{3,417},{4,448},{5,449},{6,480},{7,481},{8... | collective-permute-start | bytes 98312 | tf_op jit(solution)/shard_map/ppermute | solution.py:314
